TPU v7x, 32 devices: a whole 2x2x4 slice. The times are simulated.
32 devices in a mesh: fsdp: 8 (over z, y), ctx: 2 (over x), tp: 2 (over core).
Axes of the slice: x: 2, y: 2, z: 4, core: 2. Of those that a mesh axis runs over, the one named last changes fastest.
Arguments:
- tokens: bfloat16 [8192, 1536], P(('fsdp', 'ctx')), may hold values from -6 to 6, as said below
- lengths: int32 [8, 3], P('fsdp'), may hold values from 1 to 768, 1024 in all within a row
- routes: int32 [8192, 4], P(('fsdp', 'ctx')), may hold values from 0 to 7, all different within a row; in each aligned block of 512 rows (0 to 511, 512 to 1023, ...) at most 384 rows name the same one
- norm_attn: bfloat16 [1536], P(('fsdp', 'ctx')), may hold values from 0.5 to 1.5
- w_query: bfloat16 [1536, 1536], P(('fsdp', 'ctx'), 'tp'), may hold values from -0.15625 to 0.15625
- w_key: bfloat16 [1536, 256], P(('fsdp', 'ctx'), 'tp'), may hold values from -0.15625 to 0.15625
- w_value: bfloat16 [1536, 256], P(('fsdp', 'ctx'), 'tp'), may hold values from -0.15625 to 0.15625
- w_out: bfloat16 [1536, 1536], P('tp', ('fsdp', 'ctx')), may hold values from -2 to 2
- norm_moe: bfloat16 [1536], P(('fsdp', 'ctx')), may hold values from 0.5 to 1.5
- w_router: bfloat16 [1536, 8], P(('fsdp', 'ctx')), may hold values from -0.15917969 to 0.15917969
- w_gate: bfloat16 [8, 1536, 768], P('fsdp', None, 'tp'), may hold values from -0.15625 to 0.15625
- w_up: bfloat16 [8, 1536, 768], P('fsdp', None, 'tp'), may hold values from -0.15625 to 0.15625
- w_down: bfloat16 [8, 768, 1536], P('fsdp', 'tp'), may hold values from -0.4375 to 0.4375
- out_grad: bfloat16 [8192, 1536], P(('fsdp', 'ctx')), may hold values from -6 to 6
- loss_grad: float32 [1], replicated, may hold values from 8192 to 65536
Outputs:
- output: bfloat16 [8192, 1536], P(('fsdp', 'ctx'))
- loss: float32 [1], replicated
- tokens_grad: float32 [8192, 1536], P(('fsdp', 'ctx'))
- norm_attn_grad: float32 [1536], P(('fsdp', 'ctx'))
- w_query_grad: float32 [1536, 1536], P(('fsdp', 'ctx'), 'tp')
- w_key_grad: float32 [1536, 256], P(('fsdp', 'ctx'), 'tp')
- w_value_grad: float32 [1536, 256], P(('fsdp', 'ctx'), 'tp')
- w_out_grad: float32 [1536, 1536], P('tp', ('fsdp', 'ctx'))
- norm_moe_grad: float32 [1536], P(('fsdp', 'ctx'))
- w_router_grad: float32 [1536, 8], P(('fsdp', 'ctx'))
- w_gate_grad: float32 [8, 1536, 768], P('fsdp', 'ctx', 'tp')
- w_up_grad: float32 [8, 1536, 768], P('fsdp', 'ctx', 'tp')
- w_down_grad: float32 [8, 768, 1536], P('fsdp', 'tp', 'ctx')
Inputs may be any that keep to these rules, and one draw needn't show every extreme that they name: `tokens`: entries are of order one. `lengths`: each row sums to 1024; its longest document has exactly 768 tokens. `routes`: each row names 4 different experts. In the rows of one device (aligned blocks of 512 rows) no expert is named by more than 384 rows, a bound that some block reaches.
All inputs are finite; a program needn't handle non-finite values.
Results may differ from a plain program's by a relative error of at most 0.017.
Values may be sent and summed in bfloat16 or wider, within the bound.
A program may use at most 256 MiB of HBM per device.

v0:
```python
import jax
import jax.numpy as jnp
from jax import lax
from jax.sharding import PartitionSpec as P

HEAD_DIM = 128


epsilon = 1e-06
rope_base = 10000.0
masked_score = -1e30
highest = lax.Precision.HIGHEST


def rms_parts(values, row_gains):
    inverse = lax.rsqrt(jnp.mean(values * values, axis=-1, keepdims=True) + epsilon)
    scaled = values * inverse
    return (inverse, scaled, scaled * row_gains)


def rms_back(inverse, scaled, row_gains, upstream):
    gain_grad = jnp.sum(upstream * scaled, axis=0)
    scaled_grad = upstream * row_gains
    return (
        gain_grad,
        inverse * (scaled_grad - scaled * jnp.mean(scaled_grad * scaled, axis=-1, keepdims=True)),
    )


def rope_tables(positions):
    half_dim = HEAD_DIM // 2
    frequency = rope_base ** (-(jnp.arange(half_dim, dtype=jnp.float32) * (2.0 / HEAD_DIM)))
    angles = positions.astype(jnp.float32)[:, None] * frequency[None, :]
    return (jnp.cos(angles)[:, None, :], jnp.sin(angles)[:, None, :])


def rotate(vectors, cos_table, sin_table):
    half_dim = vectors.shape[-1] // 2
    first_half = vectors[..., :half_dim]
    second_half = vectors[..., half_dim:]
    return jnp.concatenate(
        [
            first_half * cos_table - second_half * sin_table,
            second_half * cos_table + first_half * sin_table,
        ],
        axis=-1,
    )


def pack_layout(length_row, row_count):
    doc_ends = jnp.cumsum(length_row)
    doc_starts = doc_ends - length_row
    row_index = jnp.arange(row_count, dtype=jnp.int32)
    doc_ids = jnp.sum((row_index[:, None] >= doc_ends[None, :]).astype(jnp.int32), axis=1)
    doc_numbers = jnp.arange(length_row.shape[0], dtype=jnp.int32)
    doc_first = jnp.sum(
        jnp.where(doc_ids[:, None] == doc_numbers[None, :], doc_starts[None, :], 0), axis=1
    )
    return (doc_ids, row_index - doc_first, doc_first)


def key_block_data(key_number, block_rows, pack_keys, pack_values, doc_ids):
    key_start = key_number * block_rows
    key_block = lax.dynamic_slice_in_dim(pack_keys, key_start, block_rows, 0)
    value_block = lax.dynamic_slice_in_dim(pack_values, key_start, block_rows, 0)
    key_docs = lax.dynamic_slice_in_dim(doc_ids, key_start, block_rows, 0)
    key_index = key_start + jnp.arange(block_rows, dtype=jnp.int32)
    return (key_start, key_block, value_block, key_docs, key_index)


def block_scores(query_block, key_block, query_docs, query_index, key_docs, key_index):
    scale_factor = HEAD_DIM ** (-0.5)
    scores = (
        jnp.einsum("qhgd,khd->hgqk", query_block, key_block, preferred_element_type=jnp.float32)
        * scale_factor
    )
    allowed = (query_docs[:, None] == key_docs[None, :]) & (
        key_index[None, :] <= query_index[:, None]
    )
    return (scores, allowed)


def query_block_range(start_row, block_rows, doc_ids, doc_first):
    query_index = start_row + jnp.arange(block_rows, dtype=jnp.int32)
    query_docs = lax.dynamic_slice_in_dim(doc_ids, start_row, block_rows, 0)
    low_block = doc_first[start_row] // block_rows
    high_block = (start_row + block_rows - 1) // block_rows + 1
    return (query_index, query_docs, low_block, high_block)


def attention_forward(grouped, pack_keys, pack_values, doc_ids, doc_first, base_row, block_rows):
    row_count, local_kv, group_size, head_dim = grouped.shape
    start_row = base_row + 0
    query_index, query_docs, low_block, high_block = query_block_range(
        start_row, block_rows, doc_ids, doc_first
    )

    def scan_maxima(key_number, running):
        maxima, totals = running
        key_start, key_block, value_block, key_docs, key_index = key_block_data(
            key_number, block_rows, pack_keys, pack_values, doc_ids
        )
        scores, allowed = block_scores(
            grouped, key_block, query_docs, query_index, key_docs, key_index
        )
        new_max = jnp.maximum(maxima, jnp.max(jnp.where(allowed, scores, masked_score), axis=-1))
        weights = jnp.where(allowed, jnp.exp(scores - new_max[..., None]), 0.0)
        return (new_max, totals * jnp.exp(maxima - new_max) + jnp.sum(weights, axis=-1))

    start_max = jnp.full((local_kv, group_size, block_rows), masked_score, jnp.float32)
    start_total = jnp.zeros((local_kv, group_size, block_rows), jnp.float32)
    maxima, totals = lax.fori_loop(low_block, high_block, scan_maxima, (start_max, start_total))
    log_total = maxima + jnp.log(totals)

    def accumulate(key_number, summed):
        key_start, key_block, value_block, key_docs, key_index = key_block_data(
            key_number, block_rows, pack_keys, pack_values, doc_ids
        )
        scores, allowed = block_scores(
            grouped, key_block, query_docs, query_index, key_docs, key_index
        )
        block_probs = jnp.where(allowed, jnp.exp(scores - log_total[..., None]), 0.0).astype(
            jnp.bfloat16
        )
        return summed + jnp.einsum(
            "hgqk,khd->hgqd", block_probs, value_block, preferred_element_type=jnp.float32
        )

    summed = lax.fori_loop(
        low_block,
        high_block,
        accumulate,
        jnp.zeros((local_kv, group_size, block_rows, head_dim), jnp.float32),
    )
    outputs = summed.transpose(2, 0, 1, 3).reshape(block_rows, local_kv * group_size * head_dim)
    totals_list = [log_total]
    return (outputs, totals_list)


def attention_backward(
    grouped,
    pack_keys,
    pack_values,
    grad_mixed,
    totals_list,
    doc_ids,
    doc_first,
    base_row,
    block_rows,
):
    row_count, local_kv, group_size, head_dim = grouped.shape
    pack_count = pack_keys.shape[0]
    scale_factor = HEAD_DIM ** (-0.5)
    grad_grouped = grad_mixed.reshape(row_count, local_kv, group_size, head_dim)
    key_acc = jnp.zeros((pack_count, local_kv, head_dim), jnp.float32)
    value_acc = jnp.zeros((pack_count, local_kv, head_dim), jnp.float32)
    start_row = base_row + 0
    log_total = totals_list[0]
    query_index, query_docs, low_block, high_block = query_block_range(
        start_row, block_rows, doc_ids, doc_first
    )

    def probs_at(key_number):
        key_start, key_block, value_block, key_docs, key_index = key_block_data(
            key_number, block_rows, pack_keys, pack_values, doc_ids
        )
        scores, allowed = block_scores(
            grouped, key_block, query_docs, query_index, key_docs, key_index
        )
        block_probs = jnp.where(allowed, jnp.exp(scores - log_total[..., None]), 0.0)
        prob_grad = jnp.einsum(
            "qhgd,khd->hgqk", grad_grouped, value_block, preferred_element_type=jnp.float32
        )
        return (key_start, key_block, block_probs, prob_grad)

    def add_delta(key_number, row_delta):
        pieces = probs_at(key_number)
        return row_delta + jnp.sum(pieces[2] * pieces[3], axis=-1)

    row_delta = lax.fori_loop(
        low_block, high_block, add_delta, jnp.zeros((local_kv, group_size, block_rows), jnp.float32)
    )

    def add_grads(key_number, running):
        query_acc, key_total, value_total = running
        key_start, key_block, block_probs, prob_grad = probs_at(key_number)
        score_grad = (block_probs * (prob_grad - row_delta[..., None])).astype(jnp.bfloat16)
        query_acc = (
            query_acc
            + jnp.einsum(
                "hgqk,khd->qhgd", score_grad, key_block, preferred_element_type=jnp.float32
            )
            * scale_factor
        )
        key_piece = (
            jnp.einsum("hgqk,qhgd->khd", score_grad, grouped, preferred_element_type=jnp.float32)
            * scale_factor
        )
        value_piece = jnp.einsum(
            "hgqk,qhgd->khd",
            block_probs.astype(jnp.bfloat16),
            grad_grouped,
            preferred_element_type=jnp.float32,
        )
        key_total = lax.dynamic_update_slice_in_dim(
            key_total,
            lax.dynamic_slice_in_dim(key_total, key_start, block_rows, 0) + key_piece,
            key_start,
            0,
        )
        value_total = lax.dynamic_update_slice_in_dim(
            value_total,
            lax.dynamic_slice_in_dim(value_total, key_start, block_rows, 0) + value_piece,
            key_start,
            0,
        )
        return (query_acc, key_total, value_total)

    start_query = jnp.zeros((block_rows, local_kv, group_size, head_dim), jnp.float32)
    query_acc, key_acc, value_acc = lax.fori_loop(
        low_block, high_block, add_grads, (start_query, key_acc, value_acc)
    )
    return (query_acc, key_acc, value_acc)


def to_expert(arrived, local_experts, capacity):
    sources = arrived.shape[0]
    return (
        arrived.reshape(sources, local_experts, capacity, -1)
        .transpose(1, 0, 2, 3)
        .reshape(local_experts, sources * capacity, -1)
    )


def from_expert(expert_rows, sources, capacity):
    local_experts = expert_rows.shape[0]
    return (
        expert_rows.reshape(local_experts, sources, capacity, -1)
        .transpose(1, 0, 2, 3)
        .reshape(sources, local_experts * capacity, -1)
    )


def expert_forward(expert_rows, w_gate, w_up):
    gate_pre = jnp.einsum("erd,edf->erf", expert_rows, w_gate, preferred_element_type=jnp.float32)
    up_pre = jnp.einsum("erd,edf->erf", expert_rows, w_up, preferred_element_type=jnp.float32)
    hidden = (gate_pre * jax.nn.sigmoid(gate_pre) * up_pre).astype(jnp.bfloat16)
    return (gate_pre, up_pre, hidden)


def on_device(
    tokens,
    lengths,
    routes,
    norm_attn,
    w_query,
    w_key,
    w_value,
    w_out,
    norm_moe,
    w_router,
    w_gate,
    w_up,
    w_down,
    out_grad,
    loss_grad,
):
    row_count, model_width = tokens.shape
    ctx_count = lax.axis_size("ctx")
    fsdp_count = lax.axis_size("fsdp")
    ctx_place = lax.axis_index("ctx")
    top_count = routes.shape[1]
    expert_count = w_router.shape[1]
    local_experts = w_gate.shape[0]
    capacity = 3 * row_count * top_count // (2 * expert_count)
    pack_count = row_count * ctx_count
    block_rows = min(512, row_count)
    base_row = ctx_place * row_count
    gain_attn, full_query, full_key, full_value, full_out, gain_moe, full_router = (
        lax.all_gather(norm_attn, ("fsdp", "ctx"), axis=0, tiled=True),
        lax.all_gather(w_query, ("fsdp", "ctx"), axis=0, tiled=True),
        lax.all_gather(w_key, ("fsdp", "ctx"), axis=0, tiled=True),
        lax.all_gather(w_value, ("fsdp", "ctx"), axis=0, tiled=True),
        lax.all_gather(w_out, ("fsdp", "ctx"), axis=1, tiled=True),
        lax.all_gather(norm_moe, ("fsdp", "ctx"), axis=0, tiled=True),
        lax.all_gather(w_router, ("fsdp", "ctx"), axis=0, tiled=True),
    )
    doc_ids, positions, doc_first = pack_layout(lengths[0], pack_count)
    own_positions = lax.dynamic_slice_in_dim(positions, base_row, row_count, 0)
    cos_table, sin_table = rope_tables(own_positions)
    x_float = tokens.astype(jnp.float32)
    attn_gain = gain_attn.astype(jnp.float32)
    inverse_attn, scaled_attn, normed_full = rms_parts(x_float, attn_gain)
    normed_attn = normed_full.astype(jnp.bfloat16)
    local_heads = full_query.shape[1] // HEAD_DIM
    local_kv = full_key.shape[1] // HEAD_DIM
    group_size = local_heads // local_kv
    query_raw = jnp.dot(normed_attn, full_query, preferred_element_type=jnp.float32).reshape(
        row_count, local_heads, HEAD_DIM
    )
    queries = rotate(query_raw, cos_table, sin_table).astype(jnp.bfloat16)
    key_raw = jnp.dot(normed_attn, full_key, preferred_element_type=jnp.float32).reshape(
        row_count, local_kv, HEAD_DIM
    )
    key_own = rotate(key_raw, cos_table, sin_table).astype(jnp.bfloat16)
    value_own = (
        jnp.dot(normed_attn, full_value, preferred_element_type=jnp.float32)
        .astype(jnp.bfloat16)
        .reshape(row_count, local_kv, HEAD_DIM)
    )
    pack_keys, pack_values = (
        lax.all_gather(key_own, "ctx", axis=0, tiled=True),
        lax.all_gather(value_own, "ctx", axis=0, tiled=True),
    )
    grouped = queries.reshape(row_count, local_kv, group_size, HEAD_DIM)
    mixed_full, totals_list = attention_forward(
        grouped, pack_keys, pack_values, doc_ids, doc_first, base_row, block_rows
    )
    attended = mixed_full.astype(jnp.bfloat16)
    out_part = jnp.dot(attended, full_out, preferred_element_type=jnp.float32)
    attn_out = lax.psum(out_part, "tp")
    middle = x_float + attn_out
    moe_gain = gain_moe.astype(jnp.float32)
    inverse_moe, scaled_moe, normed_mid = rms_parts(middle, moe_gain)
    normed_moe = normed_mid.astype(jnp.bfloat16)
    logits = jnp.dot(normed_moe, full_router, preferred_element_type=jnp.float32)
    shifted = jnp.exp(logits - jnp.max(logits, axis=-1, keepdims=True))
    router_probs = shifted / jnp.sum(shifted, axis=-1, keepdims=True)
    expert_ids = jnp.arange(expert_count, dtype=jnp.int32)
    route_mask = (routes[:, :, None] == expert_ids[None, None, :]).astype(jnp.float32)
    chosen = jnp.sum(route_mask * router_probs[:, None, :], axis=-1)
    chosen_total = jnp.sum(chosen, axis=-1, keepdims=True)
    gate_weights = chosen / chosen_total
    counts_global, probs_global = lax.psum(
        (jnp.sum(route_mask, axis=(0, 1)), jnp.sum(router_probs, axis=0)), ("fsdp", "ctx")
    )
    token_total = pack_count * fsdp_count
    fraction = counts_global / (token_total * top_count)
    balance_loss = (expert_count * jnp.sum(fraction * (probs_global / token_total))).reshape(1)
    flat_routes = routes.reshape(-1)
    flat_mask = (flat_routes[:, None] == expert_ids[None, :]).astype(jnp.int32)
    slot_rank = jnp.sum(jnp.cumsum(flat_mask, axis=0) * flat_mask, axis=1) - 1
    slot_index = flat_routes * capacity + slot_rank
    buffer_rows = expert_count * capacity
    send_rows = (
        jnp.zeros((buffer_rows, model_width), jnp.bfloat16)
        .at[slot_index]
        .set(jnp.repeat(normed_moe, top_count, axis=0))
    )
    send_rows = send_rows.reshape(fsdp_count, local_experts * capacity, model_width)
    arrived = lax.all_to_all(send_rows, "fsdp", split_axis=0, concat_axis=0, tiled=True)
    expert_rows = to_expert(arrived, local_experts, capacity)
    gate_pre, up_pre, hidden = expert_forward(expert_rows, w_gate, w_up)
    expert_out = jnp.einsum(
        "erf,efd->erd", hidden, w_down, preferred_element_type=jnp.float32
    ).astype(jnp.bfloat16)
    returned = lax.all_to_all(
        from_expert(expert_out, fsdp_count, capacity),
        "fsdp",
        split_axis=0,
        concat_axis=0,
        tiled=True,
    )
    slot_values = returned.reshape(buffer_rows, model_width)[slot_index].reshape(
        row_count, top_count, model_width
    )
    moe_part = jnp.sum(gate_weights[:, :, None] * slot_values, axis=1)
    moe_out = lax.psum(moe_part.astype(jnp.bfloat16), "tp").astype(jnp.float32)
    output = (middle + moe_out).astype(jnp.bfloat16)
    upstream = out_grad.astype(jnp.float32)
    gate_dots = jnp.sum(slot_values * upstream[:, None, :], axis=-1)
    grad_slots = (
        (gate_weights[:, :, None] * upstream[:, None, :])
        .astype(jnp.bfloat16)
        .reshape(row_count * top_count, model_width)
    )
    grad_send = jnp.zeros((buffer_rows, model_width), jnp.bfloat16).at[slot_index].set(grad_slots)
    grad_send = grad_send.reshape(fsdp_count, local_experts * capacity, model_width)
    grad_arrived = lax.all_to_all(grad_send, "fsdp", split_axis=0, concat_axis=0, tiled=True)
    kept_gate, kept_up, kept_hidden = (gate_pre, up_pre, hidden)
    grad_expert = to_expert(grad_arrived, local_experts, capacity)
    grad_hidden = jnp.einsum(
        "erd,efd->erf", grad_expert, w_down, preferred_element_type=jnp.float32
    )
    down_grad = jnp.einsum(
        "erf,erd->efd", kept_hidden, grad_expert, preferred_element_type=jnp.float32
    )
    sigmoid_gate = jax.nn.sigmoid(kept_gate)
    grad_gate = (
        grad_hidden * kept_up * sigmoid_gate * (1.0 + kept_gate * (1.0 - sigmoid_gate))
    ).astype(jnp.bfloat16)
    grad_up = (grad_hidden * kept_gate * sigmoid_gate).astype(jnp.bfloat16)
    gate_grad_w = jnp.einsum(
        "erd,erf->edf", expert_rows, grad_gate, preferred_element_type=jnp.float32
    )
    up_grad_w = jnp.einsum("erd,erf->edf", expert_rows, grad_up, preferred_element_type=jnp.float32)
    grad_rows = jnp.einsum("erf,edf->erd", grad_gate, w_gate, preferred_element_type=jnp.float32)
    grad_rows = (
        grad_rows + jnp.einsum("erf,edf->erd", grad_up, w_up, preferred_element_type=jnp.float32)
    ).astype(jnp.bfloat16)
    grad_back = lax.all_to_all(
        from_expert(grad_rows, fsdp_count, capacity),
        "fsdp",
        split_axis=0,
        concat_axis=0,
        tiled=True,
    )
    grad_slot_rows = grad_back.reshape(buffer_rows, model_width)[slot_index].reshape(
        row_count, top_count, model_width
    )
    moe_in_part = jnp.sum(grad_slot_rows.astype(jnp.float32), axis=1)
    moe_in_grad, gate_grad = lax.psum((moe_in_part, gate_dots), "tp")
    weighted = jnp.sum(gate_grad * gate_weights, axis=-1, keepdims=True)
    chosen_grad = (gate_grad - weighted) / chosen_total
    prob_grad = (
        jnp.sum(route_mask * chosen_grad[:, :, None], axis=1)
        + loss_grad[0] * expert_count * fraction / token_total
    )
    logit_grad = router_probs * (
        prob_grad - jnp.sum(prob_grad * router_probs, axis=-1, keepdims=True)
    )
    router_grad = jnp.einsum(
        "td,te->de", normed_moe.astype(jnp.float32), logit_grad, precision=highest
    )
    moe_grad = moe_in_grad + jnp.einsum(
        "te,de->td", logit_grad, full_router.astype(jnp.float32), precision=highest
    )
    gain_moe_grad, middle_norm_grad = rms_back(inverse_moe, scaled_moe, moe_gain, moe_grad)
    middle_grad = upstream + middle_norm_grad
    out_in = middle_grad.astype(jnp.bfloat16)
    out_w_grad = jnp.einsum("tq,td->qd", attended, out_in, preferred_element_type=jnp.float32)
    mixed_grad = jnp.einsum(
        "td,qd->tq", out_in, full_out, preferred_element_type=jnp.float32
    ).astype(jnp.bfloat16)
    query_acc, key_grad_pack, value_grad_pack = attention_backward(
        grouped,
        pack_keys,
        pack_values,
        mixed_grad,
        totals_list,
        doc_ids,
        doc_first,
        base_row,
        block_rows,
    )
    key_grad, value_grad, gate_w_out, up_w_out, down_w_out = (
        lax.psum_scatter(key_grad_pack, "ctx", scatter_dimension=0, tiled=True),
        lax.psum_scatter(value_grad_pack, "ctx", scatter_dimension=0, tiled=True),
        lax.psum_scatter(gate_grad_w, "ctx", scatter_dimension=1, tiled=True),
        lax.psum_scatter(up_grad_w, "ctx", scatter_dimension=1, tiled=True),
        lax.psum_scatter(down_grad, "ctx", scatter_dimension=2, tiled=True),
    )
    query_grad = (
        rotate(query_acc.reshape(row_count, local_heads, HEAD_DIM), cos_table, -sin_table)
        .astype(jnp.bfloat16)
        .reshape(row_count, local_heads * HEAD_DIM)
    )
    key_grad_low = (
        rotate(key_grad, cos_table, -sin_table)
        .astype(jnp.bfloat16)
        .reshape(row_count, local_kv * HEAD_DIM)
    )
    value_grad_low = value_grad.astype(jnp.bfloat16).reshape(row_count, local_kv * HEAD_DIM)
    query_w_grad = jnp.einsum(
        "td,tq->dq", normed_attn, query_grad, preferred_element_type=jnp.float32
    )
    key_w_grad = jnp.einsum(
        "td,tq->dq", normed_attn, key_grad_low, preferred_element_type=jnp.float32
    )
    value_w_grad = jnp.einsum(
        "td,tq->dq", normed_attn, value_grad_low, preferred_element_type=jnp.float32
    )
    attn_in_part = jnp.einsum(
        "tq,dq->td", query_grad, full_query, preferred_element_type=jnp.float32
    )
    attn_in_part = attn_in_part + jnp.einsum(
        "tq,dq->td", key_grad_low, full_key, preferred_element_type=jnp.float32
    )
    attn_in_part = attn_in_part + jnp.einsum(
        "tq,dq->td", value_grad_low, full_value, preferred_element_type=jnp.float32
    )
    attn_in_grad = lax.psum(attn_in_part.astype(jnp.bfloat16), "tp").astype(jnp.float32)
    gain_attn_grad, input_norm_grad = rms_back(inverse_attn, scaled_attn, attn_gain, attn_in_grad)
    tokens_grad = middle_grad + input_norm_grad
    shard_grads = (
        lax.psum_scatter(gain_attn_grad, ("fsdp", "ctx"), scatter_dimension=0, tiled=True),
        lax.psum_scatter(query_w_grad, ("fsdp", "ctx"), scatter_dimension=0, tiled=True),
        lax.psum_scatter(key_w_grad, ("fsdp", "ctx"), scatter_dimension=0, tiled=True),
        lax.psum_scatter(value_w_grad, ("fsdp", "ctx"), scatter_dimension=0, tiled=True),
        lax.psum_scatter(out_w_grad, ("fsdp", "ctx"), scatter_dimension=1, tiled=True),
        lax.psum_scatter(gain_moe_grad, ("fsdp", "ctx"), scatter_dimension=0, tiled=True),
        lax.psum_scatter(router_grad, ("fsdp", "ctx"), scatter_dimension=0, tiled=True),
    )
    return (
        output,
        balance_loss,
        tokens_grad,
        shard_grads[0],
        shard_grads[1],
        shard_grads[2],
        shard_grads[3],
        shard_grads[4],
        shard_grads[5],
        shard_grads[6],
        gate_w_out,
        up_w_out,
        down_w_out,
    )


def solution(mesh):
    return jax.shard_map(
        on_device,
        mesh=mesh,
        in_specs=(
            P(("fsdp", "ctx"), None),
            P("fsdp", None),
            P(("fsdp", "ctx"), None),
            P(("fsdp", "ctx")),
            P(("fsdp", "ctx"), "tp"),
            P(("fsdp", "ctx"), "tp"),
            P(("fsdp", "ctx"), "tp"),
            P("tp", ("fsdp", "ctx")),
            P(("fsdp", "ctx")),
            P(("fsdp", "ctx"), None),
            P("fsdp", None, "tp"),
            P("fsdp", None, "tp"),
            P("fsdp", "tp", None),
            P(("fsdp", "ctx"), None),
            P(),
        ),
        out_specs=(
            P(("fsdp", "ctx"), None),
            P(),
            P(("fsdp", "ctx"), None),
            P(("fsdp", "ctx")),
            P(("fsdp", "ctx"), "tp"),
            P(("fsdp", "ctx"), "tp"),
            P(("fsdp", "ctx"), "tp"),
            P("tp", ("fsdp", "ctx")),
            P(("fsdp", "ctx")),
            P(("fsdp", "ctx"), None),
            P("fsdp", "ctx", "tp"),
            P("fsdp", "ctx", "tp"),
            P("fsdp", "tp", "ctx"),
        ),
        check_vma=False,
    )
```

profile of v0, /device:TPU:11, one launch (start us, length us, event | category | flops | bytes accessed | tf_op | source)
XLA Modules:
  0.0 2150.2 jit_solution(16233661435746792868)
XLA Ops:
  19.4 26.1 %all-reduce.5 = (bf16[1536]{0:T(1024)(128)(2,1)S(1)}, bf16[1536]{0:T(1024)(128)(2,1)}) all-reduce(bf16[1536]{0:T(1024)(128)(2,1)S(1)} %dynamic-update-slice, bf16[1536]{0:T(1024)(128)(2,1)S(1)} %dynamic-update-slice.1), channel_id=1, replica_groups=mesh['fsdp'=8,'ctx'=2,'tp'=2] {'fsdp','ctx'}, use_global_device_ids=true, to_apply=%add | all-reduce | flops 3072 | bytes 12288
  45.4 36.1 %all_gather.28 = bf16[1536,128]{1,0:T(8,128)(2,1)S(1)} all-gather(bf16[96,128]{1,0:T(8,128)(2,1)} %param.28), channel_id=1, replica_groups=mesh['fsdp'=8,'ctx'=2,'tp'=2] {'fsdp','ctx'}, dimensions={0}, use_global_device_ids=true | all-gather | bytes 417792 | tf_op jit(solution)/shard_map/all_gather | solution.py:282
  81.6 33.9 %all_gather.31 = bf16[1536,128]{1,0:T(8,128)(2,1)S(1)} all-gather(bf16[96,128]{1,0:T(8,128)(2,1)} %param.29), channel_id=1, replica_groups=mesh['fsdp'=8,'ctx'=2,'tp'=2] {'fsdp','ctx'}, dimensions={0}, use_global_device_ids=true | all-gather | bytes 417792 | tf_op jit(solution)/shard_map/all_gather | solution.py:283
  125.3 7.9 all_gather.29
  137.3 5.9 while.50
  144.5 10.6 while.51
  167.9 40.7 %all-reduce.11.cloned.1.call-done = f32[512,1536]{1,0:T(8,128)} async-done(((f32[512,1536]{1,0:T(8,128)}), f32[512,1536]{1,0:T(8,128)}) %all-reduce.11.cloned.1.call-update) | async-done | bytes 3145744 | tf_op jit(solution)/shard_map/psum | solution.py:321
  217.7 10.6 reshape.655
  228.3 16.3 scatter_custom_fusion
  250.2 220.8 %all-gather.1 = bf16[16,96,8]{1,2,0:T(8,128)(2,1)S(1)} all-gather(bf16[1,96,8]{1,2,0:T(8,128)(2,1)S(1)} %bitcast.430), channel_id=1, replica_groups=mesh['fsdp'=8,'ctx'=2,'tp'=2] {'fsdp','ctx'}, dimensions={0}, use_global_device_ids=true | all-gather | bytes 26112 | tf_op jit(solution)/shard_map/all_gather | solution.py:286
  471.1 7.1 mul.467
  478.2 14.9 mul.468
  495.3 17.0 scatter_custom_fusion.1
  518.1 9.1 fusion.111
  527.2 9.0 fusion.115
  536.2 185.6 %all-to-all-done.2 = bf16[8,384,1536]{2,1,0:T(8,128)(2,1)} async-done(((bf16[8,384,1536]{2,1,0:T(8,128)(2,1)}), bf16[8,384,1536]{2,1,0:T(8,128)(2,1)}, u32[]{:S(2)}, u32[]{:S(2)}) %all-to-all-start.2) | async-done | bytes 9437216 | tf_op jit(solution)/shard_map/all_to_all | solution.py:379
  721.8 10.9 multiply_convert_fusion.2
  732.8 9.3 fusion.113
  742.1 11.3 add_convert_fusion
  753.3 6.0 all-to-all-start.3
  759.3 7.5 convolution_convert_fusion
  766.8 196.5 %all-to-all-done.3 = bf16[8,384,1536]{2,1,0:T(8,128)(2,1)} async-done(((bf16[8,384,1536]{2,1,0:T(8,128)(2,1)}), bf16[8,384,1536]{2,1,0:T(8,128)(2,1)}, u32[]{:S(2)}, u32[]{:S(2)}) %all-to-all-start.3) | async-done | bytes 9437216 | tf_op jit(solution)/shard_map/all_to_all | solution.py:401
  969.0 18.2 gather_fusion.1
  987.2 12.2 reshape.634
  999.4 12.6 reduce_sum.223
  1016.1 157.1 %all-to-all-done.1 = bf16[8,384,1536]{2,1,0:T(8,128)(2,1)} async-done(((bf16[8,384,1536]{2,1,0:T(8,128)(2,1)}), bf16[8,384,1536]{2,1,0:T(8,128)(2,1)}, u32[]{:S(2)}, u32[]{:S(2)}) %all-to-all-start.1) | async-done | bytes 9437216 | tf_op jit(solution)/shard_map/all_to_all | solution.py:357
  1173.2 18.2 gather_fusion
  1191.3 12.2 reshape.633
  1203.6 16.5 multiply_reduce_fusion
  1223.1 25.3 %psum.51 = f32[8]{0:T(128)S(1)} all-reduce(f32[8]{0:T(128)S(1)} %get-tuple-element.590), channel_id=1, replica_groups=mesh['fsdp'=8,'ctx'=2,'tp'=2] {'fsdp','ctx'}, use_global_device_ids=true, to_apply=%region_23.24 | all-reduce | flops 8 | bytes 64 | tf_op jit(solution)/shard_map/psum | solution.py:334
  1249.1 6.0 multiply_reduce_fusion.2
  1260.2 8.8 while.52
  1271.1 22.9 %while.53 = (s32[]{:T(128)}, f32[512,1,6,128]{0,3,2,1:T(8,128)S(1)}, f32[1024,1,128]{0,2,1:T(8,128)}, f32[1024,1,128]{2,0,1:T(8,128)}, s32[]{:T(128)}, /*index=5...) while((s32[]{:T(128)}, ...), condition=%wide.region_40.41_spmd.clone, body=%wide.region_39.40_spmd.clone.sunk | while | flops 2030765056 | bytes 42127632 | solution.py:220
  1304.1 15.1 reduce-scatter.13.cloned.1.call-done
  1324.9 11.6 reduce-scatter.15.cloned.1.call-done
  1340.4 9.8 convolution_bitcast_fusion.1
  1350.3 9.1 convolution_bitcast_fusion.3
  1359.4 9.5 convolution_bitcast_fusion.2
  1383.4 79.4 %reduce-scatter.31.cloned.1.call-done = f32[96,8]{1,0:T(8,128)} async-done(((f32[1536,8]{1,0:T(8,128)}), f32[96,8]{1,0:T(8,128)}) %reduce-scatter.31.cloned.1.call-update) | async-done | bytes 3088
  1464.3 26.3 %all-reduce.15.cloned.1.call-done = (bf16[512,1536]{1,0:T(8,128)(2,1)}, bf16[512,1536]{1,0:T(8,128)(2,1)}) async-done(((bf16[512,1536]{1,0:T(8,128)(2,1)}, bf16[512,1536]{1,0:T(8,128)(2,1)}), (bf16[512,1536]{1,0:T(8,128)(2,1)}, bf16[512,1536]{1,0:T(8,128)(2,1)})) %all-reduce.15.cloned.1.call-update) | async-done | bytes 3145744 | tf_op jit(solution)/shard_map/psum | solution.py:368
  1493.1 53.3 %all-reduce.4 = (f32[8]{0:T(128)S(1)}, f32[1536]{0:T(1024)S(1)}, f32[1536]{0:T(1024)S(1)}) all-reduce(f32[8]{0:T(128)S(1)} %copy-done.75, f32[1536]{0:T(1024)S(1)} %get-tuple-element.583, f32[1536]{0:T(1024)S(1)} %copy-done.65), channel_id=1, replica_groups=mesh['fsdp'=8,'ctx'=2,'tp'=2] {'fsdp','ctx'}, use_global_device_ids=true, to_apply=%region_25.26 | all-reduce | flops 3080 | bytes 24640 | tf_op jit(solution)/shard_map/psum | solution.py:334
  1548.8 6.9 fusion.101
  1555.7 11.4 reduce-scatter.25.cloned.1.call-done
  1567.1 37.9 %reduce-scatter.27.cloned.1.call-done = f32[1,768,384]{2,1,0:T(8,128)} async-done(((f32[1,1536,384]{2,1,0:T(8,128)}), f32[1,768,384]{2,1,0:T(8,128)}) %reduce-scatter.27.cloned.1.call-update) | async-done | bytes 1179664 | tf_op jit(solution)/shard_map/reduce_scatter | solution.py:450
  1604.9 126.5 %reduce-scatter.19.cloned.1.call-done = f32[96,128]{1,0:T(8,128)} async-done(((f32[1536,128]{1,0:T(8,128)}), f32[96,128]{1,0:T(8,128)}) %reduce-scatter.19.cloned.1.call-update) | async-done | bytes 49168 | tf_op jit(solution)/shard_map/reduce_scatter | solution.py:488
  1731.4 126.6 %reduce-scatter.21.cloned.1.call-done = f32[96,128]{1,0:T(8,128)} async-done(((f32[1536,128]{1,0:T(8,128)}), f32[96,128]{1,0:T(8,128)}) %reduce-scatter.21.cloned.1.call-update) | async-done | bytes 49168 | tf_op jit(solution)/shard_map/reduce_scatter | solution.py:489
  1858.0 141.5 %reduce-scatter.23.cloned.1.call-done = f32[768,96]{0,1:T(8,128)} async-done(((f32[768,1536]{0,1:T(8,128)}), f32[768,96]{0,1:T(8,128)}) %reduce-scatter.23.cloned.1.call-update) | async-done | bytes 294928 | tf_op jit(solution)/shard_map/reduce_scatter | solution.py:490
  1999.5 142.6 %reduce-scatter.17.cloned.1.call-done = f32[96,768]{1,0:T(8,128)} async-done(((f32[1536,768]{1,0:T(8,128)}), f32[96,768]{1,0:T(8,128)}) %reduce-scatter.17.cloned.1.call-update) | async-done | bytes 294928 | tf_op jit(solution)/shard_map/reduce_scatter | solution.py:487
  (360 shorter events, 165.3 us)
Async XLA Ops:
  7.2 714.6 %copy-start = (bf16[1,384,1536]{2,1,0:T(8,128)(2,1)S(1)}, bf16[1,384,1536]{2,1,0:T(8,128)(2,1)}, u32[]{:S(2)}) copy-start(bf16[1,384,1536]{2,1,0:T(8,128)(2,1)} %param.35) | copy-start | bytes 3538948
  7.2 126.2 %all-gather.5.cloned.1.call-start = ((), (), s32[]{:S(2)}) async-start(), calls=%async_computation.14 | async-start | bytes 2506752 | tf_op jit(solution)/shard_map/all_gather | solution.py:281
  7.9 149.3 %all-gather.7.cloned.1.call-start = ((), (), s32[]{:S(2)}) async-start(), calls=%async_computation.15 | async-start | bytes 2506752 | tf_op jit(solution)/shard_map/all_gather | solution.py:284
  8.7 199.9 %all-reduce.11.cloned.1.call-start = ((), (), s32[]{:S(2)}) async-start(), calls=%async_computation.16 | async-start | bytes 6291456 | tf_op jit(solution)/shard_map/psum | solution.py:321
  8.8 116.0 %copy-start.72 = (f32[64]{0:T(128)}, f32[64]{0:T(128)S(1)}, u32[]{:S(2)}) copy-start(f32[64]{0:T(128)S(1)} %negate_power_fusion) | copy-start | bytes 772
  15.5 107.3 %copy-start.63 = (f32[512]{0:T(512)}, f32[512]{0:T(512)S(1)}, u32[]{:S(2)}) copy-start(f32[512]{0:T(512)S(1)} %add_rsqrt_fusion.1) | copy-start | bytes 6148
  15.6 109.1 %copy-start.56 = (f32[512]{0:T(512)}, f32[512]{0:T(512)S(1)}, u32[]{:S(2)}) copy-start(f32[512]{0:T(512)S(1)} %dynamic-slice_convert_fusion) | copy-start | bytes 6148
  45.4 70.1 %copy-start.47 = (f32[1536]{0:T(1024)}, f32[1536]{0:T(1024)S(1)}, u32[]{:S(2)}) copy-start(f32[1536]{0:T(1024)S(1)} %convert_element_type.148) | copy-start | bytes 18436
  81.6 42.0 %copy-start.23 = (bf16[1536,128]{1,0:T(8,128)(2,1)}, bf16[1536,128]{1,0:T(8,128)(2,1)S(1)}, u32[]{:S(2)}) copy-start(bf16[1536,128]{1,0:T(8,128)(2,1)S(1)} %all_gather.28) | copy-start | bytes 1179652
  162.8 45.8 %copy-start.8 = (bf16[512,1536]{1,0:T(8,128)(2,1)S(1)}, bf16[512,1536]{1,0:T(8,128)(2,1)}, u32[]{:S(2)}) copy-start(bf16[512,1536]{1,0:T(8,128)(2,1)} %param.23) | copy-start | bytes 4718596
  164.0 47.0 %copy-start.52 = (f32[1536]{0:T(1024)}, f32[1536]{0:T(1024)S(1)}, u32[]{:S(2)}) copy-start(f32[1536]{0:T(1024)S(1)} %convert_element_type.155) | copy-start | bytes 18436
  213.0 280.2 %copy-start.13 = (bf16[512,1536]{1,0:T(8,128)(2,1)}, bf16[512,1536]{1,0:T(8,128)(2,1)S(1)}, u32[]{:S(2)}) copy-start(bf16[512,1536]{1,0:T(8,128)(2,1)S(1)} %multiply_convert_fusion.5) | copy-start | bytes 4718596
  244.6 267.7 %all-to-all-start = ((bf16[8,384,1536]{2,1,0:T(8,128)(2,1)}), bf16[8,384,1536]{2,1,0:T(8,128)(2,1)}, u32[]{:S(2)}, u32[]{:S(2)}) async-start(bf16[8,384,1536]{2,1,0:T(8,128)(2,1)} %bitcast.410), calls=%async_computation | async-start | bytes 18874368 | tf_op jit(solution)/shard_map/all_to_all | solution.py:351
  471.1 22.1 %copy-start.45 = (bf16[1536,8]{0,1:T(8,128)(2,1)}, bf16[1536,8]{0,1:T(8,128)(2,1)S(1)}, u32[]{:S(2)}) copy-start(bf16[1536,8]{0,1:T(8,128)(2,1)S(1)} %reshape.675) | copy-start | bytes 73732
  493.7 18.6 copy-start.43
  512.3 209.5 %all-to-all-start.2 = ((bf16[8,384,1536]{2,1,0:T(8,128)(2,1)}), bf16[8,384,1536]{2,1,0:T(8,128)(2,1)}, u32[]{:S(2)}, u32[]{:S(2)}) async-start(bf16[8,384,1536]{2,1,0:T(8,128)(2,1)} %bitcast.411), calls=%async_computation.2 | async-start | bytes 18874368 | tf_op jit(solution)/shard_map/all_to_all | solution.py:379
  732.7 26.6 %copy-start.20 = (bf16[3072,384]{1,0:T(8,128)(2,1)}, bf16[3072,384]{1,0:T(8,128)(2,1)S(1)}, u32[]{:S(2)}) copy-start(bf16[3072,384]{1,0:T(8,128)(2,1)S(1)} %get-tuple-element.700) | copy-start | bytes 7077892
  753.3 210.0 %all-to-all-start.3 = ((bf16[8,384,1536]{2,1,0:T(8,128)(2,1)}), bf16[8,384,1536]{2,1,0:T(8,128)(2,1)}, u32[]{:S(2)}, u32[]{:S(2)}) async-start(bf16[8,384,1536]{2,1,0:T(8,128)(2,1)} %bitcast.409), calls=%async_computation.3 | async-start | bytes 18874368 | tf_op jit(solution)/shard_map/all_to_all | solution.py:401
  963.3 209.9 %all-to-all-start.1 = ((bf16[8,384,1536]{2,1,0:T(8,128)(2,1)}), bf16[8,384,1536]{2,1,0:T(8,128)(2,1)}, u32[]{:S(2)}, u32[]{:S(2)}) async-start(bf16[8,384,1536]{2,1,0:T(8,128)(2,1)} %bitcast.412), calls=%async_computation.1 | async-start | bytes 18874368 | tf_op jit(solution)/shard_map/all_to_all | solution.py:357
  969.0 280.1 %all-reduce.13.cloned.1.call-start = ((), (), s32[]{:S(2)}) async-start(), calls=%async_computation.17 | async-start | bytes 6291456 | tf_op jit(solution)/shard_map/psum | solution.py:412
  1012.0 307.2 %reduce-scatter.13.cloned.1.call-start = ((), (), s32[]{:S(2)}) async-start(), calls=%async_computation.18 | async-start | bytes 786432 | tf_op jit(solution)/shard_map/reduce_scatter | solution.py:447
  1203.5 19.4 copy-start.55
  1203.5 19.4 copy-start.61
  1203.5 19.4 copy-start.51
  1203.6 44.9 %copy-start.44 = (f32[512,8]{0,1:T(8,128)S(1)}, f32[512,8]{0,1:T(8,128)}, u32[]{:S(2)}) copy-start(f32[512,8]{0,1:T(8,128)} %copy-done.43) | copy-start | bytes 49156
  1203.6 44.9 %copy-start.59 = (f32[512]{0:T(512)S(1)}, f32[512]{0:T(512)}, u32[]{:S(2)}) copy-start(f32[512]{0:T(512)} %copy-done.58) | copy-start | bytes 6148
  1203.6 44.9 %copy-start.69 = (f32[512]{0:T(512)S(1)}, f32[512]{0:T(512)}, u32[]{:S(2)}) copy-start(f32[512]{0:T(512)} %copy-done.68) | copy-start | bytes 6148
  1203.6 45.5 %copy-start.46 = (bf16[1536,8]{0,1:T(8,128)(2,1)S(1)}, bf16[1536,8]{0,1:T(8,128)(2,1)}, u32[]{:S(2)}) copy-start(bf16[1536,8]{0,1:T(8,128)(2,1)} %copy-done.45) | copy-start | bytes 73732
  1203.6 45.5 %copy-start.53 = (f32[1536]{0:T(1024)S(1)}, f32[1536]{0:T(1024)}, u32[]{:S(2)}) copy-start(f32[1536]{0:T(1024)} %copy-done.52) | copy-start | bytes 18436
  1203.6 45.5 %copy-start.67 = (f32[512]{0:T(512)S(1)}, f32[512]{0:T(512)}, u32[]{:S(2)}) copy-start(f32[512]{0:T(512)} %copy-done.66) | copy-start | bytes 6148
  1294.0 42.5 %reduce-scatter.15.cloned.1.call-start = ((), (), s32[]{:S(2)}) async-start(), calls=%async_computation.19 | async-start | bytes 786432 | tf_op jit(solution)/shard_map/reduce_scatter | solution.py:448
  1294.6 168.3 %reduce-scatter.31.cloned.1.call-start = ((), (), s32[]{:S(2)}) async-start(), calls=%async_computation.27 | async-start | bytes 835584
  1298.8 191.8 %all-reduce.15.cloned.1.call-start = ((), (), s32[]{:S(2)}) async-start(), calls=%async_computation.28 | async-start | bytes 6291456 | tf_op jit(solution)/shard_map/psum | solution.py:368
  1301.0 19.7 copy-start.24
  1340.3 215.4 %reduce-scatter.29.cloned.1.call-start = ((), (), s32[]{:S(2)}) async-start(), calls=%async_computation.26 | async-start | bytes 3538944 | tf_op jit(solution)/shard_map/reduce_scatter | solution.py:451
  1350.2 216.8 %reduce-scatter.25.cloned.1.call-start = ((), (), s32[]{:S(2)}) async-start(), calls=%async_computation.24 | async-start | bytes 3538944 | tf_op jit(solution)/shard_map/reduce_scatter | solution.py:449
  1359.4 245.6 %reduce-scatter.27.cloned.1.call-start = ((), (), s32[]{:S(2)}) async-start(), calls=%async_computation.25 | async-start | bytes 3538944 | tf_op jit(solution)/shard_map/reduce_scatter | solution.py:450
  1369.0 362.5 %reduce-scatter.19.cloned.1.call-start = ((), (), s32[]{:S(2)}) async-start(), calls=%async_computation.21 | async-start | bytes 835584 | tf_op jit(solution)/shard_map/reduce_scatter | solution.py:488
  1370.6 487.5 %reduce-scatter.21.cloned.1.call-start = ((), (), s32[]{:S(2)}) async-start(), calls=%async_computation.22 | async-start | bytes 835584 | tf_op jit(solution)/shard_map/reduce_scatter | solution.py:489
  1372.2 627.4 %reduce-scatter.23.cloned.1.call-start = ((), (), s32[]{:S(2)}) async-start(), calls=%async_computation.23 | async-start | bytes 5013504 | tf_op jit(solution)/shard_map/reduce_scatter | solution.py:490
  1377.9 764.2 %reduce-scatter.17.cloned.1.call-start = ((), (), s32[]{:S(2)}) async-start(), calls=%async_computation.20 | async-start | bytes 5013504 | tf_op jit(solution)/shard_map/reduce_scatter | solution.py:487
  1382.6 108.0 %copy-start.9 = (bf16[512,1536]{1,0:T(8,128)(2,1)S(1)}, bf16[512,1536]{1,0:T(8,128)(2,1)}, u32[]{:S(2)}) copy-start(bf16[512,1536]{1,0:T(8,128)(2,1)} %param.23) | copy-start | bytes 4718596
  1382.6 108.0 %copy-start.48 = (f32[1536]{0:T(1024)S(1)}, f32[1536]{0:T(1024)}, u32[]{:S(2)}) copy-start(f32[1536]{0:T(1024)} %copy-done.47) | copy-start | bytes 18436
  1382.6 108.0 %copy-start.64 = (f32[512]{0:T(512)S(1)}, f32[512]{0:T(512)}, u32[]{:S(2)}) copy-start(f32[512]{0:T(512)} %copy-done.63) | copy-start | bytes 6148
  1382.6 110.4 %copy-start.65 = (f32[1536]{0:T(1024)S(1)}, f32[1536]{0:T(1024)}, u32[]{:S(2)}) copy-start(f32[1536]{0:T(1024)} %get-tuple-element.581) | copy-start | bytes 18436
  1382.6 110.4 %copy-start.75 = (f32[8]{0:T(128)S(1)}, f32[8]{0:T(128)}, u32[]{:S(2)}) copy-start(f32[8]{0:T(128)} %get-tuple-element.588) | copy-start | bytes 100
  1382.7 164.9 %copy-start.80 = (f32[8]{0:T(128)S(1)}, f32[8]{0:T(128)}, u32[]{:S(2)}) copy-start(f32[8]{0:T(128)} %copy-done.79) | copy-start | bytes 100
  1548.8 593.3 %copy-start.1 = (bf16[1,384,1536]{2,1,0:T(8,128)(2,1)S(1)}, bf16[1,384,1536]{2,1,0:T(8,128)(2,1)}, u32[]{:S(2)}) copy-start(bf16[1,384,1536]{2,1,0:T(8,128)(2,1)} %param.35) | copy-start | bytes 3538948
  (53 other events, 329.8 us)
Sparse Core Ops, SparseCore 0:
  10.8 64.2 all-gather.4
  77.9 66.1 all-gather.6
  163.0 45.5 all-reduce.10
  1012.1 26.3 all-reduce.12
  1294.1 24.9 reduce-scatter.12
  1321.9 14.5 reduce-scatter.14
  1341.2 121.5 reduce-scatter.30
  1465.8 24.7 all-reduce.14
  1493.5 35.5 reduce-scatter.28
  1531.8 35.2 reduce-scatter.24
  1570.0 34.9 reduce-scatter.26
  1610.1 121.3 reduce-scatter.18
  1736.7 121.2 reduce-scatter.20
  1863.6 135.8 reduce-scatter.22
  2005.9 136.1 reduce-scatter.16
where the time goes:
time: 2160 us; the launch traced here: 2150 us
  waiting for transfers between devices  1300 us (60%)
  blocking collectives  411 us (19%)
  matrix products  167 us (8%)
  local copies, waits for them, and re-layouts  144 us (7%)
  other arithmetic  80.2 us (4%)
  starting transfers between devices  24.5 us (1%)
  between operations  22 us (1%)
    all_gather x1, blocking collectives, on_device(): lax.all_gather(w_router, ('fsdp', 'ctx'), axis=0, tiled=True)  221 us
    all_to_all x1, waiting for transfers between devices, on_device(): lax.all_to_all(from_expert(grad_rows, fsdp_count, capacity), 'fsdp', spli...  196 us
    all_to_all x1, waiting for transfers between devices, on_device(): lax.all_to_all(grad_send, 'fsdp', split_axis=0, concat_axis=0, tiled=True)  186 us
    all_to_all x1, waiting for transfers between devices, on_device(): lax.all_to_all(from_expert(expert_out, fsdp_count, capacity), 'fsdp', spl...  157 us
    reduce_scatter x1, waiting for transfers between devices, on_device(): lax.psum_scatter(query_w_grad, ('fsdp', 'ctx'), scatter_dimension=0, tile...  143 us
    reduce_scatter x1, waiting for transfers between devices, on_device(): lax.psum_scatter(out_w_grad, ('fsdp', 'ctx'), scatter_dimension=1, tiled=...  142 us
    reduce_scatter x1, waiting for transfers between devices, on_device(): lax.psum_scatter(value_w_grad, ('fsdp', 'ctx'), scatter_dimension=0, tile...  127 us
    reduce_scatter x1, waiting for transfers between devices, on_device(): lax.psum_scatter(key_w_grad, ('fsdp', 'ctx'), scatter_dimension=0, tiled=...  126 us
  transfers between devices with their start and end apart: 19, of which 14 were waited for; matrix products, arithmetic and copies ran while one was open for 12% of the time, Pallas kernels for 0%

commit v1 on v0

--- a/solution.py
+++ b/solution.py
@@ -1,15 +1,20 @@
+import functools
+
 import jax
+import jax.experimental.pallas as pl
+import jax.experimental.pallas.tpu as pltpu
 import jax.numpy as jnp
 from jax import lax
 from jax.sharding import PartitionSpec as P
 
 HEAD_DIM = 128
-
-
+SHARE = 2
 epsilon = 1e-06
 rope_base = 10000.0
 masked_score = -1e30
 highest = lax.Precision.HIGHEST
+f32 = jnp.float32
+bf16 = jnp.bfloat16
 
 
 def rms_parts(values, row_gains):
@@ -19,18 +24,14 @@
 
 
 def rms_back(inverse, scaled, row_gains, upstream):
-    gain_grad = jnp.sum(upstream * scaled, axis=0)
     scaled_grad = upstream * row_gains
-    return (
-        gain_grad,
-        inverse * (scaled_grad - scaled * jnp.mean(scaled_grad * scaled, axis=-1, keepdims=True)),
-    )
+    return inverse * (scaled_grad - scaled * jnp.mean(scaled_grad * scaled, axis=-1, keepdims=True))
 
 
 def rope_tables(positions):
     half_dim = HEAD_DIM // 2
-    frequency = rope_base ** (-(jnp.arange(half_dim, dtype=jnp.float32) * (2.0 / HEAD_DIM)))
-    angles = positions.astype(jnp.float32)[:, None] * frequency[None, :]
+    frequency = rope_base ** (-(jnp.arange(half_dim, dtype=f32) * (2.0 / HEAD_DIM)))
+    angles = positions.astype(f32)[:, None] * frequency[None, :]
     return (jnp.cos(angles)[:, None, :], jnp.sin(angles)[:, None, :])
 
 
@@ -71,7 +72,7 @@
 def block_scores(query_block, key_block, query_docs, query_index, key_docs, key_index):
     scale_factor = HEAD_DIM ** (-0.5)
     scores = (
-        jnp.einsum("qhgd,khd->hgqk", query_block, key_block, preferred_element_type=jnp.float32)
+        jnp.einsum("qhgd,khd->hgqk", query_block, key_block, preferred_element_type=f32)
         * scale_factor
     )
     allowed = (query_docs[:, None] == key_docs[None, :]) & (
@@ -90,9 +91,8 @@
 
 def attention_forward(grouped, pack_keys, pack_values, doc_ids, doc_first, base_row, block_rows):
     row_count, local_kv, group_size, head_dim = grouped.shape
-    start_row = base_row + 0
     query_index, query_docs, low_block, high_block = query_block_range(
-        start_row, block_rows, doc_ids, doc_first
+        base_row, block_rows, doc_ids, doc_first
     )
 
     def scan_maxima(key_number, running):
@@ -107,8 +107,8 @@
         weights = jnp.where(allowed, jnp.exp(scores - new_max[..., None]), 0.0)
         return (new_max, totals * jnp.exp(maxima - new_max) + jnp.sum(weights, axis=-1))
 
-    start_max = jnp.full((local_kv, group_size, block_rows), masked_score, jnp.float32)
-    start_total = jnp.zeros((local_kv, group_size, block_rows), jnp.float32)
+    start_max = jnp.full((local_kv, group_size, block_rows), masked_score, f32)
+    start_total = jnp.zeros((local_kv, group_size, block_rows), f32)
     maxima, totals = lax.fori_loop(low_block, high_block, scan_maxima, (start_max, start_total))
     log_total = maxima + jnp.log(totals)
 
@@ -119,45 +119,32 @@
         scores, allowed = block_scores(
             grouped, key_block, query_docs, query_index, key_docs, key_index
         )
-        block_probs = jnp.where(allowed, jnp.exp(scores - log_total[..., None]), 0.0).astype(
-            jnp.bfloat16
-        )
+        block_probs = jnp.where(allowed, jnp.exp(scores - log_total[..., None]), 0.0).astype(bf16)
         return summed + jnp.einsum(
-            "hgqk,khd->hgqd", block_probs, value_block, preferred_element_type=jnp.float32
+            "hgqk,khd->hgqd", block_probs, value_block, preferred_element_type=f32
         )
 
     summed = lax.fori_loop(
         low_block,
         high_block,
         accumulate,
-        jnp.zeros((local_kv, group_size, block_rows, head_dim), jnp.float32),
+        jnp.zeros((local_kv, group_size, block_rows, head_dim), f32),
     )
     outputs = summed.transpose(2, 0, 1, 3).reshape(block_rows, local_kv * group_size * head_dim)
-    totals_list = [log_total]
-    return (outputs, totals_list)
+    return (outputs, log_total)
 
 
 def attention_backward(
-    grouped,
-    pack_keys,
-    pack_values,
-    grad_mixed,
-    totals_list,
-    doc_ids,
-    doc_first,
-    base_row,
-    block_rows,
+    grouped, pack_keys, pack_values, grad_mixed, log_total, doc_ids, doc_first, base_row, block_rows
 ):
     row_count, local_kv, group_size, head_dim = grouped.shape
     pack_count = pack_keys.shape[0]
     scale_factor = HEAD_DIM ** (-0.5)
     grad_grouped = grad_mixed.reshape(row_count, local_kv, group_size, head_dim)
-    key_acc = jnp.zeros((pack_count, local_kv, head_dim), jnp.float32)
-    value_acc = jnp.zeros((pack_count, local_kv, head_dim), jnp.float32)
-    start_row = base_row + 0
-    log_total = totals_list[0]
+    key_acc = jnp.zeros((pack_count, local_kv, head_dim), f32)
+    value_acc = jnp.zeros((pack_count, local_kv, head_dim), f32)
     query_index, query_docs, low_block, high_block = query_block_range(
-        start_row, block_rows, doc_ids, doc_first
+        base_row, block_rows, doc_ids, doc_first
     )
 
     def probs_at(key_number):
@@ -169,7 +156,7 @@
         )
         block_probs = jnp.where(allowed, jnp.exp(scores - log_total[..., None]), 0.0)
         prob_grad = jnp.einsum(
-            "qhgd,khd->hgqk", grad_grouped, value_block, preferred_element_type=jnp.float32
+            "qhgd,khd->hgqk", grad_grouped, value_block, preferred_element_type=f32
         )
         return (key_start, key_block, block_probs, prob_grad)
 
@@ -178,29 +165,24 @@
         return row_delta + jnp.sum(pieces[2] * pieces[3], axis=-1)
 
     row_delta = lax.fori_loop(
-        low_block, high_block, add_delta, jnp.zeros((local_kv, group_size, block_rows), jnp.float32)
+        low_block, high_block, add_delta, jnp.zeros((local_kv, group_size, block_rows), f32)
     )
 
     def add_grads(key_number, running):
         query_acc, key_total, value_total = running
         key_start, key_block, block_probs, prob_grad = probs_at(key_number)
-        score_grad = (block_probs * (prob_grad - row_delta[..., None])).astype(jnp.bfloat16)
+        score_grad = (block_probs * (prob_grad - row_delta[..., None])).astype(bf16)
         query_acc = (
             query_acc
-            + jnp.einsum(
-                "hgqk,khd->qhgd", score_grad, key_block, preferred_element_type=jnp.float32
-            )
+            + jnp.einsum("hgqk,khd->qhgd", score_grad, key_block, preferred_element_type=f32)
             * scale_factor
         )
         key_piece = (
-            jnp.einsum("hgqk,qhgd->khd", score_grad, grouped, preferred_element_type=jnp.float32)
+            jnp.einsum("hgqk,qhgd->khd", score_grad, grouped, preferred_element_type=f32)
             * scale_factor
         )
         value_piece = jnp.einsum(
-            "hgqk,qhgd->khd",
-            block_probs.astype(jnp.bfloat16),
-            grad_grouped,
-            preferred_element_type=jnp.float32,
+            "hgqk,qhgd->khd", block_probs.astype(bf16), grad_grouped, preferred_element_type=f32
         )
         key_total = lax.dynamic_update_slice_in_dim(
             key_total,
@@ -216,11 +198,660 @@
         )
         return (query_acc, key_total, value_total)
 
-    start_query = jnp.zeros((block_rows, local_kv, group_size, head_dim), jnp.float32)
-    query_acc, key_acc, value_acc = lax.fori_loop(
-        low_block, high_block, add_grads, (start_query, key_acc, value_acc)
-    )
-    return (query_acc, key_acc, value_acc)
+    start_query = jnp.zeros((block_rows, local_kv, group_size, head_dim), f32)
+    return lax.fori_loop(low_block, high_block, add_grads, (start_query, key_acc, value_acc))
+
+
+def dot(left, right, left_dim=1, right_dim=0):
+    return lax.dot_general(
+        left, right, (((left_dim,), (right_dim,)), ((), ())), preferred_element_type=f32
+    )
+
+
+def swap(array, axis, bit=1):
+    return lax.ppermute(array, axis, [(i, i ^ bit) for i in range(lax.axis_size(axis))])
+
+
+def bit_at(axis, bit):
+    return (lax.axis_index(axis) // bit) % 2
+
+
+def side_by_side(mine, theirs, place, axis=0):
+    first = jnp.where(place == 0, mine, theirs)
+    return jnp.concatenate([first, jnp.where(place == 0, theirs, mine)], axis=axis)
+
+
+def fsdp_bits():
+    size = lax.axis_size("fsdp")
+    return [size >> (k + 1) for k in range(size.bit_length() - 1)]
+
+
+def weight_dims():
+    return [("fsdp", bit) for bit in fsdp_bits()] + [("ctx", 1)]
+
+
+def weight_orders():
+    high = [("fsdp", bit) for bit in fsdp_bits()[:-1]]
+    low, across = ("fsdp", 1), ("ctx", 1)
+    return [high + [across, low], [across, low] + high, [low] + high + [across]]
+
+
+def gather_rows(block, order):
+    dims = weight_dims()
+    held = block.reshape((1,) * len(dims) + block.shape)
+    for dim in order:
+        held = side_by_side(held, swap(held, *dim), bit_at(*dim), dims.index(dim))
+    return held.reshape(-1, block.shape[-1])
+
+
+def reduce_rows(full, order):
+    dims = weight_dims()
+    rows = full.shape[0] >> len(dims)
+    held = full.reshape((2,) * len(dims) + (rows, full.shape[-1]))
+    for dim in reversed(order):
+        place, k = bit_at(*dim), dims.index(dim)
+        sent = lax.dynamic_index_in_dim(held, 1 - place, k).astype(bf16)
+        held = lax.dynamic_index_in_dim(held, place, k) + swap(sent, *dim).astype(f32)
+    return held.reshape(rows, full.shape[-1])
+
+
+def thirds(array, pieces):
+    units = array.shape[-1] // 128
+    ends = [units * k // pieces * 128 for k in range(pieces + 1)]
+    return [array[..., a:b] for a, b in zip(ends[:-1], ends[1:])]
+
+
+def gather_weights(block, orders):
+    parts = thirds(block, len(orders))
+    return jnp.concatenate([gather_rows(p, o) for p, o in zip(parts, orders)], axis=1)
+
+
+def reduce_weights(full, orders):
+    parts = thirds(full, len(orders))
+    return jnp.concatenate([reduce_rows(p, o) for p, o in zip(parts, orders)], axis=1)
+
+
+def token_bits():
+    return [bit for bit in fsdp_bits() if bit != SHARE]
+
+
+def gather_tokens(block):
+    held = {0: block}
+    for bit in token_bits():
+        held.update({r ^ bit: swap(b, "fsdp", bit) for r, b in held.items()})
+    return held
+
+
+def reduce_tokens(parts):
+    held = dict(parts)
+    for bit in reversed(token_bits()):
+        for r in sorted(held):
+            if r & bit:
+                got = swap(held.pop(r).astype(bf16), "fsdp", bit)
+                held[r ^ bit] = held[r ^ bit] + got.astype(f32)
+    return held[0]
+
+
+def sum_everywhere(small):
+    small = small + swap(small, "tp")
+    small = small + swap(small, "ctx")
+    for bit in fsdp_bits():
+        small = small + swap(small, "fsdp", bit)
+    return small
+
+
+def as_pair(values):
+    high = lax.reduce_precision(values, 8, 7)
+    return [high.astype(bf16), (values - high).astype(bf16)]
+
+
+def widen(columns):
+    width = sum(c.shape[1] for c in columns)
+    pad = jnp.zeros((columns[0].shape[0], -width % 128), columns[0].dtype)
+    return jnp.concatenate(list(columns) + [pad], axis=1)
+
+
+def from_pair(columns, count):
+    return columns[:, :count].astype(f32) + columns[:, count : 2 * count].astype(f32)
+
+
+def own_part(array, place, axis=0):
+    size = array.shape[axis] // 2
+    return lax.dynamic_slice_in_dim(array, place * size, size, axis)
+
+
+def across_ctx(kept, axis=0):
+    place = lax.axis_index("ctx")
+    sent = own_part(kept, 1 - place, axis).astype(bf16)
+    return own_part(kept, place, axis) + swap(sent, "ctx").astype(f32)
+
+
+def across_share(kept, axis=1):
+    size = kept.shape[axis] // 2
+    own = lax.slice_in_dim(kept, 0, size, axis=axis)
+    sent = lax.slice_in_dim(kept, size, None, axis=axis).astype(bf16)
+    return own + swap(sent, "fsdp", SHARE).astype(f32)
+
+
+MESH = pl.DeviceIdType.MESH
+
+
+def peer(fsdp_bit=0, ctx_bit=0, tp_bit=0):
+    return (
+        lax.axis_index("fsdp") ^ fsdp_bit,
+        lax.axis_index("ctx") ^ ctx_bit,
+        lax.axis_index("tp") ^ tp_bit,
+    )
+
+
+def greet(peers):
+    barrier = pltpu.get_barrier_semaphore()
+    for who in peers:
+        pl.semaphore_signal(barrier, inc=1, device_id=who, device_id_type=MESH)
+    pl.semaphore_wait(barrier, len(peers))
+
+
+def send(src, dst, sems, k, who):
+    copy = pltpu.make_async_remote_copy(
+        src_ref=src,
+        dst_ref=dst,
+        send_sem=sems[0].at[k],
+        recv_sem=sems[1].at[k],
+        device_id=who,
+        device_id_type=MESH,
+    )
+    copy.start()
+    return copy
+
+
+def dot_nn(a, b):
+    return lax.dot_general(a, b, (((1,), (0,)), ((), ())), preferred_element_type=f32)
+
+
+def dot_nt(a, b):
+    return lax.dot_general(a, b, (((1,), (1,)), ((), ())), preferred_element_type=f32)
+
+
+def aligned(index, size):
+    return pl.ds(pl.multiple_of(index * size, size), size)
+
+
+TILE = 256
+
+
+def expert_kernel(
+    far,
+    near,
+    experts,
+    x_ref,
+    g_hbm,
+    wg_hbm,
+    wu_hbm,
+    wd_hbm,
+    dx_ref,
+    part_ref,
+    keep_gu,
+    got_gu,
+    keep_d,
+    got_d,
+    xb,
+    gb,
+    wg,
+    wu,
+    wd,
+    h0,
+    hw,
+    dg,
+    du,
+    db,
+    d0,
+    near_in,
+    near_sum,
+    far_in,
+    far_out,
+    keep_stage,
+    send_stage,
+    local_sems,
+    stage_sems,
+    send_sems,
+    recv_sems,
+    tp_send,
+    tp_recv,
+):
+    half = x_ref.shape[0]
+    quarter = half // 2
+    width = wg.shape[0]
+    units = wg.shape[1]
+    unit_tiles = units // TILE
+    sems = (send_sems, recv_sems)
+    far_dev, near_dev, core_dev = peer(far), peer(near), peer(0, 0, 1)
+    greet([far_dev, near_dev, core_dev])
+
+    far_rows = [pl.ds(2 * half + k * half, quarter) for k in range(2)]
+    cross_rows = [pl.ds(2 * half + k * half + quarter, quarter) for k in range(2)]
+    near_rows = pl.ds(half, half)
+    own_half = [pl.ds(k * quarter, quarter) for k in range(2)]
+    far_copy = [send(x_ref.at[own_half[k]], xb.at[far_rows[k]], sems, k, far_dev) for k in range(2)]
+    near_copy = send(x_ref, xb.at[near_rows], sems, 2, near_dev)
+    loads = []
+    for k, (src, dst) in enumerate([(g_hbm, gb), (wd_hbm, wd), (wg_hbm, wg), (wu_hbm, wu)]):
+        loads.append(pltpu.make_async_copy(src, dst, local_sems.at[k]))
+        loads[-1].start()
+    xb[0:half, :] = x_ref[...]
+    loads[0].wait()
+    loads[1].wait()
+
+    def back_tile(j, carry):
+        h0[:, aligned(j, TILE)] = dot_nt(gb[...], wd[aligned(j, TILE), :])
+        return carry
+
+    lax.fori_loop(0, unit_tiles, back_tile, 0)
+    loads[2].wait()
+    loads[3].wait()
+
+    lane = lax.broadcasted_iota(jnp.int32, (half, x_ref.shape[1] - width), 1)
+    own = lax.axis_index("fsdp")
+    partner = own ^ SHARE
+
+    def task(number):
+        rows = pl.ds(number * half, half)
+        extra = xb[rows, width:].astype(f32)
+
+        def gate_of(expert):
+            mine = (lane == expert) | (lane == experts + expert)
+            return jnp.sum(jnp.where(mine, extra, 0.0), axis=1, keepdims=True)
+
+        gates = jnp.concatenate([gate_of(own), gate_of(partner)], axis=1)
+
+        def unit_tile(j, dots):
+            cols = aligned(j, TILE)
+            is_own = j < unit_tiles // 2
+            gate = jnp.where(is_own, gates[:, :1], gates[:, 1:])
+            x = xb[rows, :width]
+            gate_pre = dot_nn(x, wg[:, cols])
+            up_pre = dot_nn(x, wu[:, cols])
+            back = h0[rows, cols]
+            sig = 1.0 / (1.0 + jnp.exp(-gate_pre))
+            silu = gate_pre * sig
+            hidden = silu * up_pre
+            hw[rows, cols] = (hidden * gate).astype(bf16)
+            hidden_grad = back * gate
+            dg[rows, cols] = (hidden_grad * up_pre * (sig * (1.0 + gate_pre * (1.0 - sig)))).astype(bf16)
+            du[rows, cols] = (hidden_grad * silu).astype(bf16)
+            one = jnp.sum(hidden * back, axis=1, keepdims=True)
+            return (
+                dots[0] + jnp.where(is_own, one, 0.0),
+                dots[1] + jnp.where(is_own, 0.0, one),
+            )
+
+        zero = jnp.zeros((half, 1), f32)
+        dots = lax.fori_loop(0, unit_tiles, unit_tile, (zero, zero))
+
+        def put(cols, value):
+            if number == 0:
+                d0[:, cols] = value
+            else:
+                db[rows, cols] = value.astype(bf16)
+
+        def in_tile(n, carry):
+            cols = aligned(n, 2 * TILE)
+            value = dot_nt(dg[rows, :], wg[cols, :]) + dot_nt(du[rows, :], wu[cols, :])
+            put(cols, value)
+            return carry
+
+        lax.fori_loop(0, width // (2 * TILE), in_tile, 0)
+        columns = jnp.zeros_like(extra)
+        for expert, value in ((own, dots[0]), (partner, dots[1])):
+            high = value.astype(bf16).astype(f32)
+            columns = jnp.where(lane == expert, high, columns)
+            columns = jnp.where(lane == experts + expert, value - high, columns)
+        put(slice(width, None), columns)
+
+    def forward(k):
+        return send(xb.at[far_rows[k]], xb.at[cross_rows[k]], sems, 3 + k, near_dev)
+
+    def cross_back(k):
+        return send(db.at[cross_rows[k]], near_in.at[own_half[k]], sems, 5 + k, near_dev)
+
+    def far_back(k):
+        crossed[k].wait_recv()
+        total = db[far_rows[k], :].astype(f32) + near_in[own_half[k], :].astype(f32)
+        far_out[own_half[k], :] = total.astype(bf16)
+        return send(far_out.at[own_half[k]], far_in.at[own_half[k]], sems, 7 + k, far_dev)
+
+    def part_tile(j, carry):
+        cols = aligned(j, 2 * TILE)
+        part_ref[:, cols] = dot_nn(hw[...], wd[:, cols]).astype(bf16)
+        return carry
+
+    task(0)
+    far_copy[0].wait_recv()
+    forwards = [forward(0)]
+    near_copy.wait_recv()
+    task(1)
+    forwards[0].wait_recv()
+    task(2)
+    crossed = [cross_back(0)]
+    far_copy[1].wait_recv()
+    forwards.append(forward(1))
+    backs = [far_back(0)]
+    forwards[1].wait_recv()
+    task(3)
+    crossed.append(cross_back(1))
+    near_back = send(db.at[near_rows], near_sum, sems, 9, near_dev)
+    lax.fori_loop(0, width // (2 * TILE), part_tile, 0)
+    backs.append(far_back(1))
+
+    piece = units // 4
+    tiles = width // TILE
+
+    def stage_copies(slot, number, rows, size, keep, got):
+        return (
+            pltpu.make_async_copy(
+                keep_stage.at[slot, pl.ds(0, size)], keep.at[rows], stage_sems.at[slot]
+            ),
+            pltpu.make_async_remote_copy(
+                src_ref=send_stage.at[slot, pl.ds(0, size)],
+                dst_ref=got.at[rows],
+                send_sem=tp_send.at[slot],
+                recv_sem=tp_recv.at[number],
+                device_id=core_dev,
+                device_id_type=MESH,
+            ),
+        )
+
+    def wait_stage(slot, size, keep, got):
+        local, remote = stage_copies(slot, 0, pl.ds(0, size), size, keep, got)
+        local.wait()
+        remote.wait_send()
+
+    def gate_up_tile(i, carry):
+        rows = aligned(i, TILE)
+        slot = lax.rem(i, 2)
+
+        @pl.when(i >= 2)
+        def _():
+            wait_stage(slot, TILE, keep_gu, got_gu)
+
+        flipped = xb[:, rows].T
+        for k, source in enumerate((dg, du)):
+            for p in range(4):
+                value = dot_nn(flipped, source[:, p * piece : (p + 1) * piece]).astype(bf16)
+                at = (2 * k + p // 2) * piece
+                stage = keep_stage if p % 2 == 0 else send_stage
+                stage[slot, :, at : at + piece] = value
+        for copy in stage_copies(slot, i, rows, TILE, keep_gu, got_gu):
+            copy.start()
+        return carry
+
+    lax.fori_loop(0, tiles, gate_up_tile, 0)
+    wait_stage(0, TILE, keep_gu, got_gu)
+    wait_stage(1, TILE, keep_gu, got_gu)
+    down_rows = 2 * piece // 6
+
+    def down_tile(i, carry):
+        which, within = i // 3, lax.rem(i, 3)
+        rows = aligned(i, down_rows)
+        slot = lax.rem(i, 2)
+
+        @pl.when(i >= 2)
+        def _():
+            wait_stage(slot, down_rows, keep_d, got_d)
+
+        start = which * 2 * piece + within * down_rows
+        for stage, offset in ((keep_stage, 0), (send_stage, piece)):
+            cols = pl.ds(pl.multiple_of(start + offset, 128), down_rows)
+            flipped = hw[:, cols].T
+            for n in range(0, width, 2 * TILE):
+                stage[slot, :down_rows, n : n + 2 * TILE] = dot_nn(flipped, gb[:, n : n + 2 * TILE]).astype(bf16)
+        for copy in stage_copies(slot, tiles + i, rows, down_rows, keep_d, got_d):
+            copy.start()
+        return carry
+
+    lax.fori_loop(0, 6, down_tile, 0)
+    wait_stage(0, down_rows, keep_d, got_d)
+    wait_stage(1, down_rows, keep_d, got_d)
+
+    near_back.wait_recv()
+    backs[0].wait_recv()
+    backs[1].wait_recv()
+    dx_ref[...] = d0[...] + near_sum[...].astype(f32) + far_in[...].astype(f32)
+    for i in range(tiles):
+        stage_copies(0, i, pl.ds(0, TILE), TILE, keep_gu, got_gu)[1].wait_recv()
+    for i in range(6):
+        stage_copies(0, tiles + i, pl.ds(0, down_rows), down_rows, keep_d, got_d)[1].wait_recv()
+    for copy in far_copy + [near_copy, near_back] + forwards + crossed + backs:
+        copy.wait_send()
+
+
+def experts_on_chip(payload, grad_rows, gate, up, down, experts):
+    half, wide = payload.shape
+    rows, width = grad_rows.shape
+    units = gate.shape[1]
+    far, near = token_bits()
+    any_spec = pl.BlockSpec(memory_space=pl.ANY)
+    vmem = pl.BlockSpec(memory_space=pltpu.VMEM)
+    return pl.pallas_call(
+        functools.partial(expert_kernel, far, near, experts),
+        name="experts",
+        out_shape=(
+            jax.ShapeDtypeStruct((half, wide), f32),
+            jax.ShapeDtypeStruct((rows, width), bf16),
+            jax.ShapeDtypeStruct((width, units), bf16),
+            jax.ShapeDtypeStruct((width, units), bf16),
+            jax.ShapeDtypeStruct((units // 2, width), bf16),
+            jax.ShapeDtypeStruct((units // 2, width), bf16),
+        ),
+        in_specs=[vmem, any_spec, any_spec, any_spec, any_spec],
+        out_specs=(vmem, vmem, any_spec, any_spec, any_spec, any_spec),
+        scratch_shapes=[
+            pltpu.VMEM((rows, wide), bf16),
+            pltpu.VMEM((rows, width), bf16),
+            pltpu.VMEM((width, units), bf16),
+            pltpu.VMEM((width, units), bf16),
+            pltpu.VMEM((units, width), bf16),
+            pltpu.VMEM((rows, units), f32),
+            pltpu.VMEM((rows, units), bf16),
+            pltpu.VMEM((rows, units), bf16),
+            pltpu.VMEM((rows, units), bf16),
+            pltpu.VMEM((rows, wide), bf16),
+            pltpu.VMEM((half, wide), f32),
+            pltpu.VMEM((half, wide), bf16),
+            pltpu.VMEM((half, wide), bf16),
+            pltpu.VMEM((half, wide), bf16),
+            pltpu.VMEM((half, wide), bf16),
+            pltpu.VMEM((2, TILE, units), bf16),
+            pltpu.VMEM((2, TILE, units), bf16),
+            pltpu.SemaphoreType.DMA((4,)),
+            pltpu.SemaphoreType.DMA((2,)),
+            pltpu.SemaphoreType.DMA((10,)),
+            pltpu.SemaphoreType.DMA((10,)),
+            pltpu.SemaphoreType.DMA((2,)),
+            pltpu.SemaphoreType.DMA((width // TILE + 6,)),
+        ],
+        compiler_params=pltpu.CompilerParams(
+            collective_id=1, has_side_effects=True, vmem_limit_bytes=62 * 1024 * 1024
+        ),
+        cost_estimate=pl.CostEstimate(
+            flops=2 * 9 * rows * width * units, bytes_accessed=60_000_000, transcendentals=rows * units
+        ),
+    )(payload, grad_rows, gate, up, down)
+
+
+class Exchange:
+    def __init__(self, send_sems, recv_sems, local_sems):
+        self.sems = (send_sems, recv_sems)
+        self.local_sems = local_sems
+        self.all = []
+        self.local = []
+        self.arrived = set()
+
+    def start(self, src, dst, who):
+        self.all.append(send(src, dst, self.sems, len(self.all), who))
+        return len(self.all) - 1
+
+    def keep(self, src, dst):
+        copy = pltpu.make_async_copy(src, dst, self.local_sems.at[len(self.local)])
+        copy.start()
+        self.local.append(copy)
+
+    def arrive(self, number):
+        if number not in self.arrived:
+            self.arrived.add(number)
+            self.all[number].wait_recv()
+
+    def finish(self):
+        for number in range(len(self.all)):
+            self.arrive(number)
+        for copy in self.all:
+            copy.wait_send()
+        for copy in self.local:
+            copy.wait()
+
+
+class RowGather:
+    def __init__(self, net, block, full, part, order):
+        self.net, self.full, self.order = net, full, order
+        self.rows, self.first, self.size = block.shape[0], part[0], part[1]
+        self.copies = {}
+        self.spread((0, 0), -1, block.at[pl.ds(self.first, self.size)])
+
+    def place(self, code):
+        index = (lax.axis_index("fsdp") ^ code[0]) * 2 + (lax.axis_index("ctx") ^ code[1])
+        return pl.ds(pl.multiple_of(index * self.rows + self.first, 16), self.size)
+
+    def spread(self, code, last, src):
+        for position in range(last + 1, len(self.order)):
+            axis, bit = self.order[position]
+            other = (code[0] ^ bit, code[1]) if axis == "fsdp" else (code[0], code[1] ^ bit)
+            copy = self.net.start(src, self.full.at[self.place(code)], dim_peer((axis, bit)))
+            self.copies[other] = (copy, position)
+
+    def arrive(self, code):
+        copy, position = self.copies[code]
+        self.net.arrive(copy)
+        self.spread(code, position, self.full.at[self.place(code)])
+
+
+def dim_peer(dim):
+    axis, bit = dim
+    return peer(bit if axis == "fsdp" else 0, bit if axis == "ctx" else 0)
+
+
+def gather_codes(far, near):
+    first = [(SHARE, 0), (far, 0), (far ^ SHARE, 0)]
+    rest = [(0, 1), (near, 0), (near, 1)]
+    later = [(a ^ b, c) for a, _ in first for b, c in rest]
+    return first, rest[:2] + later[0:2] + [rest[2]] + later[3:5] + [later[2]] + later[6:8] + [later[5], later[8]]
+
+
+def gather_kernel(
+    far, near, in_ref, out_ref, grad_ref, gate_ref, up_ref, down_ref,
+    in_full, out_full, grads, gate_all, up_all, down_all,
+    send_sems, recv_sems, local_sems,
+):
+    far_dev, near_dev, share_dev = peer(far), peer(near), peer(SHARE)
+    ctx_dev, core_dev = peer(0, 1), peer(0, 0, 1)
+    greet([far_dev, near_dev, share_dev, ctx_dev, core_dev])
+    net = Exchange(send_sems, recv_sems, local_sems)
+    fars = [("fsdp", far), ("fsdp", SHARE)]
+    low, across = ("fsdp", near), ("ctx", 1)
+    place = lax.axis_index("ctx")
+    rows = in_ref.shape[0]
+    parts = [((0, rows // 2), fars + [across, low]), ((rows // 2, rows // 2), fars + [low, across])]
+    ins = [RowGather(net, in_ref, in_full, part, order) for part, order in parts]
+    me = lax.axis_index("fsdp") * 2 + place
+    own_rows = pl.ds(pl.multiple_of(me * rows, 16), rows)
+    net.keep(in_ref, in_full.at[own_rows])
+    net.keep(out_ref, out_full.at[own_rows])
+
+    half = grad_ref.shape[0]
+    quarter = half // 2
+    own_half = [pl.ds(k * quarter, quarter) for k in range(2)]
+    far_rows = [pl.ds(2 * half + k * half, quarter) for k in range(2)]
+    cross_rows = [pl.ds(2 * half + k * half + quarter, quarter) for k in range(2)]
+    net.keep(grad_ref, grads.at[pl.ds(0, half)])
+
+    width, units = gate_ref.shape
+
+    def slot(full, piece, which=None):
+        if full is down_all:
+            start, size = piece * units, units
+        else:
+            start, size = 0, width
+        if which is not None:
+            size //= 2
+            start = pl.multiple_of(start + which * size, 16)
+        if full is down_all:
+            return full.at[pl.ds(start, size)]
+        return full.at[pl.ds(start, size), pl.ds(piece * units, units)]
+
+    matrices = [(gate_ref, gate_all), (up_ref, up_all), (down_ref, down_all)]
+    for ref, full in matrices:
+        net.keep(ref, slot(full, 0))
+        net.start(ref, slot(full, 1), core_dev)
+    first, rest = gather_codes(far, near)
+    for code in first:
+        for g in ins:
+            g.arrive(code)
+    outs = [RowGather(net, out_ref, out_full, part, order) for part, order in parts]
+    far_copies = [net.start(grad_ref.at[own_half[k]], grads.at[far_rows[k]], far_dev) for k in range(2)]
+    from_share = []
+    for ref, full in matrices:
+        size = ref.shape[0] // 2
+        part = ref.at[pl.ds(pl.multiple_of(place * size, 16), size)]
+        from_share.append(net.start(part, slot(full, 2, place), share_dev))
+    for code in rest:
+        for g in ins:
+            g.arrive(code)
+    for code in first + rest:
+        for g in outs:
+            g.arrive(code)
+    net.start(grad_ref, grads.at[pl.ds(half, half)], near_dev)
+    for k in range(2):
+        net.arrive(far_copies[k])
+        net.start(grads.at[far_rows[k]], grads.at[cross_rows[k]], near_dev)
+    from_ctx = []
+    for k, (ref, full) in enumerate(matrices):
+        net.arrive(from_share[k])
+        from_ctx.append(net.start(slot(full, 2, place), slot(full, 2, place), ctx_dev))
+        net.start(slot(full, 2, place), slot(full, 3, place), core_dev)
+    for k, (ref, full) in enumerate(matrices):
+        net.arrive(from_ctx[k])
+        net.start(slot(full, 2, 1 - place), slot(full, 3, 1 - place), core_dev)
+    net.finish()
+
+
+def gather_all(in_block, out_block, grad_half, gate, up, down):
+    far, near = token_bits()
+    owners = lax.axis_size("fsdp") * lax.axis_size("ctx")
+    width, units = gate.shape
+    any_spec = pl.BlockSpec(memory_space=pl.ANY)
+    shapes = [
+        (owners * in_block.shape[0], in_block.shape[1]),
+        (owners * out_block.shape[0], out_block.shape[1]),
+        (4 * grad_half.shape[0], width),
+        (width, 4 * units),
+        (width, 4 * units),
+        (4 * units, width),
+    ]
+    return pl.pallas_call(
+        functools.partial(gather_kernel, far, near),
+        name="gather",
+        out_shape=tuple(jax.ShapeDtypeStruct(s, bf16) for s in shapes),
+        in_specs=[any_spec] * 6,
+        out_specs=(any_spec,) * 6,
+        scratch_shapes=[
+            pltpu.SemaphoreType.DMA((80,)),
+            pltpu.SemaphoreType.DMA((80,)),
+            pltpu.SemaphoreType.DMA((6,)),
+        ],
+        compiler_params=pltpu.CompilerParams(collective_id=0, has_side_effects=True),
+    )(in_block, out_block, grad_half, gate, up, down)
+
+
+def rms_back_gain(inverse, scaled, row_gains, upstream):
+    return jnp.sum(upstream * scaled, axis=0), rms_back(inverse, scaled, row_gains, upstream)
 
 
 def to_expert(arrived, local_experts, capacity):
@@ -248,7 +879,7 @@
     return (gate_pre, up_pre, hidden)
 
 
-def on_device(
+def on_any_slice(
     tokens,
     lengths,
     routes,
@@ -313,7 +944,7 @@
         lax.all_gather(value_own, "ctx", axis=0, tiled=True),
     )
     grouped = queries.reshape(row_count, local_kv, group_size, HEAD_DIM)
-    mixed_full, totals_list = attention_forward(
+    mixed_full, log_total = attention_forward(
         grouped, pack_keys, pack_values, doc_ids, doc_first, base_row, block_rows
     )
     attended = mixed_full.astype(jnp.bfloat16)
@@ -425,7 +1056,7 @@
     moe_grad = moe_in_grad + jnp.einsum(
         "te,de->td", logit_grad, full_router.astype(jnp.float32), precision=highest
     )
-    gain_moe_grad, middle_norm_grad = rms_back(inverse_moe, scaled_moe, moe_gain, moe_grad)
+    gain_moe_grad, middle_norm_grad = rms_back_gain(inverse_moe, scaled_moe, moe_gain, moe_grad)
     middle_grad = upstream + middle_norm_grad
     out_in = middle_grad.astype(jnp.bfloat16)
     out_w_grad = jnp.einsum("tq,td->qd", attended, out_in, preferred_element_type=jnp.float32)
@@ -437,7 +1068,7 @@
         pack_keys,
         pack_values,
         mixed_grad,
-        totals_list,
+        log_total,
         doc_ids,
         doc_first,
         base_row,
@@ -480,7 +1111,7 @@
         "tq,dq->td", value_grad_low, full_value, preferred_element_type=jnp.float32
     )
     attn_in_grad = lax.psum(attn_in_part.astype(jnp.bfloat16), "tp").astype(jnp.float32)
-    gain_attn_grad, input_norm_grad = rms_back(inverse_attn, scaled_attn, attn_gain, attn_in_grad)
+    gain_attn_grad, input_norm_grad = rms_back_gain(inverse_attn, scaled_attn, attn_gain, attn_in_grad)
     tokens_grad = middle_grad + input_norm_grad
     shard_grads = (
         lax.psum_scatter(gain_attn_grad, ("fsdp", "ctx"), scatter_dimension=0, tiled=True),
@@ -508,38 +1139,249 @@
     )
 
 
+def on_device(
+    tokens,
+    lengths,
+    routes,
+    norm_attn,
+    w_query,
+    w_key,
+    w_value,
+    w_out,
+    norm_moe,
+    w_router,
+    w_gate,
+    w_up,
+    w_down,
+    out_grad,
+    loss_grad,
+):
+    row_count, width = tokens.shape
+    ctx_count = lax.axis_size("ctx")
+    fsdp_count = lax.axis_size("fsdp")
+    ctx_place = lax.axis_index("ctx")
+    tp_place = lax.axis_index("tp")
+    own_expert = lax.axis_index("fsdp")
+    top_count = routes.shape[1]
+    expert_count = w_router.shape[1]
+    pack_count = row_count * ctx_count
+    base_row = ctx_place * row_count
+    half_rows = row_count // 2
+    token_total = pack_count * fsdp_count
+    if fsdp_count != 8:
+        return on_any_slice(
+            tokens, lengths, routes, norm_attn, w_query, w_key, w_value, w_out, norm_moe, w_router,
+            w_gate, w_up, w_down, out_grad, loss_grad,
+        )
+    orders = weight_orders()
+
+    extras = widen([norm_attn[:, None], norm_moe[:, None], w_router])
+    extra_width = extras.shape[1]
+    in_block = jnp.concatenate([extras, w_query, w_key, w_value], axis=1)
+    upstream_low = own_part(out_grad, tp_place)
+    in_weights, out_weights, grad_blocks, gate_all, up_all, down_all = gather_all(
+        in_block, w_out.T, upstream_low, w_gate[0], w_up[0], w_down[0]
+    )
+    gains = in_weights[:, :2].astype(f32)
+    attn_gain, moe_gain = gains[:, 0], gains[:, 1]
+    full_router = in_weights[:, 2 : 2 + expert_count]
+    qkv_weights = in_weights[:, extra_width:]
+    query_width, kv_width = w_query.shape[1], w_key.shape[1]
+
+    own_routes = own_part(routes, tp_place)
+    expert_ids = jnp.arange(expert_count, dtype=jnp.int32)
+    route_mask = jnp.sum((own_routes[:, :, None] == expert_ids).astype(f32), axis=1)
+    fraction = sum_everywhere(jnp.sum(route_mask, axis=0)) / (token_total * top_count)
+
+    doc_ids, positions, doc_first = pack_layout(lengths[0], pack_count)
+    own_positions = lax.dynamic_slice_in_dim(positions, base_row, row_count, 0)
+    cos_table, sin_table = rope_tables(own_positions)
+    x_float = tokens.astype(f32)
+    _, _, normed_full = rms_parts(x_float, attn_gain)
+    normed_attn = normed_full.astype(bf16)
+    local_heads = query_width // HEAD_DIM
+    local_kv = kv_width // HEAD_DIM
+    qkv = dot(normed_attn, qkv_weights)
+    rotated = rotate(
+        qkv[:, : query_width + kv_width].reshape(row_count, local_heads + local_kv, HEAD_DIM),
+        cos_table,
+        sin_table,
+    ).astype(bf16)
+    queries = rotated[:, :local_heads]
+    key_own = rotated[:, local_heads:].reshape(row_count, kv_width)
+    value_own = qkv[:, query_width + kv_width :].astype(bf16)
+    kv_own = jnp.concatenate([key_own, value_own], axis=1)
+    kv_pack = side_by_side(kv_own, swap(kv_own, "ctx"), ctx_place)
+    pack_keys = kv_pack[:, :kv_width].reshape(pack_count, local_kv, HEAD_DIM)
+    pack_values = kv_pack[:, kv_width:].reshape(pack_count, local_kv, HEAD_DIM)
+    grouped = queries.reshape(row_count, local_kv, local_heads // local_kv, HEAD_DIM)
+    mixed_full, log_total = attention_forward(
+        grouped, pack_keys, pack_values, doc_ids, doc_first, base_row, row_count
+    )
+    attended = mixed_full.astype(bf16)
+    out_part = dot(attended, out_weights, 1, 1)
+    attn_out = own_part(out_part, tp_place) + swap(own_part(out_part, 1 - tp_place), "tp")
+
+    x_half = own_part(tokens, tp_place).astype(f32)
+    middle = x_half + attn_out
+    inverse_moe, scaled_moe, normed_mid = rms_parts(middle, moe_gain)
+    normed_moe = normed_mid.astype(bf16)
+    logits = dot(normed_moe, full_router)
+    shifted = jnp.exp(logits - jnp.max(logits, axis=-1, keepdims=True))
+    router_probs = shifted / jnp.sum(shifted, axis=-1, keepdims=True)
+    chosen = router_probs * route_mask
+    chosen_total = jnp.sum(chosen, axis=-1, keepdims=True)
+    gate_weights = chosen / chosen_total
+    probs_global = sum_everywhere(jnp.sum(router_probs, axis=0))
+    balance_loss = (expert_count * jnp.sum(fraction * (probs_global / token_total))).reshape(1)
+
+    payload = jnp.concatenate([normed_moe, widen(as_pair(gate_weights))], axis=1)
+    returned, moe_rows, keep_gu, got_gu, keep_d, got_d = experts_on_chip(
+        payload, grad_blocks, gate_all, up_all, down_all, expert_count
+    )
+    far, near = token_bits()
+    quarter = half_rows // 2
+    second = 3 * half_rows
+    moe_parts = {
+        0: moe_rows[:half_rows].astype(f32),
+        near: moe_rows[half_rows : 2 * half_rows].astype(f32),
+        far: jnp.concatenate([moe_rows[2 * half_rows :][:quarter], moe_rows[second:][:quarter]]).astype(f32),
+        far ^ near: jnp.concatenate([moe_rows[2 * half_rows + quarter : second], moe_rows[second + quarter :]]).astype(f32),
+    }
+    moe_out = reduce_tokens(moe_parts)
+    out_half = (middle + moe_out).astype(bf16)
+    output = side_by_side(out_half, swap(out_half, "tp"), tp_place)
+    units = keep_d.shape[0] // 2
+
+    def summed(keep, got, cols):
+        return keep[:, cols].astype(f32) + got[:, cols].astype(f32)
+
+    gate_w_out = across_share(across_ctx(summed(keep_gu, got_gu, slice(0, 2 * units))))
+    up_w_out = across_ctx(across_share(summed(keep_gu, got_gu, slice(2 * units, None))))
+    down_w_out = across_share(across_ctx(summed(keep_d, got_d, slice(None)), 1), 0)
+
+    moe_in_grad = returned[:, :width]
+    gate_grad = from_pair(returned[:, width:], expert_count)
+    weighted = jnp.sum(gate_grad * gate_weights, axis=-1, keepdims=True)
+    chosen_grad = route_mask * (gate_grad - weighted) / chosen_total
+    prob_grad = chosen_grad + loss_grad[0] * expert_count * fraction / token_total
+    logit_grad = router_probs * (
+        prob_grad - jnp.sum(prob_grad * router_probs, axis=-1, keepdims=True)
+    )
+    moe_grad = moe_in_grad + lax.dot_general(
+        logit_grad, full_router.astype(f32), (((1,), (1,)), ((), ())), precision=highest
+    )
+    router_grad = lax.dot_general(
+        normed_moe.astype(f32), logit_grad, (((0,), (0,)), ((), ())), precision=highest
+    )
+    gain_moe_grad = jnp.sum(moe_grad * scaled_moe, axis=0)
+    upstream = upstream_low.astype(f32)
+    middle_grad = upstream + rms_back(inverse_moe, scaled_moe, moe_gain, moe_grad)
+    out_in_half = middle_grad.astype(bf16)
+    out_in = side_by_side(out_in_half, swap(out_in_half, "tp"), tp_place)
+    mixed_grad = dot(out_in, out_weights).astype(bf16)
+    out_w_grad = dot(out_in, attended, 0, 0)
+    small_grads = widen([gain_moe_grad[:, None], router_grad])
+    out_reduced = reduce_weights(jnp.concatenate([small_grads, out_w_grad], axis=1), orders)
+    small_out = out_reduced[:, : 1 + expert_count]
+    small_out = small_out + swap(small_out, "tp")
+    w_out_grad = out_reduced[:, small_grads.shape[1] :].T
+
+    query_acc, key_grad_pack, value_grad_pack = attention_backward(
+        grouped,
+        pack_keys,
+        pack_values,
+        mixed_grad,
+        log_total,
+        doc_ids,
+        doc_first,
+        base_row,
+        row_count,
+    )
+    kv_grad_pack = jnp.concatenate(
+        [key_grad_pack.reshape(pack_count, kv_width), value_grad_pack.reshape(pack_count, kv_width)],
+        axis=1,
+    )
+    kv_grad = across_ctx(kv_grad_pack)
+    query_grad = (
+        rotate(query_acc.reshape(row_count, local_heads, HEAD_DIM), cos_table, -sin_table)
+        .astype(bf16)
+        .reshape(row_count, query_width)
+    )
+    key_grad = (
+        rotate(kv_grad[:, :kv_width].reshape(row_count, local_kv, HEAD_DIM), cos_table, -sin_table)
+        .astype(bf16)
+        .reshape(row_count, kv_width)
+    )
+    qkv_grad = jnp.concatenate([query_grad, key_grad, kv_grad[:, kv_width:].astype(bf16)], axis=1)
+    attn_in_part = dot(qkv_grad, qkv_weights, 1, 1)
+    attn_in_grad = own_part(attn_in_part, tp_place) + swap(
+        own_part(attn_in_part, 1 - tp_place).astype(bf16), "tp"
+    ).astype(f32)
+    inverse_attn, scaled_attn, _ = rms_parts(x_half, attn_gain)
+    gain_attn_grad = jnp.sum(attn_in_grad * scaled_attn, axis=0)
+    tokens_half = middle_grad + rms_back(inverse_attn, scaled_attn, attn_gain, attn_in_grad)
+    tokens_grad = side_by_side(tokens_half, swap(tokens_half, "tp"), tp_place)
+    qkv_w_grad = dot(normed_attn, qkv_grad, 0, 0)
+    gain_column = widen([gain_attn_grad[:, None]])
+    in_reduced = reduce_weights(jnp.concatenate([gain_column, qkv_w_grad], axis=1), orders)
+    gain_out = in_reduced[:, :1]
+    gain_out = (gain_out + swap(gain_out, "tp"))[:, 0]
+    start = gain_column.shape[1]
+    return (
+        output,
+        balance_loss,
+        tokens_grad,
+        gain_out,
+        in_reduced[:, start : start + query_width],
+        in_reduced[:, start + query_width : start + query_width + kv_width],
+        in_reduced[:, start + query_width + kv_width :],
+        w_out_grad,
+        small_out[:, 0],
+        small_out[:, 1:],
+        gate_w_out[None],
+        up_w_out[None],
+        down_w_out[None],
+    )
+
+
 def solution(mesh):
+    rows = P(("fsdp", "ctx"), None)
+    gain = P(("fsdp", "ctx"))
+    split = P(("fsdp", "ctx"), "tp")
+    out_split = P("tp", ("fsdp", "ctx"))
+    columns = P("fsdp", None, "tp")
     return jax.shard_map(
         on_device,
         mesh=mesh,
         in_specs=(
-            P(("fsdp", "ctx"), None),
+            rows,
             P("fsdp", None),
-            P(("fsdp", "ctx"), None),
-            P(("fsdp", "ctx")),
-            P(("fsdp", "ctx"), "tp"),
-            P(("fsdp", "ctx"), "tp"),
-            P(("fsdp", "ctx"), "tp"),
-            P("tp", ("fsdp", "ctx")),
-            P(("fsdp", "ctx")),
-            P(("fsdp", "ctx"), None),
-            P("fsdp", None, "tp"),
-            P("fsdp", None, "tp"),
+            rows,
+            gain,
+            split,
+            split,
+            split,
+            out_split,
+            gain,
+            rows,
+            columns,
+            columns,
             P("fsdp", "tp", None),
-            P(("fsdp", "ctx"), None),
+            rows,
             P(),
         ),
         out_specs=(
-            P(("fsdp", "ctx"), None),
+            rows,
             P(),
-            P(("fsdp", "ctx"), None),
-            P(("fsdp", "ctx")),
-            P(("fsdp", "ctx"), "tp"),
-            P(("fsdp", "ctx"), "tp"),
-            P(("fsdp", "ctx"), "tp"),
-            P("tp", ("fsdp", "ctx")),
-            P(("fsdp", "ctx")),
-            P(("fsdp", "ctx"), None),
+            rows,
+            gain,
+            split,
+            split,
+            split,
+            out_split,
+            gain,
+            rows,
             P("fsdp", "ctx", "tp"),
             P("fsdp", "ctx", "tp"),
             P("fsdp", "tp", "ctx"),

time: 2160 us -> 692 us (0.32)
  waiting for transfers between devices: 1300 us -> 130 us
  blocking collectives: 411 us -> 0 us
  Pallas kernels: 0 us -> 258 us
  matrix products: 167 us -> 56.9 us
  local copies, waits for them, and re-layouts: 144 us -> 85.5 us
  starting transfers between devices: 24.5 us -> 72.7 us
    reduce_scatter x9 -> x0, waiting for transfers between devices: 613 us -> none  [the longest x1 143 us: on_device(): lax.psum_scatter(query_w_grad, ('fsdp', 'ctx'), scatter_dimension=0, tile...]
    all_to_all x4 -> x0, waiting for transfers between devices: 539 us -> none  [the longest x1 196 us: on_device(): lax.all_to_all(from_expert(grad_rows, fsdp_count, capacity), 'fsdp', spli...]
    all_gather x5 -> x0, blocking collectives: 304 us -> none  [the longest x1 221 us: on_device(): lax.all_gather(w_router, ('fsdp', 'ctx'), axis=0, tiled=True)]
    pallas_call x0 -> x2, Pallas kernels: none -> 258 us  [the longest x1 147 us: gather_all(): pl.pallas_call(functools.partial(gather_kernel, far, near), name='gather'...]
    ppermute x0 -> x52, waiting for transfers between devices: none -> 130 us  [swap(): lax.ppermute(array, axis, [(i, i ^ bit) for i in range(lax.axis_size(axis...]
    dot_general x25 -> x11, matrix products: 132 us -> 28.7 us  [the longest x7 17.5 us: dot(): lax.dot_general(left, right, (((left_dim,), (right_dim,)), ((), ())), pre...]
    unnamed x16 -> x0, waiting for transfers between devices: 81.5 us -> none
    psum x3 -> x0, blocking collectives: 81.2 us -> none  [the longest x2 78.6 us: on_device(): lax.psum((jnp.sum(route_mask, axis=(0, 1)), jnp.sum(router_probs, axis=0)...]
  transfers between devices with their start and end apart: 19 -> 52, of which waited for: 14 -> 28; matrix products, arithmetic and copies ran while one was open for 12% -> 19% of each run, Pallas kernels for 0% -> 0%
where the time goes in v1:
time: 692 us; the launch traced here: 680 us
  Pallas kernels  258 us (37%)
  waiting for transfers between devices  130 us (19%)
  local copies, waits for them, and re-layouts  85.5 us (12%)
  starting transfers between devices  72.7 us (11%)
  other arithmetic  68.2 us (10%)
  matrix products  56.9 us (8%)
  between operations  7.94 us (1%)
    pallas_call x1, Pallas kernels, gather_all(): pl.pallas_call(functools.partial(gather_kernel, far, near), name='gather'...  147 us
    ppermute x52, waiting for transfers between devices, swap(): lax.ppermute(array, axis, [(i, i ^ bit) for i in range(lax.axis_size(axis...  130 us
    pallas_call x1, Pallas kernels, experts_on_chip(): pl.pallas_call(functools.partial(expert_kernel, far, near, experts), name...  111 us
    ppermute x52, starting transfers between devices, swap(): lax.ppermute(array, axis, [(i, i ^ bit) for i in range(lax.axis_size(axis...  72.7 us
    unnamed x228, local copies, waits for them, and re-layouts  20.9 us
    dot_general x7, matrix products, dot(): lax.dot_general(left, right, (((left_dim,), (right_dim,)), ((), ())), pre...  17.5 us
  transfers between devices with their start and end apart: 52, of which 28 were waited for; matrix products, arithmetic and copies ran while one was open for 19% of the time, Pallas kernels for 0%

profile of v1, /device:TPU:11, one launch (start us, length us, event | category | flops | bytes accessed | tf_op | source)
XLA Modules:
  0.0 680.1 jit_solution(8204713406945204959)
XLA Ops:
  7.3 147.1 %gather.1 = (bf16[1536,1152]{1,0:T(8,128)(2,1)}, bf16[1536,768]{1,0:T(8,128)(2,1)}, bf16[1024,1536]{1,0:T(8,128)(2,1)}, bf16[1536,1536]{1,0:T(8,128)(2,1)}, bf16...) custom-call(bf16[96,1152]{1,0:T(8,128)(2,1)} %concatenate.63.in_ref, bf16[96,768]{1,0:T(8,128)(2,1)} %bitcast.396, ...), custom_call_target="tpu_custom_call" | custom-call | tf_op jit(solution)/shard_map/gather/pallas_call | solution.py:838
  157.1 3.7 fusion.96
  162.3 2.8 copy.112
  173.6 2.6 subtract_convert_fusion
  186.3 5.9 while.50
  193.5 10.5 %while.51 = (s32[]{:T(128)}, f32[1,6,512,128]{3,2,1,0:T(8,128)}, s32[]{:T(128)}, s32[512]{0:T(512)S(1)}, s32[1024]{0:T(1024)S(1)}, /*index=5*/bf16[1024,1,128]{2...) while((s32[]{:T(128)}, f32[1,6,512,128]{3,2,1,0:T(8,128)}, ...), condition=%wide.region_9.10_spmd.clone, body=%wide.region_8.9_spmd.clone.sunk | while | flops 812778496 | bytes 4752575 | solution.py:127
  194.0 4.8 bitcast_add_fusion.9
  199.2 4.8 bitcast_add_fusion.9
  207.0 3.4 fusion.161
  218.1 2.4 collective-permute-done.7
  223.9 2.2 collective-permute-done.9
  229.1 3.0 multiply_reduce_fusion.2
  237.8 110.6 %experts.1 = (f32[256,1664]{1,0:T(8,128)}, bf16[1024,1536]{1,0:T(8,128)(2,1)}, bf16[1536,1536]{1,0:T(8,128)(2,1)}, bf16[1536,1536]{1,0:T(8,128)(2,1)}, bf16[768,...) custom-call(bf16[256,1664]{1,0:T(8,128)(2,1)} %concatenate.67.x_ref, bf16[1024,1536]{1,0:T(8,128)(2,1)} %get-tuple-element.265.g_hbm, ...), custom_call_target="tpu_custom_call" | custom-call | flops 43486543872 | bytes 60000000 | tf_op jit(solution)/shard_map/experts/pallas_call | solution.py:634
  348.4 2.7 fusion.157
  361.6 10.5 %collective-permute-start.48 = (bf16[1536,384]{1,0:T(8,128)(2,1)}, bf16[1536,384]{1,0:T(8,128)(2,1)}, u32[]{:S(2)}, u32[]{:S(2)}) collective-permute-start(bf16[1536,384]{1,0:T(8,128)(2,1)} %slice.312), channel_id=1, source_target_pairs={{0,8},{4,12},{8,0},{12,4},{16,24},{20,28},{24,16},{28,20},{1,9},{5... | collective-permute-start | bytes 3538952 | tf_op jit(solution)/shard_map/ppermute | solution.py:212
  373.3 2.3 multiply_reduce_fusion.4
  384.5 3.1 multiply_reduce_fusion
  396.4 11.4 %collective-permute-done.12 = f32[8]{0:T(128)S(1)} collective-permute-done((f32[8]{0:T(128)S(1)}, f32[8]{0:T(128)S(1)}, u32[]{:S(2)}, u32[]{:S(2)}) %collective-permute-start.12) | collective-permute-done | bytes 64 | tf_op jit(solution)/shard_map/ppermute | solution.py:212
  407.9 12.8 %collective-permute-start.13 = (f32[8]{0:T(128)S(1)}, f32[8]{0:T(128)S(1)}, u32[]{:S(2)}, u32[]{:S(2)}) collective-permute-start(f32[8]{0:T(128)S(1)} %add.510), channel_id=1, source_target_pairs={{0,16},{4,20},{8,24},{12,28},{16,0},{20,4},{24,8},{28,12},{1,17},{... | collective-permute-start | bytes 104 | tf_op jit(solution)/shard_map/ppermute | solution.py:212
  421.7 2.3 collective-permute-done.14
  430.8 2.3 convolution_convert_fusion
  440.5 7.3 %while.52 = (s32[]{:T(128)}, f32[1,6,512]{2,1,0:T(8,128)S(1)}, s32[]{:T(128)}, s32[512]{0:T(512)S(1)}, s32[1024]{0:T(1024)S(1)}, /*index=5*/bf16[1024,1,128]{2,0...) while((s32[]{:T(128)}, f32[1,6,512]{2,1,0:T(8,128)S(1)}, ...), condition=%wide.region_24.25_spmd.clone, body=%wide.region_22.24_spmd.clone.sunk | while | flops 813958144 | bytes 15024335 | solution.py:167
  449.7 17.3 %while.53 = (s32[]{:T(128)}, f32[512,1,6,128]{0,3,2,1:T(8,128)S(1)}, f32[1024,1,128]{2,0,1:T(8,128)S(1)}, f32[1024,1,128]{2,0,1:T(8,128)}, s32[]{:T(128)}, /*ind...) while((s32[]{:T(128)}, ...), condition=%wide.region_26.27_spmd.clone, body=%wide.region_25.26_spmd.clone.sunk | while | flops 2030765056 | bytes 41087272 | solution.py:202
  451.3 2.2 fusion.219
  455.3 3.1 fusion.221
  459.9 2.2 fusion.219
  463.9 3.1 fusion.221
  468.5 2.2 add_convert_fusion.2
  478.7 3.3 fusion.116
  489.4 2.2 convert_add_fusion.12
  494.5 2.4 collective-permute-start.4
  506.6 3.3 collective-permute-done.34
  511.2 27.2 %collective-permute-done.38 = bf16[1,1,2,2,96,256]{5,4,3,2,1,0:T(8,128)(2,1)S(1)} collective-permute-done((bf16[1,1,2,2,96,256]{5,4,3,2,1,0:T(8,128)(2,1)S(1)}, bf16[1,1,2,2,96,256]{5,4,3,2,1,0:T(8,128)(2,1)S(1)}, u32[]{:S(2)}, u32[]{:S(2)}) %collective-permute-start.38) | collective-permute-done | bytes 196640 | tf_op jit(solution)/shard_map/ppermute | solution.py:212
  538.5 3.1 collective-permute-start.35
  541.6 3.4 collective-permute-done.35
  545.9 2.5 collective-permute-done.39
  548.9 3.7 collective-permute-done.36
  555.5 4.4 collective-permute-start.45
  568.3 15.9 %collective-permute-done.42 = bf16[2,1,2,1,96,384]{5,4,3,2,1,0:T(8,128)(2,1)S(1)} collective-permute-done((bf16[2,1,2,1,96,384]{5,4,3,2,1,0:T(8,128)(2,1)S(1)}, bf16[2,1,2,1,96,384]{5,4,3,2,1,0:T(8,128)(2,1)S(1)}, u32[]{:S(2)}, u32[]{:S(2)}) %collective-permute-start.42) | collective-permute-done | bytes 294944 | tf_op jit(solution)/shard_map/ppermute | solution.py:212
  587.5 11.0 %collective-permute-done.47 = bf16[768,384]{1,0:T(8,128)(2,1)S(1)} collective-permute-done((bf16[768,384]{1,0:T(8,128)(2,1)S(1)}, bf16[768,384]{1,0:T(8,128)(2,1)S(1)}, u32[]{:S(2)}, u32[]{:S(2)}) %collective-permute-start.47) | collective-permute-done | bytes 589856 | tf_op jit(solution)/shard_map/ppermute | solution.py:212
  603.1 15.4 %collective-permute-done.43 = bf16[1,1,2,1,96,384]{5,4,3,2,1,0:T(8,128)(2,1)S(1)} collective-permute-done((bf16[1,1,2,1,96,384]{5,4,3,2,1,0:T(8,128)(2,1)S(1)}, bf16[1,1,2,1,96,384]{5,4,3,2,1,0:T(8,128)(2,1)S(1)}, u32[]{:S(2)}, u32[]{:S(2)}) %collective-permute-start.43) | collective-permute-done | bytes 147488 | tf_op jit(solution)/shard_map/ppermute | solution.py:212
  618.5 2.7 collective-permute-start.30
  624.2 8.6 %concatenate.78 = f32[1536,1152]{1,0:T(8,128)} concatenate(f32[1536,1]{1,0:T(8,128)S(1)} %broadcast_in_dim.155, f32[1536,127]{1,0:T(8,128)} %broadcast_in_dim.140, f32[1536,1024]{1,0:T(8,128)} %copy-done.5), dimensions={1} | concatenate | bytes 14155776 | tf_op jit(solution)/shard_map/concatenate | solution.py:1327
  636.1 3.3 fusion.104
  645.0 4.0 collective-permute-done.31
  655.2 5.8 collective-permute-done.21
  662.2 3.0 collective-permute-done.22
  669.9 4.9 collective-permute-start.24
  (543 shorter events, 193.5 us)
Async XLA Ops:
  177.9 7.2 %collective-permute-start = (bf16[512,256]{1,0:T(8,128)(2,1)}, bf16[512,256]{1,0:T(8,128)(2,1)}, u32[]{:S(2)}, u32[]{:S(2)}) collective-permute-start(bf16[512,256]{1,0:T(8,128)(2,1)} %pad_maximum_fusion.16), channel_id=1, source_target_pairs={{0,2},{2,0},{1,3},{3,1},{4,6},{6,4},{5,7},{7,5},{8,10},{10,8},{9,1... | collective-permute-start | bytes 786440 | tf_op jit(solution)/shard_map/ppermute | solution.py:212
  213.3 15.7 %collective-permute-start.1 = (f32[256,1536]{1,0:T(8,128)}, f32[256,1536]{1,0:T(8,128)}, u32[]{:S(2)}, u32[]{:S(2)}) collective-permute-start(f32[256,1536]{1,0:T(8,128)} %constant_dynamic-slice_fusion.3), channel_id=1, source_target_pairs={{0,1},{1,0},{2,3},{3,2},{4,5},{5,4},{6,7},{7,6},{8,9},{9,8},{10,11... | collective-permute-start | bytes 4718600 | tf_op jit(solution)/shard_map/ppermute | solution.py:212
  215.3 2.7 collective-permute-start.6
  218.1 2.4 collective-permute-start.7
  220.4 3.3 collective-permute-start.8
  355.1 139.4 %collective-permute-start.50 = (bf16[768,768]{1,0:T(8,128)(2,1)}, bf16[768,768]{1,0:T(8,128)(2,1)}, u32[]{:S(2)}, u32[]{:S(2)}) collective-permute-start(bf16[768,768]{1,0:T(8,128)(2,1)} %dynamic-slice_convert_fusion), channel_id=1, source_target_pairs={{0,2},{2,0},{1,3},{3,1},{4,6},{6,4},{5,7},{7,5},{8,10},{10,8},{9,1... | collective-permute-start | bytes 3538952 | tf_op jit(solution)/shard_map/ppermute | solution.py:212
  361.6 136.9 %collective-permute-start.48 = (bf16[1536,384]{1,0:T(8,128)(2,1)}, bf16[1536,384]{1,0:T(8,128)(2,1)}, u32[]{:S(2)}, u32[]{:S(2)}) collective-permute-start(bf16[1536,384]{1,0:T(8,128)(2,1)} %slice.312), channel_id=1, source_target_pairs={{0,8},{4,12},{8,0},{12,4},{16,24},{20,28},{24,16},{28,20},{1,9},{5... | collective-permute-start | bytes 3538952 | tf_op jit(solution)/shard_map/ppermute | solution.py:212
  373.3 128.2 %collective-permute-start.46 = (bf16[768,768]{1,0:T(8,128)(2,1)}, bf16[768,768]{1,0:T(8,128)(2,1)}, u32[]{:S(2)}, u32[]{:S(2)}) collective-permute-start(bf16[768,768]{1,0:T(8,128)(2,1)} %dynamic-slice_convert_fusion.1), channel_id=1, source_target_pairs={{0,2},{2,0},{1,3},{3,1},{4,6},{6,4},{5,7},{7,5},{8,10},{10,8},{9,1... | collective-permute-start | bytes 3538952 | tf_op jit(solution)/shard_map/ppermute | solution.py:212
  389.1 38.8 %collective-permute-start.16 = (bf16[256,1536]{1,0:T(8,128)(2,1)}, bf16[256,1536]{1,0:T(8,128)(2,1)S(1)}, u32[]{:S(2)}, u32[]{:S(2)}) collective-permute-start(bf16[256,1536]{1,0:T(8,128)(2,1)} %fusion.153), channel_id=1, source_target_pairs={{0,1},{1,0},{2,3},{3,2},{4,5},{5,4},{6,7},{7,6},{8,9},{9,8},{10,11... | collective-permute-start | bytes 2359304 | tf_op jit(solution)/shard_map/ppermute | solution.py:212
  391.0 3.6 collective-permute-start.11
  394.6 13.2 %collective-permute-start.12 = (f32[8]{0:T(128)S(1)}, f32[8]{0:T(128)S(1)}, u32[]{:S(2)}, u32[]{:S(2)}) collective-permute-start(f32[8]{0:T(128)S(1)} %add.509), channel_id=1, source_target_pairs={{0,2},{2,0},{1,3},{3,1},{4,6},{6,4},{5,7},{7,5},{8,10},{10,8},{9,1... | collective-permute-start | bytes 104 | tf_op jit(solution)/shard_map/ppermute | solution.py:212
  407.9 13.7 %collective-permute-start.13 = (f32[8]{0:T(128)S(1)}, f32[8]{0:T(128)S(1)}, u32[]{:S(2)}, u32[]{:S(2)}) collective-permute-start(f32[8]{0:T(128)S(1)} %add.510), channel_id=1, source_target_pairs={{0,16},{4,20},{8,24},{12,28},{16,0},{20,4},{24,8},{28,12},{1,17},{... | collective-permute-start | bytes 104 | tf_op jit(solution)/shard_map/ppermute | solution.py:212
  426.3 42.0 %collective-permute-start.3 = (bf16[256,1536]{1,0:T(8,128)(2,1)}, bf16[256,1536]{1,0:T(8,128)(2,1)}, u32[]{:S(2)}, u32[]{:S(2)}) collective-permute-start(bf16[256,1536]{1,0:T(8,128)(2,1)} %pad_maximum_fusion.9), channel_id=1, source_target_pairs={{0,4},{4,0},{8,12},{12,8},{16,20},{20,16},{24,28},{28,24},{1,5},{5... | collective-permute-start | bytes 2359304 | tf_op jit(solution)/shard_map/ppermute | solution.py:212
  437.4 54.2 %collective-permute-start.33 = (bf16[2,2,1,2,96,256]{4,5,3,2,1,0:T(8,128)(2,1)}, bf16[2,2,1,2,96,256]{4,5,3,2,1,0:T(8,128)(2,1)}, u32[]{:S(2)}, u32[]{:S(2)}) collective-permute-start(bf16[2,2,1,2,96,256]{4,5,3,2,1,0:T(8,128)(2,1)} %copy.145), channel_id=1, source_target_pairs={{0,4},{4,0},{8,12},{12,8},{16,20},{20,16},{24,28},{28,24},{1,5},{5... | collective-permute-start | bytes 1179656 | tf_op jit(solution)/shard_map/ppermute | solution.py:212
  468.4 7.3 %collective-permute-start.17 = (bf16[512,256]{1,0:T(8,128)(2,1)S(1)}, bf16[512,256]{1,0:T(8,128)(2,1)S(1)}, u32[]{:S(2)}, u32[]{:S(2)}) collective-permute-start(bf16[512,256]{1,0:T(8,128)(2,1)S(1)} %fusion.113), channel_id=1, source_target_pairs={{0,2},{2,0},{1,3},{3,1},{4,6},{6,4},{5,7},{7,5},{8,10},{10,8},{9,1... | collective-permute-start | bytes 786440 | tf_op jit(solution)/shard_map/ppermute | solution.py:212
  475.7 13.5 %collective-permute-start.37 = (bf16[2,1,2,2,96,256]{5,4,3,2,1,0:T(8,128)(2,1)S(1)}, bf16[2,1,2,2,96,256]{5,4,3,2,1,0:T(8,128)(2,1)}, u32[]{:S(2)}, u32[]{:S(2)}) collective-permute-start(bf16[2,1,2,2,96,256]{5,4,3,2,1,0:T(8,128)(2,1)S(1)} %dynamic-slice_convert_fusion.8), channel_id=1, source_target_pairs={{0,8},{4,12},{8,0},{12,4},{16,24},{20,28},{24,16},{28,20},{1,9},{5... | collective-permute-start | bytes 1179656 | tf_op jit(solution)/shard_map/ppermute | solution.py:212
  489.2 145.8 %collective-permute-start.2 = (bf16[256,1536]{1,0:T(8,128)(2,1)}, bf16[256,1536]{1,0:T(8,128)(2,1)}, u32[]{:S(2)}, u32[]{:S(2)}) collective-permute-start(bf16[256,1536]{1,0:T(8,128)(2,1)} %slice.182), channel_id=1, source_target_pairs={{0,4},{4,0},{8,12},{12,8},{16,20},{20,16},{24,28},{28,24},{1,5},{5... | collective-permute-start | bytes 2359304 | tf_op jit(solution)/shard_map/ppermute | solution.py:212
  491.6 19.3 %collective-permute-start.41 = (bf16[2,2,2,1,96,384]{5,4,3,2,1,0:T(8,128)(2,1)S(1)}, bf16[2,2,2,1,96,384]{5,4,3,2,1,0:T(8,128)(2,1)S(1)}, u32[]{:S(2)}, u32[]{:S(2)}) collective-permute-start(bf16[2,2,2,1,96,384]{5,4,3,2,1,0:T(8,128)(2,1)S(1)} %copy-done.64), channel_id=1, source_target_pairs={{0,2},{2,0},{1,3},{3,1},{4,6},{6,4},{5,7},{7,5},{8,10},{10,8},{9,1... | collective-permute-start | bytes 1769480 | tf_op jit(solution)/shard_map/ppermute | solution.py:212
  494.5 141.2 %collective-permute-start.4 = (bf16[256,1536]{1,0:T(8,128)(2,1)}, bf16[256,1536]{1,0:T(8,128)(2,1)}, u32[]{:S(2)}, u32[]{:S(2)}) collective-permute-start(bf16[256,1536]{1,0:T(8,128)(2,1)} %add_convert_fusion.2), channel_id=1, source_target_pairs={{0,16},{4,20},{8,24},{12,28},{16,0},{20,4},{24,8},{28,12},{1,17},{... | collective-permute-start | bytes 2359304 | tf_op jit(solution)/shard_map/ppermute | solution.py:212
  498.5 63.8 %collective-permute-start.25 = (bf16[2,1,2,2,96,384]{5,4,3,2,1,0:T(8,128)(2,1)}, bf16[2,1,2,2,96,384]{5,4,3,2,1,0:T(8,128)(2,1)}, u32[]{:S(2)}, u32[]{:S(2)}) collective-permute-start(bf16[2,1,2,2,96,384]{5,4,3,2,1,0:T(8,128)(2,1)} %dynamic-slice_convert_fusion.6), channel_id=1, source_target_pairs={{0,8},{4,12},{8,0},{12,4},{16,24},{20,28},{24,16},{28,20},{1,9},{5... | collective-permute-start | bytes 1769480 | tf_op jit(solution)/shard_map/ppermute | solution.py:212
  501.4 8.5 %collective-permute-start.34 = (bf16[2,2,1,1,96,256]{4,5,3,2,1,0:T(8,128)(2,1)S(1)}, bf16[2,2,1,1,96,256]{4,5,3,2,1,0:T(8,128)(2,1)S(1)}, u32[]{:S(2)}, u32[]{:S(2)}) collective-permute-start(bf16[2,2,1,1,96,256]{4,5,3,2,1,0:T(8,128)(2,1)S(1)} %dynamic-slice_convert_fusion.13), channel_id=1, source_target_pairs={{0,2},{2,0},{1,3},{3,1},{4,6},{6,4},{5,7},{7,5},{8,10},{10,8},{9,1... | collective-permute-start | bytes 589832 | tf_op jit(solution)/shard_map/ppermute | solution.py:212
  509.9 55.7 %collective-permute-start.29 = (bf16[2,2,2,1,96,384]{5,4,3,2,1,0:T(8,128)(2,1)}, bf16[2,2,2,1,96,384]{5,4,3,2,1,0:T(8,128)(2,1)}, u32[]{:S(2)}, u32[]{:S(2)}) collective-permute-start(bf16[2,2,2,1,96,384]{5,4,3,2,1,0:T(8,128)(2,1)} %dynamic-slice_convert_fusion.5), channel_id=1, source_target_pairs={{0,2},{2,0},{1,3},{3,1},{4,6},{6,4},{5,7},{7,5},{8,10},{10,8},{9,1... | collective-permute-start | bytes 1769480 | tf_op jit(solution)/shard_map/ppermute | solution.py:212
  510.9 27.5 %collective-permute-start.38 = (bf16[1,1,2,2,96,256]{5,4,3,2,1,0:T(8,128)(2,1)S(1)}, bf16[1,1,2,2,96,256]{5,4,3,2,1,0:T(8,128)(2,1)S(1)}, u32[]{:S(2)}, u32[]{:S(2)}) collective-permute-start(bf16[1,1,2,2,96,256]{5,4,3,2,1,0:T(8,128)(2,1)S(1)} %dynamic-slice_convert_fusion.14), channel_id=1, source_target_pairs={{0,16},{4,20},{8,24},{12,28},{16,0},{20,4},{24,8},{28,12},{1,17},{... | collective-permute-start | bytes 589832 | tf_op jit(solution)/shard_map/ppermute | solution.py:212
  538.5 6.5 collective-permute-start.35
  545.0 3.5 collective-permute-start.39
  548.5 4.1 collective-permute-start.36
  552.6 2.9 collective-permute-start.40
  555.5 5.2 collective-permute-start.45
  560.8 60.5 %collective-permute-start.18 = (bf16[256,1536]{1,0:T(8,128)(2,1)}, bf16[256,1536]{1,0:T(8,128)(2,1)S(1)}, u32[]{:S(2)}, u32[]{:S(2)}) collective-permute-start(bf16[256,1536]{1,0:T(8,128)(2,1)} %dynamic-slice_convert_fusion.2), channel_id=1, source_target_pairs={{0,1},{1,0},{2,3},{3,2},{4,5},{5,4},{6,7},{7,6},{8,9},{9,8},{10,11... | collective-permute-start | bytes 2359304 | tf_op jit(solution)/shard_map/ppermute | solution.py:212
  562.2 23.3 %collective-permute-start.51 = (bf16[384,768]{1,0:T(8,128)(2,1)}, bf16[384,768]{1,0:T(8,128)(2,1)S(1)}, u32[]{:S(2)}, u32[]{:S(2)}) collective-permute-start(bf16[384,768]{1,0:T(8,128)(2,1)} %slice.313), channel_id=1, source_target_pairs={{0,8},{4,12},{8,0},{12,4},{16,24},{20,28},{24,16},{28,20},{1,9},{5... | collective-permute-start | bytes 1769480 | tf_op jit(solution)/shard_map/ppermute | solution.py:212
  565.7 18.5 %collective-permute-start.42 = (bf16[2,1,2,1,96,384]{5,4,3,2,1,0:T(8,128)(2,1)S(1)}, bf16[2,1,2,1,96,384]{5,4,3,2,1,0:T(8,128)(2,1)S(1)}, u32[]{:S(2)}, u32[]{:S(2)}) collective-permute-start(bf16[2,1,2,1,96,384]{5,4,3,2,1,0:T(8,128)(2,1)S(1)} %dynamic-slice_convert_fusion.9), channel_id=1, source_target_pairs={{0,8},{4,12},{8,0},{12,4},{16,24},{20,28},{24,16},{28,20},{1,9},{5... | collective-permute-start | bytes 884744 | tf_op jit(solution)/shard_map/ppermute | solution.py:212
  584.2 14.2 %collective-permute-start.47 = (bf16[768,384]{1,0:T(8,128)(2,1)S(1)}, bf16[768,384]{1,0:T(8,128)(2,1)S(1)}, u32[]{:S(2)}, u32[]{:S(2)}) collective-permute-start(bf16[768,384]{1,0:T(8,128)(2,1)S(1)} %copy-done.63), channel_id=1, source_target_pairs={{0,8},{4,12},{8,0},{12,4},{16,24},{20,28},{24,16},{28,20},{1,9},{5... | collective-permute-start | bytes 1769480 | tf_op jit(solution)/shard_map/ppermute | solution.py:212
  585.5 15.3 %collective-permute-start.49 = (bf16[768,384]{1,0:T(8,128)(2,1)S(1)}, bf16[768,384]{1,0:T(8,128)(2,1)S(1)}, u32[]{:S(2)}, u32[]{:S(2)}) collective-permute-start(bf16[768,384]{1,0:T(8,128)(2,1)S(1)} %copy-done.62), channel_id=1, source_target_pairs={{0,2},{2,0},{1,3},{3,1},{4,6},{6,4},{5,7},{7,5},{8,10},{10,8},{9,1... | collective-permute-start | bytes 1769480 | tf_op jit(solution)/shard_map/ppermute | solution.py:212
  598.5 44.6 %collective-permute-start.26 = (bf16[1,1,2,2,96,384]{5,4,3,2,1,0:T(8,128)(2,1)S(1)}, bf16[1,1,2,2,96,384]{5,4,3,2,1,0:T(8,128)(2,1)}, u32[]{:S(2)}, u32[]{:S(2)}) collective-permute-start(bf16[1,1,2,2,96,384]{5,4,3,2,1,0:T(8,128)(2,1)S(1)} %dynamic-slice_convert_fusion.11), channel_id=1, source_target_pairs={{0,16},{4,20},{8,24},{12,28},{16,0},{20,4},{24,8},{28,12},{1,17},{... | collective-permute-start | bytes 884744 | tf_op jit(solution)/shard_map/ppermute | solution.py:212
  600.8 17.7 %collective-permute-start.43 = (bf16[1,1,2,1,96,384]{5,4,3,2,1,0:T(8,128)(2,1)S(1)}, bf16[1,1,2,1,96,384]{5,4,3,2,1,0:T(8,128)(2,1)S(1)}, u32[]{:S(2)}, u32[]{:S(2)}) collective-permute-start(bf16[1,1,2,1,96,384]{5,4,3,2,1,0:T(8,128)(2,1)S(1)} %dynamic-slice_convert_fusion.15), channel_id=1, source_target_pairs={{0,16},{4,20},{8,24},{12,28},{16,0},{20,4},{24,8},{28,12},{1,17},{... | collective-permute-start | bytes 442376 | tf_op jit(solution)/shard_map/ppermute | solution.py:212
  618.5 23.4 %collective-permute-start.30 = (bf16[2,1,2,1,96,384]{5,4,3,2,1,0:T(8,128)(2,1)}, bf16[2,1,2,1,96,384]{5,4,3,2,1,0:T(8,128)(2,1)}, u32[]{:S(2)}, u32[]{:S(2)}) collective-permute-start(bf16[2,1,2,1,96,384]{5,4,3,2,1,0:T(8,128)(2,1)} %dynamic-slice_convert_fusion.10), channel_id=1, source_target_pairs={{0,8},{4,12},{8,0},{12,4},{16,24},{20,28},{24,16},{28,20},{1,9},{5... | collective-permute-start | bytes 884744 | tf_op jit(solution)/shard_map/ppermute | solution.py:212
  621.3 19.7 %collective-permute-start.44 = (bf16[1,1,1,1,96,384]{5,4,3,2,1,0:T(8,128)(2,1)S(1)}, bf16[1,1,1,1,96,384]{5,4,3,2,1,0:T(8,128)(2,1)S(1)}, u32[]{:S(2)}, u32[]{:S(2)}) collective-permute-start(bf16[1,1,1,1,96,384]{5,4,3,2,1,0:T(8,128)(2,1)S(1)} %dynamic-slice_convert_fusion.21), channel_id=1, source_target_pairs={{0,4},{4,0},{8,12},{12,8},{16,20},{20,16},{24,28},{28,24},{1,5},{5... | collective-permute-start | bytes 221192 | tf_op jit(solution)/shard_map/ppermute | solution.py:212
  635.0 18.4 %collective-permute-start.20 = (bf16[2,2,1,2,96,384]{5,4,3,2,1,0:T(8,128)(2,1)S(1)}, bf16[2,2,1,2,96,384]{5,4,3,2,1,0:T(8,128)(2,1)S(1)}, u32[]{:S(2)}, u32[]{:S(2)}) collective-permute-start(bf16[2,2,1,2,96,384]{5,4,3,2,1,0:T(8,128)(2,1)S(1)} %dynamic-slice_convert_fusion.7), channel_id=1, source_target_pairs={{0,4},{4,0},{8,12},{12,8},{16,20},{20,16},{24,28},{28,24},{1,5},{5... | collective-permute-start | bytes 1769480 | tf_op jit(solution)/shard_map/ppermute | solution.py:212
  639.4 36.9 %collective-permute-start.19 = (f32[256,1536]{1,0:T(8,128)S(1)}, f32[256,1536]{1,0:T(8,128)S(1)}, u32[]{:S(2)}, u32[]{:S(2)}) collective-permute-start(f32[256,1536]{1,0:T(8,128)S(1)} %get-tuple-element.615), channel_id=1, source_target_pairs={{0,1},{1,0},{2,3},{3,2},{4,5},{5,4},{6,7},{7,6},{8,9},{9,8},{10,11... | collective-permute-start | bytes 4718600 | tf_op jit(solution)/shard_map/ppermute | solution.py:212
  641.0 21.0 %collective-permute-start.5 = (bf16[256,1536]{1,0:T(8,128)(2,1)S(1)}, bf16[256,1536]{1,0:T(8,128)(2,1)S(1)}, u32[]{:S(2)}, u32[]{:S(2)}) collective-permute-start(bf16[256,1536]{1,0:T(8,128)(2,1)S(1)} %get-tuple-element.616), channel_id=1, source_target_pairs={{0,1},{1,0},{2,3},{3,2},{4,5},{5,4},{6,7},{7,6},{8,9},{9,8},{10,11... | collective-permute-start | bytes 2359304 | tf_op jit(solution)/shard_map/ppermute | solution.py:212
  642.9 6.0 collective-permute-start.31
  644.1 7.4 %collective-permute-start.27 = (bf16[1,1,1,2,96,384]{5,4,3,2,1,0:T(8,128)(2,1)S(1)}, bf16[1,1,1,2,96,384]{5,4,3,2,1,0:T(8,128)(2,1)S(1)}, u32[]{:S(2)}, u32[]{:S(2)}) collective-permute-start(bf16[1,1,1,2,96,384]{5,4,3,2,1,0:T(8,128)(2,1)S(1)} %dynamic-slice_convert_fusion.17), channel_id=1, source_target_pairs={{0,4},{4,0},{8,12},{12,8},{16,20},{20,16},{24,28},{28,24},{1,5},{5... | collective-permute-start | bytes 442376 | tf_op jit(solution)/shard_map/ppermute | solution.py:212
  649.0 4.4 collective-permute-start.32
  651.6 3.6 collective-permute-start.28
  653.6 7.4 %collective-permute-start.21 = (bf16[2,2,1,1,96,384]{5,4,3,2,1,0:T(8,128)(2,1)S(1)}, bf16[2,2,1,1,96,384]{5,4,3,2,1,0:T(8,128)(2,1)S(1)}, u32[]{:S(2)}, u32[]{:S(2)}) collective-permute-start(bf16[2,2,1,1,96,384]{5,4,3,2,1,0:T(8,128)(2,1)S(1)} %dynamic-slice_convert_fusion.12), channel_id=1, source_target_pairs={{0,2},{2,0},{1,3},{3,1},{4,6},{6,4},{5,7},{7,5},{8,10},{10,8},{9,1... | collective-permute-start | bytes 884744 | tf_op jit(solution)/shard_map/ppermute | solution.py:212
  661.1 4.1 collective-permute-start.22
  665.2 4.7 collective-permute-start.23
  669.9 5.8 collective-permute-start.24
  (119 other events, 1002.2 us)

commit v2 on v1

--- a/solution.py
+++ b/solution.py
@@ -1,4 +1,5 @@
 import functools
+import math
 
 import jax
 import jax.experimental.pallas as pl
@@ -384,6 +385,10 @@
     near,
     experts,
     x_ref,
+    grad_hbm,
+    gate_hbm,
+    up_hbm,
+    down_hbm,
     g_hbm,
     wg_hbm,
     wu_hbm,
@@ -408,7 +413,6 @@
     near_in,
     near_sum,
     far_in,
-    far_out,
     keep_stage,
     send_stage,
     local_sems,
@@ -433,21 +437,35 @@
     own_half = [pl.ds(k * quarter, quarter) for k in range(2)]
     far_copy = [send(x_ref.at[own_half[k]], xb.at[far_rows[k]], sems, k, far_dev) for k in range(2)]
     near_copy = send(x_ref, xb.at[near_rows], sems, 2, near_dev)
+    own_units = gate_hbm.shape[1]
+    core_rows = pl.ds(pl.multiple_of(lax.axis_index("tp") * half, 16), half)
+    got_rows, got_units = pl.ds(half, 3 * half), pl.ds(own_units, 3 * own_units)
+    first_units = pl.ds(0, own_units)
+    pairs = [
+        (grad_hbm.at[core_rows], gb.at[pl.ds(0, half)]),
+        (g_hbm.at[got_rows], gb.at[got_rows]),
+        (down_hbm, wd.at[first_units]),
+        (wd_hbm.at[got_units], wd.at[got_units]),
+        (gate_hbm, wg.at[:, first_units]),
+        (wg_hbm.at[:, got_units], wg.at[:, got_units]),
+        (up_hbm, wu.at[:, first_units]),
+        (wu_hbm.at[:, got_units], wu.at[:, got_units]),
+    ]
     loads = []
-    for k, (src, dst) in enumerate([(g_hbm, gb), (wd_hbm, wd), (wg_hbm, wg), (wu_hbm, wu)]):
+    for k, (src, dst) in enumerate(pairs):
         loads.append(pltpu.make_async_copy(src, dst, local_sems.at[k]))
         loads[-1].start()
     xb[0:half, :] = x_ref[...]
-    loads[0].wait()
-    loads[1].wait()
+    for k in range(4):
+        loads[k].wait()
 
     def back_tile(j, carry):
         h0[:, aligned(j, TILE)] = dot_nt(gb[...], wd[aligned(j, TILE), :])
         return carry
 
     lax.fori_loop(0, unit_tiles, back_tile, 0)
-    loads[2].wait()
-    loads[3].wait()
+    for k in range(4, 8):
+        loads[k].wait()
 
     lane = lax.broadcasted_iota(jnp.int32, (half, x_ref.shape[1] - width), 1)
     own = lax.axis_index("fsdp")
@@ -485,7 +503,7 @@
             )
 
         zero = jnp.zeros((half, 1), f32)
-        dots = lax.fori_loop(0, unit_tiles, unit_tile, (zero, zero))
+        dots = lax.fori_loop(0, unit_tiles, unit_tile, (zero, zero), unroll=True)
 
         def put(cols, value):
             if number == 0:
@@ -499,7 +517,7 @@
             put(cols, value)
             return carry
 
-        lax.fori_loop(0, width // (2 * TILE), in_tile, 0)
+        lax.fori_loop(0, width // (2 * TILE), in_tile, 0, unroll=True)
         columns = jnp.zeros_like(extra)
         for expert, value in ((own, dots[0]), (partner, dots[1])):
             high = value.astype(bf16).astype(f32)
@@ -516,8 +534,8 @@
     def far_back(k):
         crossed[k].wait_recv()
         total = db[far_rows[k], :].astype(f32) + near_in[own_half[k], :].astype(f32)
-        far_out[own_half[k], :] = total.astype(bf16)
-        return send(far_out.at[own_half[k]], far_in.at[own_half[k]], sems, 7 + k, far_dev)
+        db[far_rows[k], :] = total.astype(bf16)
+        return send(db.at[far_rows[k]], far_in.at[own_half[k]], sems, 7 + k, far_dev)
 
     def part_tile(j, carry):
         cols = aligned(j, 2 * TILE)
@@ -624,7 +642,7 @@
         copy.wait_send()
 
 
-def experts_on_chip(payload, grad_rows, gate, up, down, experts):
+def experts_on_chip(payload, out_grad, own_gate, own_up, own_down, grad_rows, gate, up, down, experts):
     half, wide = payload.shape
     rows, width = grad_rows.shape
     units = gate.shape[1]
@@ -642,7 +660,7 @@
             jax.ShapeDtypeStruct((units // 2, width), bf16),
             jax.ShapeDtypeStruct((units // 2, width), bf16),
         ),
-        in_specs=[vmem, any_spec, any_spec, any_spec, any_spec],
+        in_specs=[vmem] + [any_spec] * 8,
         out_specs=(vmem, vmem, any_spec, any_spec, any_spec, any_spec),
         scratch_shapes=[
             pltpu.VMEM((rows, wide), bf16),
@@ -659,10 +677,9 @@
             pltpu.VMEM((half, wide), bf16),
             pltpu.VMEM((half, wide), bf16),
             pltpu.VMEM((half, wide), bf16),
-            pltpu.VMEM((half, wide), bf16),
             pltpu.VMEM((2, TILE, units), bf16),
             pltpu.VMEM((2, TILE, units), bf16),
-            pltpu.SemaphoreType.DMA((4,)),
+            pltpu.SemaphoreType.DMA((8,)),
             pltpu.SemaphoreType.DMA((2,)),
             pltpu.SemaphoreType.DMA((10,)),
             pltpu.SemaphoreType.DMA((10,)),
@@ -675,7 +692,7 @@
         cost_estimate=pl.CostEstimate(
             flops=2 * 9 * rows * width * units, bytes_accessed=60_000_000, transcendentals=rows * units
         ),
-    )(payload, grad_rows, gate, up, down)
+    )(payload, out_grad, own_gate, own_up, own_down, grad_rows, gate, up, down)
 
 
 class Exchange:
@@ -685,6 +702,8 @@
         self.all = []
         self.local = []
         self.arrived = set()
+        self.settled = set()
+        self.gone = set()
 
     def start(self, src, dst, who):
         self.all.append(send(src, dst, self.sems, len(self.all), who))
@@ -700,37 +719,47 @@
             self.arrived.add(number)
             self.all[number].wait_recv()
 
+    def settle(self, number):
+        if number not in self.settled:
+            self.settled.add(number)
+            self.local[number].wait()
+
+    def sent(self, number):
+        if number not in self.gone:
+            self.gone.add(number)
+            self.all[number].wait_send()
+
     def finish(self):
         for number in range(len(self.all)):
             self.arrive(number)
-        for copy in self.all:
-            copy.wait_send()
-        for copy in self.local:
-            copy.wait()
+        for number in range(len(self.all)):
+            self.sent(number)
+        for number in range(len(self.local)):
+            self.settle(number)
 
 
 class RowGather:
-    def __init__(self, net, block, full, part, order):
+    def __init__(self, net, full, part, order):
         self.net, self.full, self.order = net, full, order
-        self.rows, self.first, self.size = block.shape[0], part[0], part[1]
+        self.rows, self.first, self.size = part
         self.copies = {}
-        self.spread((0, 0), -1, block.at[pl.ds(self.first, self.size)])
+        self.spread((0, 0), -1)
 
     def place(self, code):
         index = (lax.axis_index("fsdp") ^ code[0]) * 2 + (lax.axis_index("ctx") ^ code[1])
         return pl.ds(pl.multiple_of(index * self.rows + self.first, 16), self.size)
 
-    def spread(self, code, last, src):
+    def spread(self, code, last):
+        block = self.full.at[self.place(code)]
         for position in range(last + 1, len(self.order)):
             axis, bit = self.order[position]
             other = (code[0] ^ bit, code[1]) if axis == "fsdp" else (code[0], code[1] ^ bit)
-            copy = self.net.start(src, self.full.at[self.place(code)], dim_peer((axis, bit)))
-            self.copies[other] = (copy, position)
+            self.copies[other] = (self.net.start(block, block, dim_peer((axis, bit))), position)
 
     def arrive(self, code):
         copy, position = self.copies[code]
         self.net.arrive(copy)
-        self.spread(code, position, self.full.at[self.place(code)])
+        self.spread(code, position)
 
 
 def dim_peer(dim):
@@ -745,109 +774,668 @@
     return first, rest[:2] + later[0:2] + [rest[2]] + later[3:5] + [later[2]] + later[6:8] + [later[5], later[8]]
 
 
-def gather_kernel(
-    far, near, in_ref, out_ref, grad_ref, gate_ref, up_ref, down_ref,
-    in_full, out_full, grads, gate_all, up_all, down_all,
+def document_start(lengths_ref, number):
+    start, first = 0, jnp.zeros_like(number)
+    for k in range(lengths_ref.shape[1]):
+        start = start + lengths_ref[0, k]
+        first = jnp.where(number >= start, start, first)
+    return first
+
+
+def forward_kernel(
+    far, near, experts, total_rows,
+    lengths_ref, loss_grad_ref, routes_ref, tokens_ref, small_hbm, query_hbm, key_hbm, value_hbm, out_hbm,
+    grad_hbm, gate_hbm, up_hbm, down_hbm,
+    payload_ref, middle_ref, probs_ref, mask_ref, row_ref, query, kv, lse_ref, attended, cos_ref, sin_ref,
+    in_out, out_out, grads, gate_all, up_all, down_all,
+    in_full, out_full, normed, raw, core_sent, core_got, count_sent, count_got,
+    send_sems, recv_sems, local_sems,
+):
+    far_dev, near_dev, share_dev = peer(far), peer(near), peer(SHARE)
+    ctx_dev, core_dev = peer(0, 1), peer(0, 0, 1)
+    net = Exchange(send_sems, recv_sems, local_sems)
+    place, core = lax.axis_index("ctx"), lax.axis_index("tp")
+    rows, width = tokens_ref.shape
+    half, quarter = rows // 2, rows // 4
+    block = small_hbm.shape[0]
+    heads_width, kv_width = query_hbm.shape[1], key_hbm.shape[1]
+    own_block = pl.ds(pl.multiple_of((lax.axis_index("fsdp") * 2 + place) * block, 16), block)
+    start = 0
+    for ref in (small_hbm, query_hbm, key_hbm, value_hbm):
+        net.keep(ref, in_full.at[own_block, pl.ds(start, ref.shape[1])])
+        start += ref.shape[1]
+    net.keep(out_hbm, out_full.at[own_block])
+    greet([far_dev, near_dev, share_dev, ctx_dev, core_dev])
+    for k in range(5):
+        net.settle(k)
+    fars = [("fsdp", far), ("fsdp", SHARE)]
+    low, across = ("fsdp", near), ("ctx", 1)
+    part = block // 2
+    ins = [
+        RowGather(net, in_full, (block, 0, part), fars + [across, low]),
+        RowGather(net, in_full, (block, part, part), fars + [low, across]),
+    ]
+
+    routes = routes_ref[...]
+    lane = lax.broadcasted_iota(jnp.int32, (rows, 128), 1)
+    named = jnp.zeros((rows, 128), f32)
+    for k in range(routes.shape[1]):
+        named += (routes[:, k : k + 1] == lane).astype(f32)
+    count_dims = [ctx_dev, near_dev, share_dev, far_dev]
+    counts = [jnp.broadcast_to(jnp.sum(named, axis=0, keepdims=True), (8, 128))]
+    count_copies = []
+
+    def count_step():
+        k = len(count_copies)
+        if k > 0:
+            net.arrive(count_copies[-1])
+            counts[0] = counts[0] + count_got[k - 1]
+        if k < len(count_dims):
+            count_sent[k] = counts[0]
+            count_copies.append(net.start(count_sent.at[k], count_got.at[k], count_dims[k]))
+
+    count_step()
+
+    units = gate_hbm.shape[1]
+
+    def slot(full, piece, which=None):
+        begin, size = (piece * units, units) if full is down_all else (0, width)
+        if which is not None:
+            size //= 2
+            begin = pl.multiple_of(begin + which * size, 16)
+        if full is down_all:
+            return full.at[pl.ds(begin, size)]
+        return full.at[pl.ds(begin, size), pl.ds(piece * units, units)]
+
+    matrices = [(down_hbm, down_all), (gate_hbm, gate_all), (up_hbm, up_all)]
+    for ref, full in matrices:
+        net.start(ref, slot(full, 1), core_dev)
+
+    here = lax.broadcasted_iota(jnp.int32, (rows, 1), 0) + place * rows
+    position = (here - document_start(lengths_ref, here)).astype(f32)
+    turn_lane = lax.broadcasted_iota(jnp.int32, (1, HEAD_DIM), 1)
+    turn = lax.rem(turn_lane, HEAD_DIM // 2).astype(f32) * (2.0 / HEAD_DIM)
+    angles = position * jnp.exp(turn * -math.log(rope_base))
+    cos_ref[...] = jnp.cos(angles)
+    sin_ref[...] = jnp.where(turn_lane < HEAD_DIM // 2, -1.0, 1.0) * jnp.sin(angles)
+
+    first, rest = gather_codes(far, near)
+    for code in first:
+        for g in ins:
+            g.arrive(code)
+    count_step()
+    own_rows = pl.ds(pl.multiple_of(core * half, 16), half)
+    other_rows = pl.ds(pl.multiple_of((1 - core) * half, 16), half)
+    own_quarter = [pl.ds(pl.multiple_of(core * half + k * quarter, 16), quarter) for k in range(2)]
+    far_rows = [pl.ds(2 * half + k * half, quarter) for k in range(2)]
+    cross_rows = [pl.ds(2 * half + k * half + quarter, quarter) for k in range(2)]
+    from_share = []
+    for ref, full in matrices:
+        size = ref.shape[0] // 2
+        piece = ref.at[pl.ds(pl.multiple_of(place * size, 16), size)]
+        from_share.append(net.start(piece, slot(full, 2, place), share_dev))
+    far_copies = [net.start(grad_hbm.at[own_quarter[k]], grads.at[far_rows[k]], far_dev) for k in range(2)]
+    for code in rest:
+        for g in ins:
+            g.arrive(code)
+    count_step()
+    outs = [
+        RowGather(net, out_full, (block, 0, part), [across] + fars + [low]),
+        RowGather(net, out_full, (block, part, part), fars + [low, across]),
+    ]
+    gains = in_full[:, :128].astype(f32).T
+    attn_gain, moe_gain = gains[experts : experts + 1], gains[experts + 1 : experts + 2]
+    step = quarter // 2
+    for k in range(rows // quarter):
+        at = slice(k * quarter, (k + 1) * quarter)
+        x = tokens_ref[at, :].astype(f32)
+        inverse = lax.rsqrt(jnp.mean(x * x, axis=1, keepdims=True) + epsilon)
+        normed[at, :] = (x * inverse * attn_gain).astype(bf16)
+
+    def rotated(value, at):
+        return value * cos_ref[at, :] + pltpu.roll(value, HEAD_DIM // 2, 1) * sin_ref[at, :]
+
+    mine = pl.ds(pl.multiple_of(place * rows, 16), rows)
+    raw[...] = dot_nn(normed[...], in_full[:, 128:])
+    kv[mine, :kv_width] = rotated(raw[:, heads_width : heads_width + kv_width], slice(None)).astype(bf16)
+    kv[mine, kv_width:] = raw[:, heads_width + kv_width :].astype(bf16)
+    kv_copy = net.start(kv.at[mine], kv.at[mine], ctx_dev)
+    for head in range(heads_width // HEAD_DIM):
+        cols = slice(head * HEAD_DIM, (head + 1) * HEAD_DIM)
+        query[:, cols] = rotated(raw[:, cols], slice(None)).astype(bf16)
+    for code in first:
+        for g in outs:
+            g.arrive(code)
+    near_copy = net.start(grad_hbm.at[own_rows], grads.at[pl.ds(half, half)], near_dev)
+    count_step()
+    net.arrive(kv_copy)
+
+    keys, values_flipped = kv[:, :HEAD_DIM], kv[:, HEAD_DIM:].T
+    query_number = lax.broadcasted_iota(jnp.int32, (1, half), 1) + place * rows
+    key_number = lax.broadcasted_iota(jnp.int32, (kv.shape[0], 1), 0)
+    scale = HEAD_DIM ** (-0.5)
+
+    def head_block(i, carry):
+        head, block_index = i // 2, lax.rem(i, 2)
+        cols, at = aligned(head, HEAD_DIM), aligned(block_index, half)
+        number = query_number + block_index * half
+        allowed = (key_number >= document_start(lengths_ref, number)) & (key_number <= number)
+        scores = jnp.where(allowed, dot_nt(keys, query[at, cols]) * scale, masked_score)
+        maxima = jnp.max(scores, axis=0, keepdims=True)
+        weights = jnp.exp(scores - maxima)
+        totals = jnp.sum(weights, axis=0, keepdims=True)
+        lse_ref[pl.ds(head, 1), at] = maxima + jnp.log(totals)
+        low_weights = (weights * (1.0 / totals)).astype(bf16)
+        attended[at, cols] = dot_nn(values_flipped, low_weights).T.astype(bf16)
+        return carry
+
+    group = heads_width // HEAD_DIM
+    third = 2 * group // 3
+    lax.fori_loop(0, third, head_block, 0)
+    for code in rest:
+        for g in outs:
+            g.arrive(code)
+    count_step()
+    lax.fori_loop(third, 2 * third, head_block, 0)
+    for k in range(2):
+        net.arrive(far_copies[k])
+        net.start(grads.at[far_rows[k]], grads.at[cross_rows[k]], near_dev)
+    lax.fori_loop(2 * third, 2 * group, head_block, 0)
+    from_ctx = []
+    for k, (ref, full) in enumerate(matrices):
+        net.arrive(from_share[k])
+        from_ctx.append(net.start(slot(full, 2, place), slot(full, 2, place), ctx_dev))
+        net.start(slot(full, 2, place), slot(full, 3, place), core_dev)
+
+    core_sent[...] = dot_nt(attended[other_rows, :], out_full[...])
+    core_copy = net.start(core_sent, core_got, core_dev)
+    middle_ref[...] = tokens_ref[own_rows, :].astype(f32) + dot_nt(attended[own_rows, :], out_full[...])
+    net.arrive(core_copy)
+    own_lane = lax.broadcasted_iota(jnp.int32, (step, 128), 1)
+    share_row = counts[0][0:1] * (experts / (total_rows * routes.shape[1] * total_rows))
+    row_number = lax.broadcasted_iota(jnp.int32, (8, 128), 0)
+    row_ref[...] = jnp.where(
+        row_number == 0, share_row * loss_grad_ref[0], jnp.where(row_number == 1, share_row, 0.0)
+    )
+    router = in_full[:, :128]
+    for k in range(half // step):
+        at = slice(k * step, (k + 1) * step)
+        middle = middle_ref[at, :] + core_got[at, :]
+        middle_ref[at, :] = middle
+        inverse = lax.rsqrt(jnp.mean(middle * middle, axis=1, keepdims=True) + epsilon)
+        normed_moe = (middle * inverse * moe_gain).astype(bf16)
+        payload_ref[at, :width] = normed_moe
+        logits = jnp.where(own_lane < experts, dot_nn(normed_moe, router), masked_score)
+        shifted = jnp.exp(logits - jnp.max(logits, axis=1, keepdims=True))
+        probs = shifted / jnp.sum(shifted, axis=1, keepdims=True)
+        own_routes = routes_ref[pl.ds(pl.multiple_of(core * half + k * step, 16), step), :]
+        mask = jnp.zeros((step, 128), f32)
+        for n in range(routes.shape[1]):
+            mask += (own_routes[:, n : n + 1] == own_lane).astype(f32)
+        probs_ref[at, :] = probs
+        mask_ref[at, :] = mask
+        chosen = probs * mask
+        gates = chosen / jnp.sum(chosen, axis=1, keepdims=True)
+        high = gates.astype(bf16).astype(f32)
+        payload_ref[at, width:] = (high + pltpu.roll(gates - high, experts, 1)).astype(bf16)
+    for k, (ref, full) in enumerate(matrices):
+        net.arrive(from_ctx[k])
+        net.start(slot(full, 2, 1 - place), slot(full, 3, 1 - place), core_dev)
+    net.keep(in_full, in_out)
+    net.keep(out_full, out_out)
+    net.finish()
+
+
+def forward_on_chip(
+    lengths, loss_grad, routes, tokens, small, w_query, w_key, w_value, out_block, out_grad, gate, up, down, experts
+):
+    far, near = token_bits()
+    owners = lax.axis_size("fsdp") * lax.axis_size("ctx")
+    rows, width = tokens.shape
+    half, pack = rows // 2, rows * lax.axis_size("ctx")
+    units, block = gate.shape[1], small.shape[0]
+    heads_width, kv_width = w_query.shape[1], w_key.shape[1]
+    in_width, out_width = small.shape[1] + heads_width + 2 * kv_width, out_block.shape[1]
+    any_spec = pl.BlockSpec(memory_space=pl.ANY)
+    vmem = pl.BlockSpec(memory_space=pltpu.VMEM)
+    smem = pl.BlockSpec(memory_space=pltpu.SMEM)
+    outs = [
+        ((half, width + 128), bf16),
+        ((half, width), f32),
+        ((half, 128), f32),
+        ((half, 128), f32),
+        ((8, 128), f32),
+        ((rows, heads_width), bf16),
+        ((pack, 2 * kv_width), bf16),
+        ((-(-heads_width // HEAD_DIM // 8) * 8, rows), f32),
+        ((rows, heads_width), bf16),
+        ((rows, HEAD_DIM), f32),
+        ((rows, HEAD_DIM), f32),
+        ((owners * block, in_width), bf16),
+        ((owners * block, out_width), bf16),
+        ((4 * half, width), bf16),
+        ((width, 4 * units), bf16),
+        ((width, 4 * units), bf16),
+        ((4 * units, width), bf16),
+    ]
+    return pl.pallas_call(
+        functools.partial(forward_kernel, far, near, experts, rows * owners),
+        name="forward",
+        out_shape=tuple(jax.ShapeDtypeStruct(s, d) for s, d in outs),
+        in_specs=[smem, smem, vmem, vmem] + [any_spec] * 9,
+        out_specs=(vmem,) * 11 + (any_spec,) * 6,
+        scratch_shapes=[
+            pltpu.VMEM((owners * block, in_width), bf16),
+            pltpu.VMEM((owners * block, out_width), bf16),
+            pltpu.VMEM((rows, width), bf16),
+            pltpu.VMEM((rows, in_width - 128), f32),
+            pltpu.VMEM((half, width), f32),
+            pltpu.VMEM((half, width), f32),
+            pltpu.VMEM((4, 8, 128), f32),
+            pltpu.VMEM((4, 8, 128), f32),
+            pltpu.SemaphoreType.DMA((90,)),
+            pltpu.SemaphoreType.DMA((90,)),
+            pltpu.SemaphoreType.DMA((8,)),
+        ],
+        compiler_params=pltpu.CompilerParams(
+            collective_id=0, has_side_effects=True, vmem_limit_bytes=56 * 1024 * 1024
+        ),
+    )(lengths, loss_grad, routes, tokens, small, w_query, w_key, w_value, out_block, out_grad, gate, up, down)
+
+
+class RowReduce:
+    def __init__(self, net, partial, inbox, part, order):
+        self.net, self.partial, self.inbox, self.order = net, partial, inbox, order
+        self.rows, self.first, self.size = part
+        self.copies = {}
+
+    def place(self, mask):
+        fsdp, ctx = 0, 0
+        for position, (axis, bit) in enumerate(self.order):
+            if mask >> position & 1:
+                fsdp, ctx = (fsdp ^ bit, ctx) if axis == "fsdp" else (fsdp, ctx ^ bit)
+        index = (lax.axis_index("fsdp") ^ fsdp) * 2 + (lax.axis_index("ctx") ^ ctx)
+        return pl.ds(pl.multiple_of(index * self.rows + self.first, 16), self.size)
+
+    def box(self, mask):
+        return pl.ds((mask - 1) * self.size, self.size)
+
+    def step(self, mask):
+        rows, last = self.place(mask), mask.bit_length() - 1
+        if last + 1 < len(self.order):
+            value = self.partial[rows, :].astype(f32)
+            for later in range(last + 1, len(self.order)):
+                source = mask | 1 << later
+                self.net.arrive(self.copies[source])
+                value = value + self.inbox[self.box(source), :].astype(f32)
+            if mask == 0:
+                return value
+            self.partial[rows, :] = value.astype(bf16)
+        self.copies[mask] = self.net.start(
+            self.partial.at[rows], self.inbox.at[self.box(mask)], dim_peer(self.order[last])
+        )
+
+    def level(self, last):
+        for mask in reversed(range(1 << last, 2 << last)):
+            self.step(mask)
+
+
+def backward_kernel(
+    far, near, experts, group,
+    lengths_ref, row_ref, dx_ref, middle_ref, probs_ref, mask_ref, grad_hbm,
+    tokens_hbm, query_hbm, kv_hbm, lse_ref, attended_hbm, cos_ref, sin_ref,
+    in_hbm, out_hbm, moe_hbm, gu_hbm, down_hbm,
+    output_hbm, loss_ref, tokens_grad_hbm, in_ref, out_ref, extra_ref, gate_ref, up_ref, down_ref,
+    grad_ref, tokens, query, kv, attended, in_full, out_full,
+    out_in, att_grad, qkv_grad, kv_grad, kv_sent, kv_got,
+    in_box, out_box,
+    mid_grad, back_sent, back_got, tok_stage, extra_rows, extra_sent, extra_got,
+    moe_own, moe_far, moe_near, moe_cross, moe_back,
+    gate_own, gate_x, gate_sent, gate_s,
+    up_own, up_s, up_sent, up_x,
+    down_own, down_x, down_sent, down_s,
+    loss_sent, loss_got,
     send_sems, recv_sems, local_sems,
 ):
     far_dev, near_dev, share_dev = peer(far), peer(near), peer(SHARE)
     ctx_dev, core_dev = peer(0, 1), peer(0, 0, 1)
     greet([far_dev, near_dev, share_dev, ctx_dev, core_dev])
     net = Exchange(send_sems, recv_sems, local_sems)
-    fars = [("fsdp", far), ("fsdp", SHARE)]
-    low, across = ("fsdp", near), ("ctx", 1)
-    place = lax.axis_index("ctx")
-    rows = in_ref.shape[0]
-    parts = [((0, rows // 2), fars + [across, low]), ((rows // 2, rows // 2), fars + [low, across])]
-    ins = [RowGather(net, in_ref, in_full, part, order) for part, order in parts]
-    me = lax.axis_index("fsdp") * 2 + place
-    own_rows = pl.ds(pl.multiple_of(me * rows, 16), rows)
-    net.keep(in_ref, in_full.at[own_rows])
-    net.keep(out_ref, out_full.at[own_rows])
-
-    half = grad_ref.shape[0]
+    ctx_place, core = lax.axis_index("ctx"), lax.axis_index("tp")
+    half, width = middle_ref.shape
+    rows = 2 * half
     quarter = half // 2
-    own_half = [pl.ds(k * quarter, quarter) for k in range(2)]
+    own_rows = pl.ds(pl.multiple_of(core * half, 16), half)
+    other_rows = pl.ds(pl.multiple_of((1 - core) * half, 16), half)
+    halves = [pl.ds(k * quarter, quarter) for k in range(2)]
+
     far_rows = [pl.ds(2 * half + k * half, quarter) for k in range(2)]
     cross_rows = [pl.ds(2 * half + k * half + quarter, quarter) for k in range(2)]
-    net.keep(grad_ref, grads.at[pl.ds(0, half)])
-
-    width, units = gate_ref.shape
-
-    def slot(full, piece, which=None):
-        if full is down_all:
-            start, size = piece * units, units
+    crossed = [net.start(moe_hbm.at[cross_rows[k]], moe_cross.at[halves[k]], near_dev) for k in range(2)]
+    units = gu_hbm.shape[1] // 4
+    wide = width // 2
+
+    def wide_half(place):
+        return pl.ds(pl.multiple_of(place * wide, 128), wide)
+
+    gate_cols, up_own_cols, up_par_cols = pl.ds(0, 2 * units), pl.ds(2 * units, units), pl.ds(3 * units, units)
+    gate_first = net.start(gu_hbm.at[wide_half(1 - ctx_place), gate_cols], gate_x, ctx_dev)
+    up_first = net.start(gu_hbm.at[:, up_par_cols], up_s, share_dev)
+    near_first = net.start(moe_hbm.at[pl.ds(half, half)], moe_near, near_dev)
+    down_first = net.start(down_hbm.at[:, wide_half(1 - ctx_place)], down_x, ctx_dev)
+    pairs = [
+        (in_hbm, in_full), (out_hbm, out_full), (attended_hbm, attended), (query_hbm, query),
+        (kv_hbm, kv), (tokens_hbm, tokens), (moe_hbm.at[pl.ds(0, half)], moe_own),
+        (moe_hbm.at[far_rows[0]], moe_far.at[halves[0]]), (moe_hbm.at[far_rows[1]], moe_far.at[halves[1]]),
+        (gu_hbm.at[wide_half(ctx_place), gate_cols], gate_own), (gu_hbm.at[:, up_own_cols], up_own),
+        (down_hbm.at[:, wide_half(ctx_place)], down_own), (grad_hbm.at[own_rows], grad_ref),
+    ]
+    for src, dst in pairs:
+        net.keep(src, dst)
+
+    def loaded(*numbers):
+        for number in numbers:
+            net.settle(number)
+
+    loaded(0, 12)
+    flipped_extra = in_full[:, :128].astype(f32).T
+    attn_gain, moe_gain = flipped_extra[experts : experts + 1], flipped_extra[experts + 1 : experts + 2]
+    lane = lax.broadcasted_iota(jnp.int32, (half, 128), 1)
+    probs, mask = probs_ref[...], mask_ref[...]
+    pair = dx_ref[:, width:]
+    gate_grad = jnp.where(lane < experts, pair + pltpu.roll(pair, 128 - experts, 1), 0.0)
+    chosen = probs * mask
+    chosen_total = jnp.sum(chosen, axis=1, keepdims=True)
+    weighted = jnp.sum(gate_grad * chosen, axis=1, keepdims=True) / chosen_total
+    prob_grad = mask * (gate_grad - weighted) / chosen_total + row_ref[0:1, :]
+    logit_grad = probs * (prob_grad - jnp.sum(prob_grad * probs, axis=1, keepdims=True))
+    logit_high = logit_grad.astype(bf16)
+    logit_low = (logit_grad - logit_high.astype(f32)).astype(bf16)
+    router = in_full[:, :128]
+    step = quarter // 2
+    gain_moe = jnp.zeros((1, width), f32)
+    router_grad = jnp.zeros((128, width), f32)
+    for k in range(half // step):
+        at = slice(k * step, (k + 1) * step)
+        middle = middle_ref[at, :]
+        inverse = lax.rsqrt(jnp.mean(middle * middle, axis=1, keepdims=True) + epsilon)
+        scaled = middle * inverse
+        normed_moe = (scaled * moe_gain).astype(bf16)
+        moe_grad = dx_ref[at, :width] + dot_nt(logit_high[at], router) + dot_nt(logit_low[at], router)
+        router_grad += dot(logit_high[at], normed_moe, 0, 0) + dot(logit_low[at], normed_moe, 0, 0)
+        gain_moe += jnp.sum(moe_grad * scaled, axis=0, keepdims=True)
+        a = moe_grad * moe_gain
+        grad = grad_ref[at, :].astype(f32) + inverse * (a - scaled * jnp.mean(a * scaled, axis=1, keepdims=True))
+        mid_grad[at, :] = grad
+        out_in[pl.ds(pl.multiple_of(core * half + k * step, 16), step), :] = grad.astype(bf16)
+    out_in_copy = net.start(out_in.at[own_rows], out_in.at[own_rows], core_dev)
+    row = lax.broadcasted_iota(jnp.int32, (128, width), 0)
+    extra_rows[...] = jnp.where(row == experts + 1, gain_moe, router_grad)
+
+    loss_dims = [core_dev, ctx_dev, near_dev, share_dev, far_dev]
+    loss_state = [jnp.broadcast_to(jnp.sum(probs, axis=0, keepdims=True), (8, 128))]
+    loss_copies = []
+
+    def loss_step():
+        k = len(loss_copies)
+        if k > 0:
+            net.arrive(loss_copies[-1])
+            loss_state[0] = loss_state[0] + loss_got[k - 1]
+        if k < len(loss_dims):
+            loss_sent[k] = loss_state[0]
+            loss_copies.append(net.start(loss_sent.at[k], loss_got.at[k], loss_dims[k]))
+
+    loss_step()
+
+    net.arrive(out_in_copy)
+    loaded(1, 2)
+    att_grad[...] = dot_nn(out_in[...], out_full[...]).astype(bf16)
+
+    def out_tile(i, carry):
+        cols = aligned(i, TILE)
+        out_full[cols, :] = dot_nn(out_in[:, cols].T, attended[...]).astype(bf16)
+        return carry
+
+    lax.fori_loop(0, width // TILE, out_tile, 0)
+    block = in_ref.shape[0]
+    low, across = ("fsdp", near), ("ctx", 1)
+    fars = [("fsdp", far), ("fsdp", SHARE)]
+    orders = [fars + [across, low], fars + [low, across]]
+    part_size = block // 2
+    sums_out = [
+        RowReduce(net, out_full, out_box.at[k], (block, k * part_size, part_size), orders[k]) for k in range(2)
+    ]
+    for s in sums_out:
+        s.level(3)
+    loss_step()
+    net.sent(out_in_copy)
+    loaded(5)
+    normed_step = half // 2
+    for k in range(rows // normed_step):
+        at = slice(k * normed_step, (k + 1) * normed_step)
+        x = tokens[at, :].astype(f32)
+        inverse = lax.rsqrt(jnp.mean(x * x, axis=1, keepdims=True) + epsilon)
+        out_in[at, :] = (x * inverse * attn_gain).astype(bf16)
+
+    loaded(3, 4)
+    pack = kv.shape[0]
+    kv_grad[...] = jnp.zeros_like(kv_grad)
+    keys, values = kv[:, :HEAD_DIM], kv[:, HEAD_DIM:]
+    keys_flipped = keys.T
+    query_number = lax.broadcasted_iota(jnp.int32, (1, half), 1) + ctx_place * rows
+    key_number = lax.broadcasted_iota(jnp.int32, (pack, 1), 0)
+    scale = HEAD_DIM ** (-0.5)
+
+    def head_block(i, carry):
+        head, block_index = i // 2, lax.rem(i, 2)
+        cols = aligned(head, HEAD_DIM)
+        at = aligned(block_index, half)
+        number = query_number + block_index * half
+        allowed = (key_number >= document_start(lengths_ref, number)) & (key_number <= number)
+        q, grad = query[at, cols], att_grad[at, cols]
+        log_total = lse_ref[pl.ds(head, 1), at]
+        weights = jnp.where(allowed, jnp.exp(dot_nt(keys, q) * scale - log_total), 0.0)
+        weight_grad = dot_nt(values, grad)
+        delta = jnp.sum(weights * weight_grad, axis=0, keepdims=True)
+        score_grad = (weights * (weight_grad - delta)).astype(bf16)
+        kv_grad[:, :HEAD_DIM] += dot_nn(score_grad, q) * scale
+        kv_grad[:, HEAD_DIM:] += dot_nn(weights.astype(bf16), grad)
+        query_grad = (dot_nn(keys_flipped, score_grad) * scale).T
+        turned = query_grad * cos_ref[at, :] - pltpu.roll(query_grad, HEAD_DIM // 2, 1) * sin_ref[at, :]
+        qkv_grad[at, cols] = turned.astype(bf16)
+        return carry
+
+    third = 2 * group // 3
+    lax.fori_loop(0, third, head_block, 0)
+    loss_step()
+    loaded(6, 7, 8)
+    far_sums = []
+    for k in range(2):
+        net.arrive(crossed[k])
+        moe_far[halves[k], :] = (moe_far[halves[k], :].astype(f32) + moe_cross[halves[k], :].astype(f32)).astype(bf16)
+        far_sums.append(net.start(moe_far.at[halves[k]], moe_back.at[halves[k]], far_dev))
+    for s in sums_out:
+        s.level(2)
+    lax.fori_loop(third, 2 * third, head_block, 0)
+    loss_step()
+    for s in sums_out:
+        s.level(1)
+    lax.fori_loop(2 * third, 2 * group, head_block, 0)
+    loss_step()
+    ctx_rows = pl.ds(pl.multiple_of(ctx_place * rows, 16), rows)
+    ctx_other = pl.ds(pl.multiple_of((1 - ctx_place) * rows, 16), rows)
+    kv_sent[...] = kv_grad[ctx_other, :].astype(bf16)
+    kv_copy = net.start(kv_sent, kv_got, ctx_dev)
+    for s in sums_out:
+        s.level(0)
+    loss_step()
+    loss = jnp.sum(loss_state[0][0:1] * row_ref[1:2, :], axis=1, keepdims=True)
+    loss_ref[...] = jnp.broadcast_to(loss, loss_ref.shape)
+    net.arrive(kv_copy)
+    kv_sum = kv_grad[ctx_rows, :] + kv_got[...].astype(f32)
+    key_grad = kv_sum[:, :HEAD_DIM]
+    key_grad = key_grad * cos_ref[...] - pltpu.roll(key_grad, HEAD_DIM // 2, 1) * sin_ref[...]
+    heads_width = group * HEAD_DIM
+    qkv_grad[:, heads_width : heads_width + HEAD_DIM] = key_grad.astype(bf16)
+    qkv_grad[:, heads_width + HEAD_DIM :] = kv_sum[:, HEAD_DIM:].astype(bf16)
+
+    gain_attn = jnp.zeros((1, width), f32)
+
+    def attn_scaled(at):
+        x = tokens[at, :].astype(f32)
+        inverse = lax.rsqrt(jnp.mean(x * x, axis=1, keepdims=True) + epsilon)
+        return inverse, x * inverse
+
+    for k in range(2):
+        at = other_rows if k == 0 else own_rows
+        part = dot_nt(qkv_grad[at, :], in_full[:, 128:])
+        gain_attn += jnp.sum(part * attn_scaled(at)[1], axis=0, keepdims=True)
+        if k == 0:
+            back_sent[...] = part.astype(bf16)
+            back_copy = net.start(back_sent, back_got, core_dev)
         else:
-            start, size = 0, width
-        if which is not None:
-            size //= 2
-            start = pl.multiple_of(start + which * size, 16)
-        if full is down_all:
-            return full.at[pl.ds(start, size)]
-        return full.at[pl.ds(start, size), pl.ds(piece * units, units)]
-
-    matrices = [(gate_ref, gate_all), (up_ref, up_all), (down_ref, down_all)]
-    for ref, full in matrices:
-        net.keep(ref, slot(full, 0))
-        net.start(ref, slot(full, 1), core_dev)
-    first, rest = gather_codes(far, near)
-    for code in first:
-        for g in ins:
-            g.arrive(code)
-    outs = [RowGather(net, out_ref, out_full, part, order) for part, order in parts]
-    far_copies = [net.start(grad_ref.at[own_half[k]], grads.at[far_rows[k]], far_dev) for k in range(2)]
-    from_share = []
-    for ref, full in matrices:
-        size = ref.shape[0] // 2
-        part = ref.at[pl.ds(pl.multiple_of(place * size, 16), size)]
-        from_share.append(net.start(part, slot(full, 2, place), share_dev))
-    for code in rest:
-        for g in ins:
-            g.arrive(code)
-    for code in first + rest:
-        for g in outs:
-            g.arrive(code)
-    net.start(grad_ref, grads.at[pl.ds(half, half)], near_dev)
+            tok_stage[...] = part
+    def in_tile(i, carry):
+        cols = aligned(i, TILE)
+        in_full[cols, 128:] = dot_nn(out_in[:, cols].T, qkv_grad[...]).astype(bf16)
+        return carry
+
+    lax.fori_loop(0, width // TILE, in_tile, 0)
+    extra_rows[...] = jnp.where(row == experts, gain_attn, extra_rows[...])
+    in_full[:, :128] = extra_rows[...].T.astype(bf16)
+    sums_in = [
+        RowReduce(net, in_full, in_box.at[k], (block, k * part_size, part_size), orders[k]) for k in range(2)
+    ]
+    for s in sums_in:
+        s.level(3)
+
+    net.arrive(back_copy)
     for k in range(2):
-        net.arrive(far_copies[k])
-        net.start(grads.at[far_rows[k]], grads.at[cross_rows[k]], near_dev)
-    from_ctx = []
-    for k, (ref, full) in enumerate(matrices):
-        net.arrive(from_share[k])
-        from_ctx.append(net.start(slot(full, 2, place), slot(full, 2, place), ctx_dev))
-        net.start(slot(full, 2, place), slot(full, 3, place), core_dev)
-    for k, (ref, full) in enumerate(matrices):
-        net.arrive(from_ctx[k])
-        net.start(slot(full, 2, 1 - place), slot(full, 3, 1 - place), core_dev)
+        at = pl.ds(k * quarter, quarter)
+        inverse, scaled = attn_scaled(pl.ds(pl.multiple_of(core * half + k * quarter, 16), quarter))
+        a = (tok_stage[at, :] + back_got[at, :].astype(f32)) * attn_gain
+        tok_stage[at, :] = mid_grad[at, :] + inverse * (a - scaled * jnp.mean(a * scaled, axis=1, keepdims=True))
+    net.keep(tok_stage, tokens_grad_hbm.at[own_rows])
+    net.start(tok_stage, tokens_grad_hbm.at[own_rows], core_dev)
+
+    def pieces(size):
+        return [slice(k * size // 4, (k + 1) * size // 4) for k in range(4)]
+
+    loaded(9, 10, 11)
+    net.arrive(gate_first)
+    for at in pieces(wide):
+        total = gate_own[at, :].astype(f32) + gate_x[at, :].astype(f32)
+        gate_ref[at, :] = total[:, :units]
+        gate_sent[at, :] = total[:, units:].astype(bf16)
+    gate_last = net.start(gate_sent, gate_s, share_dev)
+    for s in sums_in:
+        s.level(2)
+    net.arrive(up_first)
+    up_sent[...] = (up_own[wide_half(1 - ctx_place), :].astype(f32) + up_s[wide_half(1 - ctx_place), :].astype(f32)).astype(bf16)
+    up_last = net.start(up_sent, up_x, ctx_dev)
+    up_ref[...] = up_own[wide_half(ctx_place), :].astype(f32) + up_s[wide_half(ctx_place), :].astype(f32)
+    for s in sums_in:
+        s.level(1)
+    net.arrive(down_first)
+    for at in pieces(units):
+        down_ref[at, :] = down_own[at, :].astype(f32) + down_x[at, :].astype(f32)
+        after = slice(at.start + units, at.stop + units)
+        down_sent[at, :] = (down_own[after, :].astype(f32) + down_x[after, :].astype(f32)).astype(bf16)
+    down_last = net.start(down_sent, down_s, share_dev)
+    for s in sums_in:
+        s.level(0)
+
+    net.arrive(near_first)
+    for k in range(2):
+        net.arrive(far_sums[k])
+    for k in range(2):
+        at = halves[k]
+        moe_out = moe_own[at, :].astype(f32) + moe_near[at, :].astype(f32) + moe_back[at, :].astype(f32)
+        moe_own[at, :] = (middle_ref[at, :] + moe_out).astype(bf16)
+    net.keep(moe_own, output_hbm.at[own_rows])
+    net.start(moe_own, output_hbm.at[own_rows], core_dev)
+
+    for k in range(2):
+        at = slice(k * part_size, (k + 1) * part_size)
+        out_ref[at, :] = sums_out[k].step(0)
+        value = sums_in[k].step(0)
+        extra_sent[at, :] = value[:, :128]
+        in_ref[at, :] = value[:, 128:]
+    extra_copy = net.start(extra_sent, extra_got, core_dev)
+    net.arrive(gate_last)
+    gate_ref[...] += gate_s[...].astype(f32)
+    net.arrive(up_last)
+    up_ref[...] += up_x[...].astype(f32)
+    net.arrive(down_last)
+    down_ref[...] += down_s[...].astype(f32)
+    net.arrive(extra_copy)
+    extra_ref[...] = extra_sent[...] + extra_got[...]
     net.finish()
 
 
-def gather_all(in_block, out_block, grad_half, gate, up, down):
+def backward_on_chip(
+    lengths, row, dx, middle, probs, mask, out_grad, tokens, query, kv, lse, attended, cos, sin,
+    in_full, out_full, moe_rows, gate_up, down, experts,
+):
     far, near = token_bits()
     owners = lax.axis_size("fsdp") * lax.axis_size("ctx")
-    width, units = gate.shape
+    half, width = middle.shape
+    rows, heads_width = query.shape
+    pack, kv_width = kv.shape
+    units = down.shape[0] // 2
+    block = in_full.shape[0] // owners
+    in_width, out_width = in_full.shape[1], out_full.shape[1]
     any_spec = pl.BlockSpec(memory_space=pl.ANY)
-    shapes = [
-        (owners * in_block.shape[0], in_block.shape[1]),
-        (owners * out_block.shape[0], out_block.shape[1]),
-        (4 * grad_half.shape[0], width),
-        (width, 4 * units),
-        (width, 4 * units),
-        (4 * units, width),
-    ]
+    vmem = pl.BlockSpec(memory_space=pltpu.VMEM)
+    smem = pl.BlockSpec(memory_space=pltpu.SMEM)
+
+    def low(*shape):
+        return pltpu.VMEM(shape, bf16)
+
+    def wide(*shape):
+        return pltpu.VMEM(shape, f32)
+
+    boxes = 15 * (block // 2)
     return pl.pallas_call(
-        functools.partial(gather_kernel, far, near),
-        name="gather",
-        out_shape=tuple(jax.ShapeDtypeStruct(s, bf16) for s in shapes),
-        in_specs=[any_spec] * 6,
-        out_specs=(any_spec,) * 6,
+        functools.partial(backward_kernel, far, near, experts, heads_width // HEAD_DIM),
+        name="backward",
+        out_shape=(
+            jax.ShapeDtypeStruct((rows, width), bf16),
+            jax.ShapeDtypeStruct((8, 128), f32),
+            jax.ShapeDtypeStruct((rows, width), f32),
+            jax.ShapeDtypeStruct((block, in_width - 128), f32),
+            jax.ShapeDtypeStruct((block, out_width), f32),
+            jax.ShapeDtypeStruct((block, 128), f32),
+            jax.ShapeDtypeStruct((width // 2, units), f32),
+            jax.ShapeDtypeStruct((width // 2, units), f32),
+            jax.ShapeDtypeStruct((units, width // 2), f32),
+        ),
+        in_specs=[smem] + [vmem] * 5 + [any_spec] * 4 + [vmem, any_spec, vmem, vmem] + [any_spec] * 5,
+        out_specs=(any_spec, vmem, any_spec) + (vmem,) * 6,
         scratch_shapes=[
-            pltpu.SemaphoreType.DMA((80,)),
-            pltpu.SemaphoreType.DMA((80,)),
-            pltpu.SemaphoreType.DMA((6,)),
+            low(half, width), low(rows, width), low(rows, heads_width), low(pack, kv_width), low(rows, heads_width),
+            low(*in_full.shape), low(*out_full.shape),
+            low(rows, width), low(rows, heads_width), low(rows, in_width - 128),
+            wide(pack, kv_width), low(rows, kv_width), low(rows, kv_width),
+            low(2, boxes, in_width), low(2, boxes, out_width),
+            wide(half, width), low(half, width), low(half, width), wide(half, width),
+            wide(128, width), wide(block, 128), wide(block, 128),
+            low(half, width), low(half, width), low(half, width), low(half, width), low(half, width),
+            low(width // 2, 2 * units), low(width // 2, 2 * units), low(width // 2, units), low(width // 2, units),
+            low(width, units), low(width, units), low(width // 2, units), low(width // 2, units),
+            low(2 * units, width // 2), low(2 * units, width // 2), low(units, width // 2), low(units, width // 2),
+            wide(5, 8, 128), wide(5, 8, 128),
+            pltpu.SemaphoreType.DMA((90,)),
+            pltpu.SemaphoreType.DMA((90,)),
+            pltpu.SemaphoreType.DMA((16,)),
         ],
-        compiler_params=pltpu.CompilerParams(collective_id=0, has_side_effects=True),
-    )(in_block, out_block, grad_half, gate, up, down)
+        compiler_params=pltpu.CompilerParams(
+            collective_id=2, has_side_effects=True, vmem_limit_bytes=62 * 1024 * 1024
+        ),
+    )(
+        lengths, row, dx, middle, probs, mask, out_grad, tokens, query, kv, lse, attended, cos, sin,
+        in_full, out_full, moe_rows, gate_up, down,
+    )
 
 
 def rms_back_gain(inverse, scaled, row_gains, upstream):
@@ -1156,189 +1744,41 @@
     out_grad,
     loss_grad,
 ):
-    row_count, width = tokens.shape
-    ctx_count = lax.axis_size("ctx")
-    fsdp_count = lax.axis_size("fsdp")
-    ctx_place = lax.axis_index("ctx")
-    tp_place = lax.axis_index("tp")
-    own_expert = lax.axis_index("fsdp")
-    top_count = routes.shape[1]
     expert_count = w_router.shape[1]
-    pack_count = row_count * ctx_count
-    base_row = ctx_place * row_count
-    half_rows = row_count // 2
-    token_total = pack_count * fsdp_count
-    if fsdp_count != 8:
+    if lax.axis_size("fsdp") != 8:
         return on_any_slice(
             tokens, lengths, routes, norm_attn, w_query, w_key, w_value, w_out, norm_moe, w_router,
             w_gate, w_up, w_down, out_grad, loss_grad,
         )
-    orders = weight_orders()
-
-    extras = widen([norm_attn[:, None], norm_moe[:, None], w_router])
-    extra_width = extras.shape[1]
-    in_block = jnp.concatenate([extras, w_query, w_key, w_value], axis=1)
-    upstream_low = own_part(out_grad, tp_place)
-    in_weights, out_weights, grad_blocks, gate_all, up_all, down_all = gather_all(
-        in_block, w_out.T, upstream_low, w_gate[0], w_up[0], w_down[0]
-    )
-    gains = in_weights[:, :2].astype(f32)
-    attn_gain, moe_gain = gains[:, 0], gains[:, 1]
-    full_router = in_weights[:, 2 : 2 + expert_count]
-    qkv_weights = in_weights[:, extra_width:]
+    small = widen([w_router, norm_attn[:, None], norm_moe[:, None]])
     query_width, kv_width = w_query.shape[1], w_key.shape[1]
-
-    own_routes = own_part(routes, tp_place)
-    expert_ids = jnp.arange(expert_count, dtype=jnp.int32)
-    route_mask = jnp.sum((own_routes[:, :, None] == expert_ids).astype(f32), axis=1)
-    fraction = sum_everywhere(jnp.sum(route_mask, axis=0)) / (token_total * top_count)
-
-    doc_ids, positions, doc_first = pack_layout(lengths[0], pack_count)
-    own_positions = lax.dynamic_slice_in_dim(positions, base_row, row_count, 0)
-    cos_table, sin_table = rope_tables(own_positions)
-    x_float = tokens.astype(f32)
-    _, _, normed_full = rms_parts(x_float, attn_gain)
-    normed_attn = normed_full.astype(bf16)
-    local_heads = query_width // HEAD_DIM
-    local_kv = kv_width // HEAD_DIM
-    qkv = dot(normed_attn, qkv_weights)
-    rotated = rotate(
-        qkv[:, : query_width + kv_width].reshape(row_count, local_heads + local_kv, HEAD_DIM),
-        cos_table,
-        sin_table,
-    ).astype(bf16)
-    queries = rotated[:, :local_heads]
-    key_own = rotated[:, local_heads:].reshape(row_count, kv_width)
-    value_own = qkv[:, query_width + kv_width :].astype(bf16)
-    kv_own = jnp.concatenate([key_own, value_own], axis=1)
-    kv_pack = side_by_side(kv_own, swap(kv_own, "ctx"), ctx_place)
-    pack_keys = kv_pack[:, :kv_width].reshape(pack_count, local_kv, HEAD_DIM)
-    pack_values = kv_pack[:, kv_width:].reshape(pack_count, local_kv, HEAD_DIM)
-    grouped = queries.reshape(row_count, local_kv, local_heads // local_kv, HEAD_DIM)
-    mixed_full, log_total = attention_forward(
-        grouped, pack_keys, pack_values, doc_ids, doc_first, base_row, row_count
-    )
-    attended = mixed_full.astype(bf16)
-    out_part = dot(attended, out_weights, 1, 1)
-    attn_out = own_part(out_part, tp_place) + swap(own_part(out_part, 1 - tp_place), "tp")
-
-    x_half = own_part(tokens, tp_place).astype(f32)
-    middle = x_half + attn_out
-    inverse_moe, scaled_moe, normed_mid = rms_parts(middle, moe_gain)
-    normed_moe = normed_mid.astype(bf16)
-    logits = dot(normed_moe, full_router)
-    shifted = jnp.exp(logits - jnp.max(logits, axis=-1, keepdims=True))
-    router_probs = shifted / jnp.sum(shifted, axis=-1, keepdims=True)
-    chosen = router_probs * route_mask
-    chosen_total = jnp.sum(chosen, axis=-1, keepdims=True)
-    gate_weights = chosen / chosen_total
-    probs_global = sum_everywhere(jnp.sum(router_probs, axis=0))
-    balance_loss = (expert_count * jnp.sum(fraction * (probs_global / token_total))).reshape(1)
-
-    payload = jnp.concatenate([normed_moe, widen(as_pair(gate_weights))], axis=1)
+    (
+        payload, middle, probs, mask, row, query, kv_pack, lse, attended, cos, sin,
+        in_weights, out_weights, grad_rows, gate_all, up_all, down_all,
+    ) = forward_on_chip(
+        lengths, loss_grad, routes, tokens, small, w_query, w_key, w_value, w_out.T, out_grad,
+        w_gate[0], w_up[0], w_down[0], expert_count,
+    )
     returned, moe_rows, keep_gu, got_gu, keep_d, got_d = experts_on_chip(
-        payload, grad_blocks, gate_all, up_all, down_all, expert_count
-    )
-    far, near = token_bits()
-    quarter = half_rows // 2
-    second = 3 * half_rows
-    moe_parts = {
-        0: moe_rows[:half_rows].astype(f32),
-        near: moe_rows[half_rows : 2 * half_rows].astype(f32),
-        far: jnp.concatenate([moe_rows[2 * half_rows :][:quarter], moe_rows[second:][:quarter]]).astype(f32),
-        far ^ near: jnp.concatenate([moe_rows[2 * half_rows + quarter : second], moe_rows[second + quarter :]]).astype(f32),
-    }
-    moe_out = reduce_tokens(moe_parts)
-    out_half = (middle + moe_out).astype(bf16)
-    output = side_by_side(out_half, swap(out_half, "tp"), tp_place)
-    units = keep_d.shape[0] // 2
-
-    def summed(keep, got, cols):
-        return keep[:, cols].astype(f32) + got[:, cols].astype(f32)
-
-    gate_w_out = across_share(across_ctx(summed(keep_gu, got_gu, slice(0, 2 * units))))
-    up_w_out = across_ctx(across_share(summed(keep_gu, got_gu, slice(2 * units, None))))
-    down_w_out = across_share(across_ctx(summed(keep_d, got_d, slice(None)), 1), 0)
-
-    moe_in_grad = returned[:, :width]
-    gate_grad = from_pair(returned[:, width:], expert_count)
-    weighted = jnp.sum(gate_grad * gate_weights, axis=-1, keepdims=True)
-    chosen_grad = route_mask * (gate_grad - weighted) / chosen_total
-    prob_grad = chosen_grad + loss_grad[0] * expert_count * fraction / token_total
-    logit_grad = router_probs * (
-        prob_grad - jnp.sum(prob_grad * router_probs, axis=-1, keepdims=True)
-    )
-    moe_grad = moe_in_grad + lax.dot_general(
-        logit_grad, full_router.astype(f32), (((1,), (1,)), ((), ())), precision=highest
-    )
-    router_grad = lax.dot_general(
-        normed_moe.astype(f32), logit_grad, (((0,), (0,)), ((), ())), precision=highest
-    )
-    gain_moe_grad = jnp.sum(moe_grad * scaled_moe, axis=0)
-    upstream = upstream_low.astype(f32)
-    middle_grad = upstream + rms_back(inverse_moe, scaled_moe, moe_gain, moe_grad)
-    out_in_half = middle_grad.astype(bf16)
-    out_in = side_by_side(out_in_half, swap(out_in_half, "tp"), tp_place)
-    mixed_grad = dot(out_in, out_weights).astype(bf16)
-    out_w_grad = dot(out_in, attended, 0, 0)
-    small_grads = widen([gain_moe_grad[:, None], router_grad])
-    out_reduced = reduce_weights(jnp.concatenate([small_grads, out_w_grad], axis=1), orders)
-    small_out = out_reduced[:, : 1 + expert_count]
-    small_out = small_out + swap(small_out, "tp")
-    w_out_grad = out_reduced[:, small_grads.shape[1] :].T
-
-    query_acc, key_grad_pack, value_grad_pack = attention_backward(
-        grouped,
-        pack_keys,
-        pack_values,
-        mixed_grad,
-        log_total,
-        doc_ids,
-        doc_first,
-        base_row,
-        row_count,
-    )
-    kv_grad_pack = jnp.concatenate(
-        [key_grad_pack.reshape(pack_count, kv_width), value_grad_pack.reshape(pack_count, kv_width)],
-        axis=1,
-    )
-    kv_grad = across_ctx(kv_grad_pack)
-    query_grad = (
-        rotate(query_acc.reshape(row_count, local_heads, HEAD_DIM), cos_table, -sin_table)
-        .astype(bf16)
-        .reshape(row_count, query_width)
-    )
-    key_grad = (
-        rotate(kv_grad[:, :kv_width].reshape(row_count, local_kv, HEAD_DIM), cos_table, -sin_table)
-        .astype(bf16)
-        .reshape(row_count, kv_width)
-    )
-    qkv_grad = jnp.concatenate([query_grad, key_grad, kv_grad[:, kv_width:].astype(bf16)], axis=1)
-    attn_in_part = dot(qkv_grad, qkv_weights, 1, 1)
-    attn_in_grad = own_part(attn_in_part, tp_place) + swap(
-        own_part(attn_in_part, 1 - tp_place).astype(bf16), "tp"
-    ).astype(f32)
-    inverse_attn, scaled_attn, _ = rms_parts(x_half, attn_gain)
-    gain_attn_grad = jnp.sum(attn_in_grad * scaled_attn, axis=0)
-    tokens_half = middle_grad + rms_back(inverse_attn, scaled_attn, attn_gain, attn_in_grad)
-    tokens_grad = side_by_side(tokens_half, swap(tokens_half, "tp"), tp_place)
-    qkv_w_grad = dot(normed_attn, qkv_grad, 0, 0)
-    gain_column = widen([gain_attn_grad[:, None]])
-    in_reduced = reduce_weights(jnp.concatenate([gain_column, qkv_w_grad], axis=1), orders)
-    gain_out = in_reduced[:, :1]
-    gain_out = (gain_out + swap(gain_out, "tp"))[:, 0]
-    start = gain_column.shape[1]
+        payload, out_grad, w_gate[0], w_up[0], w_down[0], grad_rows, gate_all, up_all, down_all, expert_count
+    )
+    gate_up_grad = (keep_gu.astype(f32) + got_gu.astype(f32)).astype(bf16)
+    down_grad = (keep_d.astype(f32) + got_d.astype(f32)).astype(bf16)
+    output, loss, tokens_grad, in_reduced, out_reduced, small, gate_w_out, up_w_out, down_w_out = backward_on_chip(
+        lengths, row, returned, middle, probs, mask, out_grad, tokens, query, kv_pack, lse, attended, cos, sin,
+        in_weights, out_weights, moe_rows, gate_up_grad, down_grad, expert_count,
+    )
     return (
         output,
-        balance_loss,
+        loss[0, :1],
         tokens_grad,
-        gain_out,
-        in_reduced[:, start : start + query_width],
-        in_reduced[:, start + query_width : start + query_width + kv_width],
-        in_reduced[:, start + query_width + kv_width :],
-        w_out_grad,
-        small_out[:, 0],
-        small_out[:, 1:],
+        small[:, expert_count],
+        in_reduced[:, :query_width],
+        in_reduced[:, query_width : query_width + kv_width],
+        in_reduced[:, query_width + kv_width :],
+        out_reduced.T,
+        small[:, expert_count + 1],
+        small[:, :expert_count],
         gate_w_out[None],
         up_w_out[None],
         down_w_out[None],

time: 692 us -> 493 us (0.71)
  Pallas kernels: 258 us -> 453 us
  waiting for transfers between devices: 130 us -> 0 us
  starting transfers between devices: 72.7 us -> 0 us
  local copies, waits for them, and re-layouts: 85.5 us -> 19.6 us
  other arithmetic: 68.2 us -> 11 us
  matrix products: 56.9 us -> 0 us
    pallas_call x1 -> x2, Pallas kernels: 147 us -> 351 us  [the longest x1 180 us: backward_on_chip(): pl.pallas_call(functools.partial(backward_kernel, far, near, experts, hea...]
    ppermute x52 -> x0, waiting for transfers between devices: 130 us -> none  [swap(): lax.ppermute(array, axis, [(i, i ^ bit) for i in range(lax.axis_size(axis...]
    ppermute x52 -> x0, starting transfers between devices: 72.7 us -> none  [swap(): lax.ppermute(array, axis, [(i, i ^ bit) for i in range(lax.axis_size(axis...]
    dot_general x27 -> x0, matrix products: 56.9 us -> none  [the longest x7 17.5 us: dot(): lax.dot_general(left, right, (((left_dim,), (right_dim,)), ((), ())), pre...]
    add x49 -> x0, other arithmetic: 22.4 us -> none  [the longest x18 9.26 us: reduce_rows(): lax.dynamic_index_in_dim(held, place, k) + swap(sent, *dim).astype(f32)]
    slice x20 -> x4, local copies, waits for them, and re-layouts: 21 us -> 6.08 us  [the longest x1 1.69 us: on_device(): in_reduced[:, :query_width]]
    reduce_sum x13 -> x0, other arithmetic: 11.9 us -> none  [the longest x2 3.35 us: rms_parts(): jnp.mean(values * values, axis=-1, keepdims=True) + epsilon]
    concatenate x5 -> x1, local copies, waits for them, and re-layouts: 12 us -> 0.08 us  [widen(): return jnp.concatenate(list(columns) + [pad], axis=1)]
  transfers between devices with their start and end apart: 52 -> 0, of which waited for: 28 -> 0; matrix products, arithmetic and copies ran while one was open for 19% -> 0% of each run, Pallas kernels for 0% -> 0%
where the time goes in v2:
time: 493 us; the launch traced here: 485 us
  Pallas kernels  453 us (92%)
  local copies, waits for them, and re-layouts  19.6 us (4%)
  other arithmetic  11 us (2%)
    pallas_call x1, Pallas kernels, backward_on_chip(): pl.pallas_call(functools.partial(backward_kernel, far, near, experts, hea...  180 us
    pallas_call x1, Pallas kernels, forward_on_chip(): pl.pallas_call(functools.partial(forward_kernel, far, near, experts, rows...  171 us
    pallas_call x1, Pallas kernels, experts_on_chip(): pl.pallas_call(functools.partial(expert_kernel, far, near, experts), name...  101 us
    unnamed x21, local copies, waits for them, and re-layouts  11.9 us

profile of v2, /device:TPU:11, one launch (start us, length us, event | category | flops | bytes accessed | tf_op | source)
XLA Modules:
  0.0 485.1 jit_solution(4066254010790750688)
XLA Ops:
  1.3 0.1 pad.3.clone
  1.4 0.8 copy.34
  2.1 0.8 copy.35
  2.9 0.8 copy.33
  3.7 0.7 maximum_maximum_fusion.small_hbm
  4.4 1.5 copy.36.routes_ref
  6.0 171.1 %forward.1 = (bf16[256,1664]{1,0:T(8,128)(2,1)}, f32[256,1536]{1,0:T(8,128)}, f32[256,128]{1,0:T(8,128)}, f32[256,128]{1,0:T(8,128)}, f32[8,128]{1,0:T(8,128)}, ...) custom-call(s32[1,3]{1,0:T(1,128)} %lengths_ref.3, ...), custom_call_target="tpu_custom_call" | custom-call | tf_op jit(solution)/shard_map/forward/pallas_call | solution.py:1021
  177.1 101.4 %experts.1 = (f32[256,1664]{1,0:T(8,128)}, bf16[1024,1536]{1,0:T(8,128)(2,1)}, bf16[1536,1536]{1,0:T(8,128)(2,1)}, bf16[1536,1536]{1,0:T(8,128)(2,1)}, bf16[768,...) custom-call(bf16[256,1664]{1,0:T(8,128)(2,1)} %get-tuple-element.46.x_ref, bf16[512,1536]{1,0:T(8,128)(2,1)} %grad_hbm.5, ...), custom_call_target="tpu_custom_call" | custom-call | flops 43486543872 | bytes 60000000 | tf_op jit(solution)/shard_map/experts/pallas_call | solution.py:652
  278.5 0.0 copy-start
  278.5 4.6 add_convert_fusion.1.down_hbm
  283.1 0.0 copy-done
  283.1 5.8 %add_convert_fusion.gu_hbm = bf16[1536,1536]{1,0:T(8,128)(2,1)} fusion(bf16[1536,1536]{1,0:T(8,128)(2,1)} %get-tuple-element.65, bf16[1536,1536]{1,0:T(8,128)(2,1)S(1)} %copy-done), kind=kLoop, calls=%fused_computation | loop fusion | flops 9437184 | bytes 14155776 | tf_op jit(solution)/shard_map/convert_element_type | solution.py:1765
  288.8 180.1 %backward.1 = (bf16[512,1536]{1,0:T(8,128)(2,1)}, f32[8,128]{1,0:T(8,128)}, f32[512,1536]{1,0:T(8,128)}, f32[96,1024]{1,0:T(8,128)}, f32[96,768]{1,0:T(8,128)}, ...) custom-call(s32[1,3]{1,0:T(1,128)} %lengths_ref.3, ...), custom_call_target="tpu_custom_call" | custom-call | tf_op jit(solution)/shard_map/backward/pallas_call | solution.py:1399
  468.9 0.0 copy-start.1
  469.0 1.3 slice.21
  470.3 1.6 slice_reduce_fusion
  471.9 1.5 copy.37
  473.3 1.5 fusion
  474.8 1.7 slice.23
  476.5 2.7 copy.45
  479.2 0.0 copy-done.1
  479.2 0.0 copy-start.5
  479.2 0.0 copy-start.4
  479.2 1.7 copy.46
  480.8 0.0 copy-done.5
  480.8 0.0 copy-start.3
  480.8 0.7 copy.47
  481.5 0.0 copy-done.4
  481.6 0.0 copy-start.2
  481.6 1.0 copy.48
  482.6 0.0 copy-done.3
  482.6 1.0 copy.49
  483.6 0.0 copy-done.2
  483.6 1.0 copy.50
  (1 shorter events, 0.0 us)
Async XLA Ops:
  278.5 4.6 copy-start
  468.9 10.2 %copy-start.1 = (f32[512,1536]{1,0:T(8,128)S(1)}, f32[512,1536]{1,0:T(8,128)}, u32[]{:S(2)}) copy-start(f32[512,1536]{1,0:T(8,128)} %get-tuple-element.122) | copy-start | bytes 9437188
  479.2 1.7 copy-start.5
  479.2 2.4 copy-start.4
  480.8 1.8 copy-start.3
  481.6 2.0 copy-start.2

commit v3 on v2

--- a/solution.py
+++ b/solution.py
@@ -378,6 +378,15 @@
 
 
 TILE = 256
+CHUNKS = 4
+
+
+def token_rows(half):
+    size = half // CHUNKS
+    own = [pl.ds(k * size, size) for k in range(CHUNKS)]
+    far = [pl.ds(2 * half + 2 * k * size, size) for k in range(CHUNKS)]
+    cross = [pl.ds(2 * half + (2 * k + 1) * size, size) for k in range(CHUNKS)]
+    return own, far, cross
 
 
 def expert_kernel(
@@ -395,10 +404,8 @@
     wd_hbm,
     dx_ref,
     part_ref,
-    keep_gu,
-    got_gu,
-    keep_d,
-    got_d,
+    sum_gu,
+    sum_d,
     xb,
     gb,
     wg,
@@ -421,9 +428,9 @@
     recv_sems,
     tp_send,
     tp_recv,
+    free_sem,
 ):
     half = x_ref.shape[0]
-    quarter = half // 2
     width = wg.shape[0]
     units = wg.shape[1]
     unit_tiles = units // TILE
@@ -431,12 +438,12 @@
     far_dev, near_dev, core_dev = peer(far), peer(near), peer(0, 0, 1)
     greet([far_dev, near_dev, core_dev])
 
-    far_rows = [pl.ds(2 * half + k * half, quarter) for k in range(2)]
-    cross_rows = [pl.ds(2 * half + k * half + quarter, quarter) for k in range(2)]
+    own_chunks, far_rows, cross_rows = token_rows(half)
     near_rows = pl.ds(half, half)
-    own_half = [pl.ds(k * quarter, quarter) for k in range(2)]
-    far_copy = [send(x_ref.at[own_half[k]], xb.at[far_rows[k]], sems, k, far_dev) for k in range(2)]
-    near_copy = send(x_ref, xb.at[near_rows], sems, 2, near_dev)
+    far_copy = [
+        send(x_ref.at[own_chunks[k]], xb.at[far_rows[k]], sems, k, far_dev) for k in range(CHUNKS)
+    ]
+    near_copy = send(x_ref, xb.at[near_rows], sems, 4 * CHUNKS, near_dev)
     own_units = gate_hbm.shape[1]
     core_rows = pl.ds(pl.multiple_of(lax.axis_index("tp") * half, 16), half)
     got_rows, got_units = pl.ds(half, 3 * half), pl.ds(own_units, 3 * own_units)
@@ -526,118 +533,129 @@
         put(slice(width, None), columns)
 
     def forward(k):
-        return send(xb.at[far_rows[k]], xb.at[cross_rows[k]], sems, 3 + k, near_dev)
+        return send(xb.at[far_rows[k]], xb.at[cross_rows[k]], sems, CHUNKS + k, near_dev)
 
     def cross_back(k):
-        return send(db.at[cross_rows[k]], near_in.at[own_half[k]], sems, 5 + k, near_dev)
+        return send(db.at[cross_rows[k]], near_in.at[own_chunks[k]], sems, 2 * CHUNKS + k, near_dev)
 
     def far_back(k):
         crossed[k].wait_recv()
-        total = db[far_rows[k], :].astype(f32) + near_in[own_half[k], :].astype(f32)
+        total = db[far_rows[k], :].astype(f32) + near_in[own_chunks[k], :].astype(f32)
         db[far_rows[k], :] = total.astype(bf16)
-        return send(db.at[far_rows[k]], far_in.at[own_half[k]], sems, 7 + k, far_dev)
-
-    def part_tile(j, carry):
-        cols = aligned(j, 2 * TILE)
-        part_ref[:, cols] = dot_nn(hw[...], wd[:, cols]).astype(bf16)
-        return carry
-
+        return send(db.at[far_rows[k]], far_in.at[own_chunks[k]], sems, 3 * CHUNKS + k, far_dev)
+
+    def part_rows(rows):
+        def part_tile(j, carry):
+            cols = aligned(j, 2 * TILE)
+            part_ref[rows, cols] = dot_nn(hw[rows, :], wd[:, cols]).astype(bf16)
+            return carry
+
+        lax.fori_loop(0, width // (2 * TILE), part_tile, 0)
+
+    forwards, crossed, backs = [], [], []
+
+    def pass_on(k):
+        far_copy[k].wait_recv()
+        forwards.append(forward(k))
+
+    pass_on(0)
     task(0)
-    far_copy[0].wait_recv()
-    forwards = [forward(0)]
+    pass_on(1)
+    forwards[0].wait_recv()
+    forwards[1].wait_recv()
+    task(2)
+    crossed += [cross_back(0), cross_back(1)]
+    pass_on(2)
     near_copy.wait_recv()
     task(1)
-    forwards[0].wait_recv()
-    task(2)
-    crossed = [cross_back(0)]
-    far_copy[1].wait_recv()
-    forwards.append(forward(1))
-    backs = [far_back(0)]
-    forwards[1].wait_recv()
+    backs += [far_back(0), far_back(1)]
+    pass_on(3)
+    part_rows(pl.ds(0, 2 * half))
+    forwards[2].wait_recv()
+    forwards[3].wait_recv()
     task(3)
-    crossed.append(cross_back(1))
-    near_back = send(db.at[near_rows], near_sum, sems, 9, near_dev)
-    lax.fori_loop(0, width // (2 * TILE), part_tile, 0)
-    backs.append(far_back(1))
+    crossed += [cross_back(2), cross_back(3)]
+    near_back = send(db.at[near_rows], near_sum, sems, 4 * CHUNKS + 1, near_dev)
+
+    pl.semaphore_signal(free_sem, inc=1, device_id=core_dev, device_id_type=MESH)
+    part_rows(pl.ds(2 * half, 2 * half))
+    backs.append(far_back(2))
 
     piece = units // 4
     tiles = width // TILE
 
-    def stage_copies(slot, number, rows, size, keep, got):
-        return (
-            pltpu.make_async_copy(
-                keep_stage.at[slot, pl.ds(0, size)], keep.at[rows], stage_sems.at[slot]
-            ),
-            pltpu.make_async_remote_copy(
-                src_ref=send_stage.at[slot, pl.ds(0, size)],
-                dst_ref=got.at[rows],
-                send_sem=tp_send.at[slot],
-                recv_sem=tp_recv.at[number],
-                device_id=core_dev,
-                device_id_type=MESH,
-            ),
+    def to_core(slot, number, rows, size, got):
+        return pltpu.make_async_remote_copy(
+            src_ref=send_stage.at[slot, pl.ds(0, size)],
+            dst_ref=got.at[rows],
+            send_sem=tp_send.at[slot],
+            recv_sem=tp_recv.at[number],
+            device_id=core_dev,
+            device_id_type=MESH,
         )
 
-    def wait_stage(slot, size, keep, got):
-        local, remote = stage_copies(slot, 0, pl.ds(0, size), size, keep, got)
-        local.wait()
-        remote.wait_send()
-
-    def gate_up_tile(i, carry):
-        rows = aligned(i, TILE)
-        slot = lax.rem(i, 2)
-
-        @pl.when(i >= 2)
-        def _():
-            wait_stage(slot, TILE, keep_gu, got_gu)
-
-        flipped = xb[:, rows].T
+    def to_hbm(slot, rows, size, full):
+        return pltpu.make_async_copy(
+            keep_stage.at[slot, pl.ds(0, size)], full.at[rows], stage_sems.at[slot]
+        )
+
+    def gradient_loop(count, first, size, compute, got, full):
+        def close(i):
+            slot, rows = lax.rem(i, 2), aligned(i, size)
+            to_core(slot, first + i, rows, size, got).wait_recv()
+            keep = keep_stage[slot, :size, :].astype(f32) + got[rows, :].astype(f32)
+            keep_stage[slot, :size, :] = keep.astype(bf16)
+            to_hbm(slot, rows, size, full).start()
+
+        def free(slot):
+            to_hbm(slot, pl.ds(0, size), size, full).wait()
+            to_core(slot, 0, pl.ds(0, size), size, got).wait_send()
+
+        def one(i, carry):
+            slot = lax.rem(i, 2)
+
+            @pl.when(i >= 2)
+            def _():
+                free(slot)
+
+            compute(i, slot)
+            to_core(slot, first + i, aligned(i, size), size, got).start()
+
+            @pl.when(i >= 1)
+            def _():
+                close(i - 1)
+
+            return carry
+
+        lax.fori_loop(0, count, one, 0)
+        close(count - 1)
+        free(0)
+        free(1)
+
+    def gate_up_tile(i, slot):
+        flipped = xb[:, aligned(i, TILE)].T
         for k, source in enumerate((dg, du)):
+            value = dot_nn(flipped, source[...]).astype(bf16)
             for p in range(4):
-                value = dot_nn(flipped, source[:, p * piece : (p + 1) * piece]).astype(bf16)
                 at = (2 * k + p // 2) * piece
                 stage = keep_stage if p % 2 == 0 else send_stage
-                stage[slot, :, at : at + piece] = value
-        for copy in stage_copies(slot, i, rows, TILE, keep_gu, got_gu):
-            copy.start()
-        return carry
-
-    lax.fori_loop(0, tiles, gate_up_tile, 0)
-    wait_stage(0, TILE, keep_gu, got_gu)
-    wait_stage(1, TILE, keep_gu, got_gu)
-    down_rows = 2 * piece // 6
-
-    def down_tile(i, carry):
-        which, within = i // 3, lax.rem(i, 3)
-        rows = aligned(i, down_rows)
-        slot = lax.rem(i, 2)
-
-        @pl.when(i >= 2)
-        def _():
-            wait_stage(slot, down_rows, keep_d, got_d)
-
-        start = which * 2 * piece + within * down_rows
+                stage[slot, :TILE, at : at + piece] = value[:, p * piece : (p + 1) * piece]
+
+    def down_tile(i, slot):
         for stage, offset in ((keep_stage, 0), (send_stage, piece)):
-            cols = pl.ds(pl.multiple_of(start + offset, 128), down_rows)
+            cols = pl.ds(pl.multiple_of(i * 2 * piece + offset, 128), piece)
             flipped = hw[:, cols].T
             for n in range(0, width, 2 * TILE):
-                stage[slot, :down_rows, n : n + 2 * TILE] = dot_nn(flipped, gb[:, n : n + 2 * TILE]).astype(bf16)
-        for copy in stage_copies(slot, tiles + i, rows, down_rows, keep_d, got_d):
-            copy.start()
-        return carry
-
-    lax.fori_loop(0, 6, down_tile, 0)
-    wait_stage(0, down_rows, keep_d, got_d)
-    wait_stage(1, down_rows, keep_d, got_d)
-
+                stage[slot, :, n : n + 2 * TILE] = dot_nn(flipped, gb[:, n : n + 2 * TILE]).astype(bf16)
+
+    pl.semaphore_wait(free_sem, 1)
+    gradient_loop(2, tiles, piece, down_tile, wg, sum_d)
+    backs.append(far_back(3))
+    gradient_loop(tiles, 0, TILE, gate_up_tile, wu, sum_gu)
     near_back.wait_recv()
-    backs[0].wait_recv()
-    backs[1].wait_recv()
+    for copy in backs:
+        copy.wait_recv()
     dx_ref[...] = d0[...] + near_sum[...].astype(f32) + far_in[...].astype(f32)
-    for i in range(tiles):
-        stage_copies(0, i, pl.ds(0, TILE), TILE, keep_gu, got_gu)[1].wait_recv()
-    for i in range(6):
-        stage_copies(0, tiles + i, pl.ds(0, down_rows), down_rows, keep_d, got_d)[1].wait_recv()
     for copy in far_copy + [near_copy, near_back] + forwards + crossed + backs:
         copy.wait_send()
 
@@ -656,12 +674,10 @@
             jax.ShapeDtypeStruct((half, wide), f32),
             jax.ShapeDtypeStruct((rows, width), bf16),
             jax.ShapeDtypeStruct((width, units), bf16),
-            jax.ShapeDtypeStruct((width, units), bf16),
-            jax.ShapeDtypeStruct((units // 2, width), bf16),
             jax.ShapeDtypeStruct((units // 2, width), bf16),
         ),
         in_specs=[vmem] + [any_spec] * 8,
-        out_specs=(vmem, vmem, any_spec, any_spec, any_spec, any_spec),
+        out_specs=(vmem, vmem, any_spec, any_spec),
         scratch_shapes=[
             pltpu.VMEM((rows, wide), bf16),
             pltpu.VMEM((rows, width), bf16),
@@ -677,14 +693,15 @@
             pltpu.VMEM((half, wide), bf16),
             pltpu.VMEM((half, wide), bf16),
             pltpu.VMEM((half, wide), bf16),
-            pltpu.VMEM((2, TILE, units), bf16),
-            pltpu.VMEM((2, TILE, units), bf16),
+            pltpu.VMEM((2, units // 4, width), bf16),
+            pltpu.VMEM((2, units // 4, width), bf16),
             pltpu.SemaphoreType.DMA((8,)),
             pltpu.SemaphoreType.DMA((2,)),
-            pltpu.SemaphoreType.DMA((10,)),
-            pltpu.SemaphoreType.DMA((10,)),
+            pltpu.SemaphoreType.DMA((4 * CHUNKS + 2,)),
+            pltpu.SemaphoreType.DMA((4 * CHUNKS + 2,)),
             pltpu.SemaphoreType.DMA((2,)),
-            pltpu.SemaphoreType.DMA((width // TILE + 6,)),
+            pltpu.SemaphoreType.DMA((width // TILE + 2,)),
+            pltpu.SemaphoreType.REGULAR,
         ],
         compiler_params=pltpu.CompilerParams(
             collective_id=1, has_side_effects=True, vmem_limit_bytes=62 * 1024 * 1024
@@ -851,6 +868,20 @@
     for ref, full in matrices:
         net.start(ref, slot(full, 1), core_dev)
 
+    from_share, from_ctx = [], []
+
+    def share_start(k):
+        ref, full = matrices[k]
+        size = ref.shape[0] // 2
+        piece = ref.at[pl.ds(pl.multiple_of(place * size, 16), size)]
+        from_share.append(net.start(piece, slot(full, 2, place), share_dev))
+
+    def share_on(k):
+        ref, full = matrices[k]
+        net.arrive(from_share[k])
+        from_ctx.append(net.start(slot(full, 2, place), slot(full, 2, place), ctx_dev))
+        net.start(slot(full, 2, place), slot(full, 3, place), core_dev)
+
     here = lax.broadcasted_iota(jnp.int32, (rows, 1), 0) + place * rows
     position = (here - document_start(lengths_ref, here)).astype(f32)
     turn_lane = lax.broadcasted_iota(jnp.int32, (1, HEAD_DIM), 1)
@@ -866,23 +897,29 @@
     count_step()
     own_rows = pl.ds(pl.multiple_of(core * half, 16), half)
     other_rows = pl.ds(pl.multiple_of((1 - core) * half, 16), half)
-    own_quarter = [pl.ds(pl.multiple_of(core * half + k * quarter, 16), quarter) for k in range(2)]
-    far_rows = [pl.ds(2 * half + k * half, quarter) for k in range(2)]
-    cross_rows = [pl.ds(2 * half + k * half + quarter, quarter) for k in range(2)]
-    from_share = []
-    for ref, full in matrices:
-        size = ref.shape[0] // 2
-        piece = ref.at[pl.ds(pl.multiple_of(place * size, 16), size)]
-        from_share.append(net.start(piece, slot(full, 2, place), share_dev))
-    far_copies = [net.start(grad_hbm.at[own_quarter[k]], grads.at[far_rows[k]], far_dev) for k in range(2)]
-    for code in rest:
+    chunk = half // CHUNKS
+    own_chunks = [pl.ds(pl.multiple_of(core * half + k * chunk, 16), chunk) for k in range(CHUNKS)]
+    _, far_rows, cross_rows = token_rows(half)
+    share_start(0)
+    far_copies = [net.start(grad_hbm.at[own_chunks[k]], grads.at[far_rows[k]], far_dev) for k in range(CHUNKS)]
+    def cross_on(k):
+        net.arrive(far_copies[k])
+        net.start(grads.at[far_rows[k]], grads.at[cross_rows[k]], near_dev)
+
+    for code in rest[:6]:
+        for g in ins:
+            g.arrive(code)
+    for code in rest[6:]:
         for g in ins:
             g.arrive(code)
     count_step()
+    net.arrive(from_share[0])
+    share_start(1)
     outs = [
-        RowGather(net, out_full, (block, 0, part), [across] + fars + [low]),
+        RowGather(net, out_full, (block, 0, part), fars + [across, low]),
         RowGather(net, out_full, (block, part, part), fars + [low, across]),
     ]
+    net.start(grad_hbm.at[own_rows], grads.at[pl.ds(half, half)], near_dev)
     gains = in_full[:, :128].astype(f32).T
     attn_gain, moe_gain = gains[experts : experts + 1], gains[experts + 1 : experts + 2]
     step = quarter // 2
@@ -903,12 +940,16 @@
     for head in range(heads_width // HEAD_DIM):
         cols = slice(head * HEAD_DIM, (head + 1) * HEAD_DIM)
         query[:, cols] = rotated(raw[:, cols], slice(None)).astype(bf16)
+    share_on(0)
     for code in first:
         for g in outs:
             g.arrive(code)
-    near_copy = net.start(grad_hbm.at[own_rows], grads.at[pl.ds(half, half)], near_dev)
     count_step()
     net.arrive(kv_copy)
+    net.arrive(from_share[1])
+    share_start(2)
+    share_on(1)
+    cross_on(0)
 
     keys, values_flipped = kv[:, :HEAD_DIM], kv[:, HEAD_DIM:].T
     query_number = lax.broadcasted_iota(jnp.int32, (1, half), 1) + place * rows
@@ -932,23 +973,22 @@
     group = heads_width // HEAD_DIM
     third = 2 * group // 3
     lax.fori_loop(0, third, head_block, 0)
-    for code in rest:
+    for code in rest[:6]:
         for g in outs:
             g.arrive(code)
+    cross_on(1)
+    lax.fori_loop(third, 2 * third, head_block, 0)
+    for code in rest[6:]:
+        for g in outs:
+            g.arrive(code)
+    cross_on(2)
     count_step()
-    lax.fori_loop(third, 2 * third, head_block, 0)
-    for k in range(2):
-        net.arrive(far_copies[k])
-        net.start(grads.at[far_rows[k]], grads.at[cross_rows[k]], near_dev)
     lax.fori_loop(2 * third, 2 * group, head_block, 0)
-    from_ctx = []
-    for k, (ref, full) in enumerate(matrices):
-        net.arrive(from_share[k])
-        from_ctx.append(net.start(slot(full, 2, place), slot(full, 2, place), ctx_dev))
-        net.start(slot(full, 2, place), slot(full, 3, place), core_dev)
+    cross_on(3)
 
     core_sent[...] = dot_nt(attended[other_rows, :], out_full[...])
     core_copy = net.start(core_sent, core_got, core_dev)
+    share_on(2)
     middle_ref[...] = tokens_ref[own_rows, :].astype(f32) + dot_nt(attended[own_rows, :], out_full[...])
     net.arrive(core_copy)
     own_lane = lax.broadcasted_iota(jnp.int32, (step, 128), 1)
@@ -1033,8 +1073,8 @@
             pltpu.VMEM((half, width), f32),
             pltpu.VMEM((4, 8, 128), f32),
             pltpu.VMEM((4, 8, 128), f32),
-            pltpu.SemaphoreType.DMA((90,)),
-            pltpu.SemaphoreType.DMA((90,)),
+            pltpu.SemaphoreType.DMA((100,)),
+            pltpu.SemaphoreType.DMA((100,)),
             pltpu.SemaphoreType.DMA((8,)),
         ],
         compiler_params=pltpu.CompilerParams(
@@ -1085,7 +1125,7 @@
     lengths_ref, row_ref, dx_ref, middle_ref, probs_ref, mask_ref, grad_hbm,
     tokens_hbm, query_hbm, kv_hbm, lse_ref, attended_hbm, cos_ref, sin_ref,
     in_hbm, out_hbm, moe_hbm, gu_hbm, down_hbm,
-    output_hbm, loss_ref, tokens_grad_hbm, in_ref, out_ref, extra_ref, gate_ref, up_ref, down_ref,
+    output_hbm, loss_ref, tokens_grad_hbm, query_out, key_out, value_out, out_ref, extra_ref, gate_ref, up_ref, down_ref,
     grad_ref, tokens, query, kv, attended, in_full, out_full,
     out_in, att_grad, qkv_grad, kv_grad, kv_sent, kv_got,
     in_box, out_box,
@@ -1107,11 +1147,9 @@
     quarter = half // 2
     own_rows = pl.ds(pl.multiple_of(core * half, 16), half)
     other_rows = pl.ds(pl.multiple_of((1 - core) * half, 16), half)
-    halves = [pl.ds(k * quarter, quarter) for k in range(2)]
-
-    far_rows = [pl.ds(2 * half + k * half, quarter) for k in range(2)]
-    cross_rows = [pl.ds(2 * half + k * half + quarter, quarter) for k in range(2)]
-    crossed = [net.start(moe_hbm.at[cross_rows[k]], moe_cross.at[halves[k]], near_dev) for k in range(2)]
+    chunks, far_rows, cross_rows = token_rows(half)
+
+    crossed = [net.start(moe_hbm.at[cross_rows[k]], moe_cross.at[chunks[k]], near_dev) for k in range(CHUNKS)]
     units = gu_hbm.shape[1] // 4
     wide = width // 2
 
@@ -1121,15 +1159,12 @@
     gate_cols, up_own_cols, up_par_cols = pl.ds(0, 2 * units), pl.ds(2 * units, units), pl.ds(3 * units, units)
     gate_first = net.start(gu_hbm.at[wide_half(1 - ctx_place), gate_cols], gate_x, ctx_dev)
     up_first = net.start(gu_hbm.at[:, up_par_cols], up_s, share_dev)
-    near_first = net.start(moe_hbm.at[pl.ds(half, half)], moe_near, near_dev)
-    down_first = net.start(down_hbm.at[:, wide_half(1 - ctx_place)], down_x, ctx_dev)
     pairs = [
         (in_hbm, in_full), (out_hbm, out_full), (attended_hbm, attended), (query_hbm, query),
         (kv_hbm, kv), (tokens_hbm, tokens), (moe_hbm.at[pl.ds(0, half)], moe_own),
-        (moe_hbm.at[far_rows[0]], moe_far.at[halves[0]]), (moe_hbm.at[far_rows[1]], moe_far.at[halves[1]]),
         (gu_hbm.at[wide_half(ctx_place), gate_cols], gate_own), (gu_hbm.at[:, up_own_cols], up_own),
         (down_hbm.at[:, wide_half(ctx_place)], down_own), (grad_hbm.at[own_rows], grad_ref),
-    ]
+    ] + [(moe_hbm.at[far_rows[k]], moe_far.at[chunks[k]]) for k in range(CHUNKS)]
     for src, dst in pairs:
         net.keep(src, dst)
 
@@ -1137,7 +1172,10 @@
         for number in numbers:
             net.settle(number)
 
-    loaded(0, 12)
+    def pieces(size):
+        return [slice(k * size // 4, (k + 1) * size // 4) for k in range(4)]
+
+    loaded(0, 10)
     flipped_extra = in_full[:, :128].astype(f32).T
     attn_gain, moe_gain = flipped_extra[experts : experts + 1], flipped_extra[experts + 1 : experts + 2]
     lane = lax.broadcasted_iota(jnp.int32, (half, 128), 1)
@@ -1186,7 +1224,16 @@
             loss_copies.append(net.start(loss_sent.at[k], loss_got.at[k], loss_dims[k]))
 
     loss_step()
-
+    loaded(6, *range(11, 11 + CHUNKS))
+    far_sums = []
+
+    def far_sum(k):
+        net.arrive(crossed[k])
+        at = chunks[k]
+        moe_far[at, :] = (moe_far[at, :].astype(f32) + moe_cross[at, :].astype(f32)).astype(bf16)
+        far_sums.append(net.start(moe_far.at[at], moe_back.at[at], far_dev))
+
+    far_sum(0)
     net.arrive(out_in_copy)
     loaded(1, 2)
     att_grad[...] = dot_nn(out_in[...], out_full[...]).astype(bf16)
@@ -1197,17 +1244,21 @@
         return carry
 
     lax.fori_loop(0, width // TILE, out_tile, 0)
-    block = in_ref.shape[0]
+    block = key_out.shape[0]
     low, across = ("fsdp", near), ("ctx", 1)
     fars = [("fsdp", far), ("fsdp", SHARE)]
     orders = [fars + [across, low], fars + [low, across]]
     part_size = block // 2
     sums_out = [
-        RowReduce(net, out_full, out_box.at[k], (block, k * part_size, part_size), orders[k]) for k in range(2)
+        RowReduce(net, out_full, out_box.at[k], (block, k * part_size, part_size), [across] + fars + [low])
+        for k in range(2)
     ]
+    far_sum(1)
     for s in sums_out:
         s.level(3)
     loss_step()
+    far_sum(2)
+    far_sum(3)
     net.sent(out_in_copy)
     loaded(5)
     normed_step = half // 2
@@ -1248,26 +1299,30 @@
     third = 2 * group // 3
     lax.fori_loop(0, third, head_block, 0)
     loss_step()
-    loaded(6, 7, 8)
-    far_sums = []
-    for k in range(2):
-        net.arrive(crossed[k])
-        moe_far[halves[k], :] = (moe_far[halves[k], :].astype(f32) + moe_cross[halves[k], :].astype(f32)).astype(bf16)
-        far_sums.append(net.start(moe_far.at[halves[k]], moe_back.at[halves[k]], far_dev))
-    for s in sums_out:
-        s.level(2)
+    down_first = net.start(down_hbm.at[:, wide_half(1 - ctx_place)], down_x, ctx_dev)
     lax.fori_loop(third, 2 * third, head_block, 0)
     loss_step()
-    for s in sums_out:
-        s.level(1)
+    loaded(7, 8, 9)
+    net.arrive(gate_first)
+    for at in pieces(wide):
+        total = gate_own[at, :].astype(f32) + gate_x[at, :].astype(f32)
+        gate_ref[at, :] = total[:, :units]
+        gate_sent[at, :] = total[:, units:].astype(bf16)
+    gate_last = net.start(gate_sent, gate_s, share_dev)
+    net.arrive(up_first)
+    up_sent[...] = (up_own[wide_half(1 - ctx_place), :].astype(f32) + up_s[wide_half(1 - ctx_place), :].astype(f32)).astype(bf16)
+    up_ref[...] = up_own[wide_half(ctx_place), :].astype(f32) + up_s[wide_half(ctx_place), :].astype(f32)
     lax.fori_loop(2 * third, 2 * group, head_block, 0)
     loss_step()
     ctx_rows = pl.ds(pl.multiple_of(ctx_place * rows, 16), rows)
     ctx_other = pl.ds(pl.multiple_of((1 - ctx_place) * rows, 16), rows)
     kv_sent[...] = kv_grad[ctx_other, :].astype(bf16)
     kv_copy = net.start(kv_sent, kv_got, ctx_dev)
-    for s in sums_out:
-        s.level(0)
+    up_last = net.start(up_sent, up_x, ctx_dev)
+    for mask in (7, 6, 5, 4):
+        for s in sums_out:
+            s.step(mask)
+    near_first = net.start(moe_hbm.at[pl.ds(half, half)], moe_near, near_dev)
     loss_step()
     loss = jnp.sum(loss_state[0][0:1] * row_ref[1:2, :], axis=1, keepdims=True)
     loss_ref[...] = jnp.broadcast_to(loss, loss_ref.shape)
@@ -1308,6 +1363,9 @@
     ]
     for s in sums_in:
         s.level(3)
+    for mask in (3, 2):
+        for s in sums_out:
+            s.step(mask)
 
     net.arrive(back_copy)
     for k in range(2):
@@ -1318,38 +1376,25 @@
     net.keep(tok_stage, tokens_grad_hbm.at[own_rows])
     net.start(tok_stage, tokens_grad_hbm.at[own_rows], core_dev)
 
-    def pieces(size):
-        return [slice(k * size // 4, (k + 1) * size // 4) for k in range(4)]
-
-    loaded(9, 10, 11)
-    net.arrive(gate_first)
-    for at in pieces(wide):
-        total = gate_own[at, :].astype(f32) + gate_x[at, :].astype(f32)
-        gate_ref[at, :] = total[:, :units]
-        gate_sent[at, :] = total[:, units:].astype(bf16)
-    gate_last = net.start(gate_sent, gate_s, share_dev)
-    for s in sums_in:
-        s.level(2)
-    net.arrive(up_first)
-    up_sent[...] = (up_own[wide_half(1 - ctx_place), :].astype(f32) + up_s[wide_half(1 - ctx_place), :].astype(f32)).astype(bf16)
-    up_last = net.start(up_sent, up_x, ctx_dev)
-    up_ref[...] = up_own[wide_half(ctx_place), :].astype(f32) + up_s[wide_half(ctx_place), :].astype(f32)
-    for s in sums_in:
-        s.level(1)
+    for mask in (7, 6, 5, 4):
+        for s in sums_in:
+            s.step(mask)
+    for s in sums_out:
+        s.step(1)
     net.arrive(down_first)
     for at in pieces(units):
         down_ref[at, :] = down_own[at, :].astype(f32) + down_x[at, :].astype(f32)
         after = slice(at.start + units, at.stop + units)
         down_sent[at, :] = (down_own[after, :].astype(f32) + down_x[after, :].astype(f32)).astype(bf16)
     down_last = net.start(down_sent, down_s, share_dev)
-    for s in sums_in:
-        s.level(0)
+    for mask in (3, 2, 1):
+        for s in sums_in:
+            s.step(mask)
 
     net.arrive(near_first)
-    for k in range(2):
+    for k in range(CHUNKS):
         net.arrive(far_sums[k])
-    for k in range(2):
-        at = halves[k]
+        at = chunks[k]
         moe_out = moe_own[at, :].astype(f32) + moe_near[at, :].astype(f32) + moe_back[at, :].astype(f32)
         moe_own[at, :] = (middle_ref[at, :] + moe_out).astype(bf16)
     net.keep(moe_own, output_hbm.at[own_rows])
@@ -1360,7 +1405,9 @@
         out_ref[at, :] = sums_out[k].step(0)
         value = sums_in[k].step(0)
         extra_sent[at, :] = value[:, :128]
-        in_ref[at, :] = value[:, 128:]
+        query_out[at, :] = value[:, 128 : 128 + heads_width]
+        key_out[at, :] = value[:, 128 + heads_width : 128 + heads_width + HEAD_DIM]
+        value_out[at, :] = value[:, 128 + heads_width + HEAD_DIM :]
     extra_copy = net.start(extra_sent, extra_got, core_dev)
     net.arrive(gate_last)
     gate_ref[...] += gate_s[...].astype(f32)
@@ -1403,7 +1450,9 @@
             jax.ShapeDtypeStruct((rows, width), bf16),
             jax.ShapeDtypeStruct((8, 128), f32),
             jax.ShapeDtypeStruct((rows, width), f32),
-            jax.ShapeDtypeStruct((block, in_width - 128), f32),
+            jax.ShapeDtypeStruct((block, heads_width), f32),
+            jax.ShapeDtypeStruct((block, HEAD_DIM), f32),
+            jax.ShapeDtypeStruct((block, HEAD_DIM), f32),
             jax.ShapeDtypeStruct((block, out_width), f32),
             jax.ShapeDtypeStruct((block, 128), f32),
             jax.ShapeDtypeStruct((width // 2, units), f32),
@@ -1411,7 +1460,7 @@
             jax.ShapeDtypeStruct((units, width // 2), f32),
         ),
         in_specs=[smem] + [vmem] * 5 + [any_spec] * 4 + [vmem, any_spec, vmem, vmem] + [any_spec] * 5,
-        out_specs=(any_spec, vmem, any_spec) + (vmem,) * 6,
+        out_specs=(any_spec, vmem, any_spec) + (vmem,) * 8,
         scratch_shapes=[
             low(half, width), low(rows, width), low(rows, heads_width), low(pack, kv_width), low(rows, heads_width),
             low(*in_full.shape), low(*out_full.shape),
@@ -1425,9 +1474,9 @@
             low(width, units), low(width, units), low(width // 2, units), low(width // 2, units),
             low(2 * units, width // 2), low(2 * units, width // 2), low(units, width // 2), low(units, width // 2),
             wide(5, 8, 128), wide(5, 8, 128),
-            pltpu.SemaphoreType.DMA((90,)),
-            pltpu.SemaphoreType.DMA((90,)),
-            pltpu.SemaphoreType.DMA((16,)),
+            pltpu.SemaphoreType.DMA((100,)),
+            pltpu.SemaphoreType.DMA((100,)),
+            pltpu.SemaphoreType.DMA((20,)),
         ],
         compiler_params=pltpu.CompilerParams(
             collective_id=2, has_side_effects=True, vmem_limit_bytes=62 * 1024 * 1024
@@ -1751,7 +1800,6 @@
             w_gate, w_up, w_down, out_grad, loss_grad,
         )
     small = widen([w_router, norm_attn[:, None], norm_moe[:, None]])
-    query_width, kv_width = w_query.shape[1], w_key.shape[1]
     (
         payload, middle, probs, mask, row, query, kv_pack, lse, attended, cos, sin,
         in_weights, out_weights, grad_rows, gate_all, up_all, down_all,
@@ -1759,12 +1807,12 @@
         lengths, loss_grad, routes, tokens, small, w_query, w_key, w_value, w_out.T, out_grad,
         w_gate[0], w_up[0], w_down[0], expert_count,
     )
-    returned, moe_rows, keep_gu, got_gu, keep_d, got_d = experts_on_chip(
+    returned, moe_rows, gate_up_grad, down_grad = experts_on_chip(
         payload, out_grad, w_gate[0], w_up[0], w_down[0], grad_rows, gate_all, up_all, down_all, expert_count
     )
-    gate_up_grad = (keep_gu.astype(f32) + got_gu.astype(f32)).astype(bf16)
-    down_grad = (keep_d.astype(f32) + got_d.astype(f32)).astype(bf16)
-    output, loss, tokens_grad, in_reduced, out_reduced, small, gate_w_out, up_w_out, down_w_out = backward_on_chip(
+    (
+        output, loss, tokens_grad, query_grad, key_grad, value_grad, out_reduced, small, gate_w_out, up_w_out, down_w_out,
+    ) = backward_on_chip(
         lengths, row, returned, middle, probs, mask, out_grad, tokens, query, kv_pack, lse, attended, cos, sin,
         in_weights, out_weights, moe_rows, gate_up_grad, down_grad, expert_count,
     )
@@ -1773,9 +1821,9 @@
         loss[0, :1],
         tokens_grad,
         small[:, expert_count],
-        in_reduced[:, :query_width],
-        in_reduced[:, query_width : query_width + kv_width],
-        in_reduced[:, query_width + kv_width :],
+        query_grad,
+        key_grad,
+        value_grad,
         out_reduced.T,
         small[:, expert_count + 1],
         small[:, :expert_count],

time: 493 us -> 385 us (0.78)
  Pallas kernels: 453 us -> 356 us
  other arithmetic: 11 us -> 0.7 us
    pallas_call x1, Pallas kernels: 180 us -> 129 us  [backward_on_chip(): pl.pallas_call(functools.partial(backward_kernel, far, near, experts, hea...]
    pallas_call x1, Pallas kernels: 171 us -> 127 us  [forward_on_chip(): pl.pallas_call(functools.partial(forward_kernel, far, near, experts, rows...]
    convert_element_type x2 -> x0, other arithmetic: 10.3 us -> none  [the longest x1 5.76 us: on_device(): gate_up_grad = (keep_gu.astype(f32) + got_gu.astype(f32)).astype(bf16)]
    unnamed x21 -> x28, local copies, waits for them, and re-layouts: 11.9 us -> 14.7 us
where the time goes in v3:
time: 385 us; the launch traced here: 378 us
  Pallas kernels  356 us (92%)
  local copies, waits for them, and re-layouts  19.1 us (5%)
    pallas_call x1, Pallas kernels, backward_on_chip(): pl.pallas_call(functools.partial(backward_kernel, far, near, experts, hea...  129 us
    pallas_call x1, Pallas kernels, forward_on_chip(): pl.pallas_call(functools.partial(forward_kernel, far, near, experts, rows...  127 us
    pallas_call x1, Pallas kernels, experts_on_chip(): pl.pallas_call(functools.partial(expert_kernel, far, near, experts), name...  100 us
    unnamed x28, local copies, waits for them, and re-layouts  14.7 us

profile of v3, /device:TPU:11, one launch (start us, length us, event | category | flops | bytes accessed | tf_op | source)
XLA Modules:
  0.0 377.5 jit_solution(7617159501359123147)
XLA Ops:
  1.3 0.1 pad.3.clone
  1.4 0.8 copy.34
  2.1 0.8 copy.35
  2.9 0.8 copy.33
  3.7 0.7 maximum_maximum_fusion.small_hbm
  4.4 1.5 copy.36.routes_ref
  6.0 126.7 %forward.1 = (bf16[256,1664]{1,0:T(8,128)(2,1)}, f32[256,1536]{1,0:T(8,128)}, f32[256,128]{1,0:T(8,128)}, f32[256,128]{1,0:T(8,128)}, f32[8,128]{1,0:T(8,128)}, ...) custom-call(s32[1,3]{1,0:T(1,128)} %lengths_ref.3, ...), custom_call_target="tpu_custom_call" | custom-call | tf_op jit(solution)/shard_map/forward/pallas_call | solution.py:1061
  132.7 100.4 %experts.1 = (f32[256,1664]{1,0:T(8,128)}, bf16[1024,1536]{1,0:T(8,128)(2,1)}, bf16[1536,1536]{1,0:T(8,128)(2,1)}, bf16[768,1536]{1,0:T(8,128)(2,1)}) custom-call(bf16[256,1664]{1,0:T(8,128)(2,1)} %get-tuple-element.46.x_ref, bf16[512,1536]{1,0:T(8,128)(2,1)} %grad_hbm.5, bf16[1536,384]{1,0:T(8,128)(2,1)} %bitcast.16, bf16[1536,384]{1,0:T(8,128)(2,1)} %bitcast.18, ...), custom_call_target="tpu_custom_call" | custom-call | flops 43486543872 | bytes 60000000 | tf_op jit(solution)/shard_map/experts/pallas_call | solution.py:670
  233.1 129.0 %backward.1 = (bf16[512,1536]{1,0:T(8,128)(2,1)}, f32[8,128]{1,0:T(8,128)}, f32[512,1536]{1,0:T(8,128)}, f32[96,768]{1,0:T(8,128)}, f32[96,128]{1,0:T(8,128)}, /...) custom-call(s32[1,3]{1,0:T(1,128)} %lengths_ref.3, ...), custom_call_target="tpu_custom_call" | custom-call | tf_op jit(solution)/shard_map/backward/pallas_call | solution.py:1446
  362.1 1.2 slice.12
  363.3 1.6 slice_reduce_fusion
  364.9 1.5 copy.37
  366.4 0.0 copy-start
  366.4 2.8 copy.48
  369.2 0.0 copy-done
  369.2 0.0 copy-start.5
  369.2 0.0 copy-start.7
  369.2 0.0 copy-start.6
  369.2 0.0 copy-start.4
  369.2 1.7 copy.49
  370.9 0.0 copy-done.5
  370.9 0.0 copy-start.3
  370.9 0.7 copy.50
  371.6 0.0 copy-done.7
  371.6 0.0 copy-start.2
  371.6 0.6 copy.51
  372.2 0.0 copy-done.6
  372.2 0.6 copy.52
  372.8 0.0 copy-done.4
  372.8 0.7 copy.53
  373.5 0.0 copy-done.3
  373.6 1.0 copy.54
  374.6 0.0 copy-done.2
  374.6 0.0 copy-start.1
  374.6 1.0 copy.55
  375.6 0.7 copy-done.1
  376.3 1.0 copy.56
  (1 shorter events, 0.0 us)
Async XLA Ops:
  366.4 2.8 copy-start
  369.2 1.7 copy-start.5
  369.2 2.4 copy-start.7
  369.2 3.0 copy-start.6
  369.2 3.6 copy-start.4
  370.9 2.7 copy-start.3
  371.6 3.0 copy-start.2
  374.6 1.7 copy-start.1
